TPU v7x, 512 devices: a whole 4x8x8 slice. The times are simulated.
512 devices in a mesh: chan: 128 (over y, z, core), period: 4 (over x).
Axes of the slice: x: 4, y: 8, z: 8, core: 2. Of those that a mesh axis runs over, the one named last changes fastest.
Arguments:
- raw_strain: bfloat16 [4, 2048, 8192], P('period', 'chan'), may hold values from -16 to 16
- bin_ids: int32 [3, 8192, 64], P(None, 'chan'), may hold values from 0 to 31, as said below
- owner_map: int32 [256], replicated, may hold values from 0 to 127, as said below
Outputs:
- stacks: float32 [512, 32, 256], P('chan')
Inputs may be any that keep to these rules, and one draw needn't show every extreme that they name: `bin_ids`: for channel c of block b = c // 64 and partner block b - d, the value is l * 8 + o: the pair lies in midpoint bin 2 * (b - 1) + l with l from 0 to 3, and in offset bin o below 8. `owner_map`: nondecreasing in the bin; bin m belongs to device m // 2 or m // 2 + 1; no device owns more than 4 bins and some device owns exactly 4.
All inputs are finite; a program needn't handle non-finite values.
Results may differ from a plain program's by a relative error of at most 0.0025.
Values may be sent and summed in bfloat16 or wider, within the bound.
No kernel may reach another device: no remote copies, remote signals or barrier semaphores. Data moves between devices by JAX's collectives and lax.ppermute only.
A program may use at most 64 MiB of HBM per device.

v0:
```python
import math

import jax
import jax.numpy as jnp
import numpy as np
from jax import lax
from jax.experimental import pallas as pl
from jax.experimental.pallas import tpu as pltpu
from jax.sharding import PartitionSpec as P

CH_DEV = 64
WIN = 256
NF = 128
NWIN = 8
MB_DEV = 2
NOFF = 8
NP = 32
CAP = 4
BINS = 2 * MB_DEV * NOFF
VMEM_LIMIT = 48 * 1024 * 1024

ROW_SAMPLE = (
    16 * np.arange(16)[None, :, None] + 8 * np.arange(2)[:, None, None] + np.arange(8)[None, None, :]
).reshape(-1)


def dft_rows():
    phase = 2.0 * math.pi / WIN * np.mod(ROW_SAMPLE[:, None] * np.arange(1, NF + 1)[None, :], WIN)
    return np.concatenate([np.cos(phase), -np.sin(phase)], axis=1).astype(np.float32)


def lag_table():
    phase = 2.0 * math.pi / WIN * np.mod(np.arange(1, NF + 1)[:, None] * np.arange(WIN)[None, :], WIN)
    return np.concatenate([np.cos(phase), -np.sin(phase)], axis=0).astype(np.float32)


def slant_tables():
    slow = (np.arange(NP) - NP // 2) / (4.0 * NP)
    offset = (np.arange(NOFF) + 0.5) * (3.0 * CH_DEV / NOFF)
    freq = np.arange(1, NF + 1) * (2.0 * math.pi / WIN)
    phase = offset[:, None, None] * slow[None, :, None] * freq[None, None, :]
    return np.stack([np.cos(phase), np.sin(phase)]).astype(np.float32)


def call(kernel, out_shape, n_in, **kw):
    return pl.pallas_call(
        kernel,
        out_shape=out_shape,
        compiler_params=pltpu.CompilerParams(vmem_limit_bytes=VMEM_LIMIT),
        **kw,
    )


def pack_kernel(raw_ref, out_ref):
    low = lax.broadcasted_iota(jnp.int32, (8, 128), 1) < 64
    for tile in range(raw_ref.shape[1] // 128):
        both = raw_ref[:, 128 * tile : 128 * tile + 128].astype(jnp.float32)
        first, second = both[:8], both[8:]
        even = jnp.where(low, first, pltpu.roll(second, 64, 1))
        odd = jnp.where(low, pltpu.roll(first, 64, 1), second)
        out_ref[tile] = jnp.concatenate([even, odd], axis=0).astype(jnp.bfloat16)


def mask_kernel(ids_ref, owner_ref, masks_ref, place_ref):
    ids = jnp.concatenate([ids_ref[0], ids_ref[1], ids_ref[2]], axis=1)
    for bin_at in range(BINS):
        masks_ref[bin_at * CH_DEV : (bin_at + 1) * CH_DEV, :] = (
            (ids == bin_at).astype(jnp.float32).astype(jnp.bfloat16)
        )
    device = lax.axis_index("chan")
    owner = owner_ref[...]
    place_ref[0] = jnp.sum((owner < device).astype(jnp.int32)) - MB_DEV * (device - 1)
    place_ref[1] = jnp.sum((owner == device).astype(jnp.int32))


def spectra_kernel(series_ref, table_ref, out_ref):
    table = table_ref[...]
    for window in range(NWIN):
        turned = series_ref[window].astype(jnp.float32).T.astype(jnp.bfloat16)
        series = jnp.concatenate([turned[:CH_DEV], turned[CH_DEV:]], axis=1)
        spectra = jnp.dot(series, table, preferred_element_type=jnp.float32)
        power = jnp.mean(spectra * spectra, axis=-1, keepdims=True)
        out_ref[window] = (spectra / jnp.sqrt(power + 1e-06)).astype(jnp.bfloat16)


def bin_kernel(masks_ref, own_ref, near_ref, far_ref, wide_ref, half_ref, sums):
    def add_window(window, carry):
        own = own_ref[window]
        partners = jnp.concatenate([own, near_ref[window], far_ref[window]], axis=0)
        own = own.astype(jnp.float32)
        own_real, own_imag = own[:, :NF], own[:, NF:]
        for bin_at in range(BINS):
            picked = jnp.dot(
                masks_ref[bin_at * CH_DEV : (bin_at + 1) * CH_DEV, :],
                partners,
                preferred_element_type=jnp.float32,
            )
            picked_real, picked_imag = picked[:, :NF], picked[:, NF:]
            real = own_real * picked_real + own_imag * picked_imag
            imag = own_imag * picked_real - own_real * picked_imag
            sums[0, bin_at] += jnp.sum(real.reshape(8, 8, NF), axis=0)
            sums[1, bin_at] += jnp.sum(imag.reshape(8, 8, NF), axis=0)
        return carry

    sums[...] = jnp.zeros_like(sums)
    lax.fori_loop(0, NWIN, add_window, 0)
    binned = jnp.concatenate([jnp.sum(sums[0], axis=1), jnp.sum(sums[1], axis=1)], axis=1)
    odd = lax.rem(lax.axis_index("chan"), 2)
    half = jnp.where(odd == 1, binned[BINS // 2 :], binned[: BINS // 2])
    for place in range(8):
        wide_ref[place] = binned
        half_ref[place] = half


def stack_kernel(place_ref, wide_ref, half_ref, slant_ref, lags_ref, out_ref, held, spec):
    device = lax.axis_index("chan")
    odd = lax.rem(device, 2)
    whole = BINS // 2

    def over_periods(ref, part, rows):
        total = ref[part * 4, rows]
        for period in range(1, 4):
            total = total + ref[part * 4 + period, rows]
        return total

    own = over_periods(wide_ref, odd, pl.ds(0, BINS))
    beside = over_periods(wide_ref, 1 - odd, pl.ds(pl.multiple_of(odd * whole, 8), whole))
    across = over_periods(half_ref, 1 - odd, pl.ds(0, whole))
    has_across = (device > 0) & (device < lax.axis_size("chan") - 1)
    across = jnp.where(has_across, across, 0.0)
    lower = own[:whole] + jnp.where(odd == 1, beside, across)
    upper = own[whole:] + jnp.where(odd == 1, across, beside)
    held[...] = jnp.zeros_like(held)
    held[:whole] = lower
    held[whole:BINS] = upper
    first = place_ref[0]
    count = place_ref[1]
    first = jnp.where(count > 0, first, 0)
    for slot in range(CAP):
        rows = held[pl.ds(pl.multiple_of((first + slot) * NOFF, 8), NOFF), :]
        rows = jnp.where(slot < count, rows, 0.0)
        real = jnp.zeros((NP, NF), jnp.float32)
        imag = jnp.zeros((NP, NF), jnp.float32)
        for offset in range(NOFF):
            bin_real = rows[offset : offset + 1, :NF]
            bin_imag = rows[offset : offset + 1, NF:]
            cos, sin = slant_ref[0, offset], slant_ref[1, offset]
            real = real + (bin_real * cos + bin_imag * sin)
            imag = imag + (bin_imag * cos - bin_real * sin)
        spec[slot * NP : (slot + 1) * NP, :NF] = real
        spec[slot * NP : (slot + 1) * NP, NF:] = imag
    traces = jnp.dot(
        spec[...], lags_ref[...], precision=lax.Precision.HIGHEST, preferred_element_type=jnp.float32
    )
    power = jnp.mean(traces * traces, axis=-1, keepdims=True)
    out_ref[...] = traces / jnp.sqrt(power + 1e-06)


def shards(raw_strain, bin_ids, owner_map):
    count = lax.axis_size("chan")
    periods = lax.axis_size("period")
    smem = pl.BlockSpec(memory_space=pltpu.SMEM)
    vmem = pl.BlockSpec(memory_space=pltpu.VMEM)
    packed = call(pack_kernel, jax.ShapeDtypeStruct((count // 2, 16, 128), jnp.bfloat16), 1)(raw_strain[0])
    series = lax.all_to_all(packed.reshape(count, 8, 128), "chan", 0, 0, tiled=True)
    masks, place = call(
        mask_kernel,
        (
            jax.ShapeDtypeStruct((BINS * CH_DEV, 3 * CH_DEV), jnp.bfloat16),
            jax.ShapeDtypeStruct((2,), jnp.int32),
        ),
        2,
        out_specs=(vmem, smem),
    )(bin_ids, owner_map.reshape(2, 128))
    own = call(spectra_kernel, jax.ShapeDtypeStruct((NWIN, CH_DEV, 2 * NF), jnp.bfloat16), 2)(
        series.reshape(NWIN, 128, 128), jnp.asarray(dft_rows(), jnp.bfloat16)
    )
    near = lax.ppermute(own, "chan", [(i, i + 1) for i in range(count - 1)])
    far = lax.ppermute(own, "chan", [(i, i + 2) for i in range(count - 2)])
    wide, half = call(
        bin_kernel,
        (
            jax.ShapeDtypeStruct((8, BINS, 2 * NF), jnp.float32),
            jax.ShapeDtypeStruct((8, BINS // 2, 2 * NF), jnp.float32),
        ),
        4,
        scratch_shapes=[pltpu.VMEM((2, BINS, 8, NF), jnp.float32)],
    )(masks, own, near, far)
    chip_pairs = [(2 * k, 2 * k + 1) for k in range(count // 2)]
    cross_pairs = [((2 * k + 2) % count, 2 * k + 1) for k in range(count // 2)]
    both = ("chan", "period")
    groups = [[c * periods + p for c in pair for p in range(periods)] for pair in chip_pairs]
    wide = lax.all_to_all(wide, both, 0, 0, tiled=True, axis_index_groups=groups)
    groups = [[c * periods + p for c in pair for p in range(periods)] for pair in cross_pairs]
    half = lax.all_to_all(half, both, 0, 0, tiled=True, axis_index_groups=groups)
    stacks = call(
        stack_kernel,
        jax.ShapeDtypeStruct((CAP * NP, WIN), jnp.float32),
        5,
        in_specs=[smem, vmem, vmem, vmem, vmem],
        scratch_shapes=[pltpu.VMEM((2 * BINS, 2 * NF), jnp.float32), pltpu.VMEM((CAP * NP, 2 * NF), jnp.float32)],
    )(place, wide, half, jnp.asarray(slant_tables()), jnp.asarray(lag_table()))
    return stacks.reshape(CAP, NP, WIN)


def solution(mesh):
    placed = (P("period", "chan", None), P(None, "chan", None), P())
    return jax.shard_map(
        shards, mesh=mesh, in_specs=placed, out_specs=P("chan", None, None), check_vma=False
    )
```

profile of v0, /device:TPU:8, one launch (start us, length us, event | category | flops | bytes accessed | tf_op | source)
XLA Modules:
  0.0 78.6 jit_solution(8480795894780465622)
XLA Ops:
  0.0 0.0 copy-start
  0.0 0.9 %copy-done = bf16[1,16,8192]{2,1,0:T(8,128)(2,1)S(1)} copy-done((bf16[1,16,8192]{2,1,0:T(8,128)(2,1)S(1)}, bf16[1,16,8192]{2,1,0:T(8,128)(2,1)}, u32[]{:S(2)}) %copy-start) | copy-done | bytes 262168
  1.0 0.1 shard_map.65
  1.1 0.0 copy-start.3
  1.1 32.1 %all_to_all.15 = bf16[128,8,128]{2,1,0:T(8,128)(2,1)S(1)} all-to-all(bf16[128,8,128]{2,1,0:T(8,128)(2,1)S(1)} %bitcast.6), channel_id=1, replica_groups=mesh['chan'=128,'period'=4] {'chan'}, dimensions={0} | all-to-all | bytes 524288 | tf_op jit(solution)/shard_map/all_to_all | solution.py:165
  33.2 0.0 copy-done.3
  33.2 0.0 copy-start.4
  33.2 0.5 shard_map.66.own_ref
  33.6 0.0 copy-start.5
  33.7 1.9 %collective-permute-start = (bf16[8,64,256]{2,1,0:T(8,128)(2,1)S(1)}, bf16[8,64,256]{2,1,0:T(8,128)(2,1)S(1)}, u32[]{:S(2)}, u32[]{:S(2)}) collective-permute-start(bf16[8,64,256]{2,1,0:T(8,128)(2,1)S(1)} %shard_map.66.own_ref), channel_id=1, source_target_pairs={{0,4},{4,8},{8,12},{12,16},{16,20},{20,24},{24,28},{28,32},{32,36}... | collective-permute-start | bytes 786440 | tf_op jit(solution)/shard_map/ppermute | solution.py:178
  35.6 2.5 %collective-permute-start.1 = (bf16[8,64,256]{2,1,0:T(8,128)(2,1)S(1)}, bf16[8,64,256]{2,1,0:T(8,128)(2,1)S(1)}, u32[]{:S(2)}, u32[]{:S(2)}) collective-permute-start(bf16[8,64,256]{2,1,0:T(8,128)(2,1)S(1)} %shard_map.66.own_ref), channel_id=1, source_target_pairs={{0,8},{4,12},{8,16},{12,20},{16,24},{20,28},{24,32},{28,36},{32,40... | collective-permute-start | bytes 786440 | tf_op jit(solution)/shard_map/ppermute | solution.py:179
  38.1 0.0 copy-done.4
  38.1 0.0 copy-done.5
  38.1 0.7 shard_map.64
  38.8 4.9 %collective-permute-done.near_ref = bf16[8,64,256]{2,1,0:T(8,128)(2,1)S(1)} collective-permute-done((bf16[8,64,256]{2,1,0:T(8,128)(2,1)S(1)}, bf16[8,64,256]{2,1,0:T(8,128)(2,1)S(1)}, u32[]{:S(2)}, u32[]{:S(2)}) %collective-permute-start) | collective-permute-done | bytes 262176 | tf_op jit(solution)/shard_map/ppermute | solution.py:178
  43.7 5.1 %collective-permute-done.1.far_ref = bf16[8,64,256]{2,1,0:T(8,128)(2,1)S(1)} collective-permute-done((bf16[8,64,256]{2,1,0:T(8,128)(2,1)S(1)}, bf16[8,64,256]{2,1,0:T(8,128)(2,1)S(1)}, u32[]{:S(2)}, u32[]{:S(2)}) %collective-permute-start.1) | collective-permute-done | bytes 262176 | tf_op jit(solution)/shard_map/ppermute | solution.py:179
  48.8 5.8 %shard_map.67 = (f32[8,32,256]{2,1,0:T(8,128)S(1)}, f32[8,16,256]{2,1,0:T(8,128)S(1)}) custom-call(bf16[2048,192]{1,0:T(8,128)(2,1)S(1)} %get-tuple-element.10.masks_ref, bf16[8,64,256]{2,1,0:T(8,128)(2,1)S(1)} %shard_map.66.own_ref, bf16[8,64,256]{2,1,0:T(8,128)(2,1)S(1)} %collective-permute-done.near_ref, ...), custom_call_target="tpu_custom_call" | custom-call | tf_op jit(solution)/shard_map/pallas_call | solution.py:180
  54.6 0.0 copy-start.2
  54.7 11.1 %all_to_all.16.wide_ref = f32[8,32,256]{2,1,0:T(8,128)S(1)} all-to-all(f32[8,32,256]{2,1,0:T(8,128)S(1)} %get-tuple-element.11), channel_id=1, replica_groups={{0,1,2,3,4,5,6,7},{8,9,10,11,12,13,14,15},{16,17,18,19,20,21,22,23},{24..., dimensions={0} | all-to-all | bytes 524288 | tf_op jit(solution)/shard_map/all_to_all | solution.py:193
  65.8 0.0 copy-start.1
  65.8 11.1 %all_to_all.17.half_ref = f32[8,16,256]{2,1,0:T(8,128)S(1)} all-to-all(f32[8,16,256]{2,1,0:T(8,128)S(1)} %get-tuple-element.12), channel_id=1, replica_groups={{8,9,10,11,4,5,6,7},{16,17,18,19,12,13,14,15},{24,25,26,27,20,21,22,23}..., dimensions={0} | all-to-all | bytes 262144 | tf_op jit(solution)/shard_map/all_to_all | solution.py:195
  76.9 0.0 copy-done.2
  76.9 0.0 copy-done.1
  76.9 1.7 %shard_map.68 = f32[128,256]{1,0:T(8,128)} custom-call(s32[2]{0:T(128)S(1)} %get-tuple-element.9.place_ref, f32[8,32,256]{2,1,0:T(8,128)S(1)} %all_to_all.16.wide_ref, f32[8,16,256]{2,1,0:T(8,128)S(1)} %all_to_all.17.half_ref, f32[2,8,32,128]{3,2,1,0:T(8,128)S(1)} %copy-done.1, f32[256,256]{1,0:T(8,128)S(1)} %copy-done.2), custom_call_target="tpu_custom_call" | custom-call | tf_op jit(solution)/shard_map/pallas_call | solution.py:196
Async XLA Ops:
  0.0 0.9 %copy-start = (bf16[1,16,8192]{2,1,0:T(8,128)(2,1)S(1)}, bf16[1,16,8192]{2,1,0:T(8,128)(2,1)}, u32[]{:S(2)}) copy-start(bf16[1,16,8192]{2,1,0:T(8,128)(2,1)} %param.6) | copy-start | bytes 786436
  1.1 32.1 %copy-start.3 = (bf16[256,256]{1,0:T(8,128)(2,1)S(1)}, bf16[256,256]{1,0:T(8,128)(2,1)}, u32[]{:S(2)}) copy-start(bf16[256,256]{1,0:T(8,128)(2,1)} %constant.6.clone.table_ref) | copy-start | bytes 393220
  33.2 4.9 %copy-start.4 = (s32[3,64,64]{2,1,0:T(8,128)S(1)}, s32[3,64,64]{2,1,0:T(8,128)}, u32[]{:S(2)}) copy-start(s32[3,64,64]{2,1,0:T(8,128)} %ids_ref.1) | copy-start | bytes 147460
  33.6 4.4 %copy-start.5 = (s32[256]{0:T(256)S(1)}, s32[256]{0:T(256)}, u32[]{:S(2)}) copy-start(s32[256]{0:T(256)} %param.8) | copy-start | bytes 3076
  33.7 10.0 %collective-permute-start = (bf16[8,64,256]{2,1,0:T(8,128)(2,1)S(1)}, bf16[8,64,256]{2,1,0:T(8,128)(2,1)S(1)}, u32[]{:S(2)}, u32[]{:S(2)}) collective-permute-start(bf16[8,64,256]{2,1,0:T(8,128)(2,1)S(1)} %shard_map.66.own_ref), channel_id=1, source_target_pairs={{0,4},{4,8},{8,12},{12,16},{16,20},{20,24},{24,28},{28,32},{32,36}... | collective-permute-start | bytes 786440 | tf_op jit(solution)/shard_map/ppermute | solution.py:178
  35.6 13.2 %collective-permute-start.1 = (bf16[8,64,256]{2,1,0:T(8,128)(2,1)S(1)}, bf16[8,64,256]{2,1,0:T(8,128)(2,1)S(1)}, u32[]{:S(2)}, u32[]{:S(2)}) collective-permute-start(bf16[8,64,256]{2,1,0:T(8,128)(2,1)S(1)} %shard_map.66.own_ref), channel_id=1, source_target_pairs={{0,8},{4,12},{8,16},{12,20},{16,24},{20,28},{24,32},{28,36},{32,40... | collective-permute-start | bytes 786440 | tf_op jit(solution)/shard_map/ppermute | solution.py:179
  54.6 22.3 %copy-start.2 = (f32[256,256]{1,0:T(8,128)S(1)}, f32[256,256]{1,0:T(8,128)}, u32[]{:S(2)}) copy-start(f32[256,256]{1,0:T(8,128)} %constant.8.clone.lags_ref) | copy-start | bytes 786436
  65.8 11.1 %copy-start.1 = (f32[2,8,32,128]{3,2,1,0:T(8,128)S(1)}, f32[2,8,32,128]{3,2,1,0:T(8,128)}, u32[]{:S(2)}) copy-start(f32[2,8,32,128]{3,2,1,0:T(8,128)} %constant.7.clone.slant_ref) | copy-start | bytes 786436
where the time goes:
time: 78.9 us; the launch traced here: 78.6 us
  blocking collectives  54.3 us (69%)
  waiting for transfers between devices  9.99 us (13%)
  Pallas kernels  8.87 us (11%)
  starting transfers between devices  4.41 us (6%)
  local copies, waits for them, and re-layouts  0.98 us (1%)
    all_to_all x1, blocking collectives, shards(): lax.all_to_all(packed.reshape(count, 8, 128), 'chan', 0, 0, tiled=True)  32.1 us
    all_to_all x1, blocking collectives, shards(): lax.all_to_all(wide, both, 0, 0, tiled=True, axis_index_groups=groups)  11.1 us
    all_to_all x1, blocking collectives, shards(): lax.all_to_all(half, both, 0, 0, tiled=True, axis_index_groups=groups)  11.1 us
    pallas_call x1, Pallas kernels, shards(): call(bin_kernel, (jax.ShapeDtypeStruct((8, BINS, 2 * NF), jnp.float32), j...  5.8 us
    ppermute x1, waiting for transfers between devices, shards(): far = lax.ppermute(own, 'chan', [(i, i + 2) for i in range(count - 2)])  5.14 us
    ppermute x1, waiting for transfers between devices, shards(): near = lax.ppermute(own, 'chan', [(i, i + 1) for i in range(count - 1)])  4.85 us
    ppermute x1, starting transfers between devices, shards(): far = lax.ppermute(own, 'chan', [(i, i + 2) for i in range(count - 2)])  2.49 us
    ppermute x1, starting transfers between devices, shards(): near = lax.ppermute(own, 'chan', [(i, i + 1) for i in range(count - 1)])  1.92 us
  transfers between devices with their start and end apart: 2, of which 2 were waited for; matrix products, arithmetic and copies ran while one was open for 0% of the time, Pallas kernels for 1%

commit v1 on v0

--- a/solution.py
+++ b/solution.py
@@ -42,10 +42,11 @@
     return np.stack([np.cos(phase), np.sin(phase)]).astype(np.float32)
 
 
-def call(kernel, out_shape, n_in, **kw):
+def call(kernel, out_shape, n_in, flops=0, **kw):
     return pl.pallas_call(
         kernel,
         out_shape=out_shape,
+        cost_estimate=pl.CostEstimate(flops=flops, bytes_accessed=flops // 256, transcendentals=0),
         compiler_params=pltpu.CompilerParams(vmem_limit_bytes=VMEM_LIMIT),
         **kw,
     )
@@ -61,12 +62,15 @@
         out_ref[tile] = jnp.concatenate([even, odd], axis=0).astype(jnp.bfloat16)
 
 
-def mask_kernel(ids_ref, owner_ref, masks_ref, place_ref):
+def mask_kernel(ids_ref, masks_ref):
     ids = jnp.concatenate([ids_ref[0], ids_ref[1], ids_ref[2]], axis=1)
     for bin_at in range(BINS):
         masks_ref[bin_at * CH_DEV : (bin_at + 1) * CH_DEV, :] = (
             (ids == bin_at).astype(jnp.float32).astype(jnp.bfloat16)
         )
+
+
+def place_kernel(owner_ref, place_ref):
     device = lax.axis_index("chan")
     owner = owner_ref[...]
     place_ref[0] = jnp.sum((owner < device).astype(jnp.int32)) - MB_DEV * (device - 1)
@@ -84,32 +88,38 @@
 
 
 def bin_kernel(masks_ref, own_ref, near_ref, far_ref, wide_ref, half_ref, sums):
-    def add_window(window, carry):
-        own = own_ref[window]
-        partners = jnp.concatenate([own, near_ref[window], far_ref[window]], axis=0)
-        own = own.astype(jnp.float32)
-        own_real, own_imag = own[:, :NF], own[:, NF:]
-        for bin_at in range(BINS):
-            picked = jnp.dot(
-                masks_ref[bin_at * CH_DEV : (bin_at + 1) * CH_DEV, :],
-                partners,
-                preferred_element_type=jnp.float32,
-            )
-            picked_real, picked_imag = picked[:, :NF], picked[:, NF:]
-            real = own_real * picked_real + own_imag * picked_imag
-            imag = own_imag * picked_real - own_real * picked_imag
-            sums[0, bin_at] += jnp.sum(real.reshape(8, 8, NF), axis=0)
-            sums[1, bin_at] += jnp.sum(imag.reshape(8, 8, NF), axis=0)
+    step = 16
+
+    def add_bins(at, carry):
+        totals = None
+        rows = pl.ds(pl.multiple_of(at * step * CH_DEV, step * CH_DEV), step * CH_DEV)
+        for window in range(NWIN):
+            own = own_ref[window]
+            partners = jnp.concatenate([own, near_ref[window], far_ref[window]], axis=0)
+            own = own.astype(jnp.float32)
+            own_real, own_imag = own[:, :NF], own[:, NF:]
+            picked = jnp.dot(masks_ref[rows, :], partners, preferred_element_type=jnp.float32)
+            terms = []
+            for bin_at in range(step):
+                picked_real = picked[bin_at * CH_DEV : (bin_at + 1) * CH_DEV, :NF]
+                picked_imag = picked[bin_at * CH_DEV : (bin_at + 1) * CH_DEV, NF:]
+                real = own_real * picked_real + own_imag * picked_imag
+                imag = own_imag * picked_real - own_real * picked_imag
+                terms.append(jnp.sum(real.reshape(8, 8, NF), axis=0))
+                terms.append(jnp.sum(imag.reshape(8, 8, NF), axis=0))
+            totals = terms if totals is None else [x + y for x, y in zip(totals, terms)]
+        for bin_at in range(step):
+            sums[0, at * step + bin_at] = totals[2 * bin_at]
+            sums[1, at * step + bin_at] = totals[2 * bin_at + 1]
         return carry
 
-    sums[...] = jnp.zeros_like(sums)
-    lax.fori_loop(0, NWIN, add_window, 0)
+    lax.fori_loop(0, BINS // step, add_bins, 0)
     binned = jnp.concatenate([jnp.sum(sums[0], axis=1), jnp.sum(sums[1], axis=1)], axis=1)
     odd = lax.rem(lax.axis_index("chan"), 2)
     half = jnp.where(odd == 1, binned[BINS // 2 :], binned[: BINS // 2])
     for place in range(8):
-        wide_ref[place] = binned
-        half_ref[place] = half
+        wide_ref[place] = binned.astype(jnp.bfloat16)
+        half_ref[place] = half.astype(jnp.bfloat16)
 
 
 def stack_kernel(place_ref, wide_ref, half_ref, slant_ref, lags_ref, out_ref, held, spec):
@@ -118,13 +128,13 @@
     whole = BINS // 2
 
     def over_periods(ref, part, rows):
-        total = ref[part * 4, rows]
+        total = ref[part * 4, rows].astype(jnp.float32)
         for period in range(1, 4):
-            total = total + ref[part * 4 + period, rows]
+            total = total + ref[part * 4 + period, rows].astype(jnp.float32)
         return total
 
     own = over_periods(wide_ref, odd, pl.ds(0, BINS))
-    beside = over_periods(wide_ref, 1 - odd, pl.ds(pl.multiple_of(odd * whole, 8), whole))
+    beside = over_periods(wide_ref, 1 - odd, pl.ds(pl.multiple_of(odd * whole, 16), whole))
     across = over_periods(half_ref, 1 - odd, pl.ds(0, whole))
     has_across = (device > 0) & (device < lax.axis_size("chan") - 1)
     across = jnp.where(has_across, across, 0.0)
@@ -163,15 +173,13 @@
     vmem = pl.BlockSpec(memory_space=pltpu.VMEM)
     packed = call(pack_kernel, jax.ShapeDtypeStruct((count // 2, 16, 128), jnp.bfloat16), 1)(raw_strain[0])
     series = lax.all_to_all(packed.reshape(count, 8, 128), "chan", 0, 0, tiled=True)
-    masks, place = call(
+    masks = call(
         mask_kernel,
-        (
-            jax.ShapeDtypeStruct((BINS * CH_DEV, 3 * CH_DEV), jnp.bfloat16),
-            jax.ShapeDtypeStruct((2,), jnp.int32),
-        ),
-        2,
-        out_specs=(vmem, smem),
-    )(bin_ids, owner_map.reshape(2, 128))
+        jax.ShapeDtypeStruct((BINS * CH_DEV, 3 * CH_DEV), jnp.bfloat16),
+        1,
+        flops=4000000000,
+    )(bin_ids)
+    series, masks = lax.optimization_barrier((series, masks))
     own = call(spectra_kernel, jax.ShapeDtypeStruct((NWIN, CH_DEV, 2 * NF), jnp.bfloat16), 2)(
         series.reshape(NWIN, 128, 128), jnp.asarray(dft_rows(), jnp.bfloat16)
     )
@@ -180,8 +188,8 @@
     wide, half = call(
         bin_kernel,
         (
-            jax.ShapeDtypeStruct((8, BINS, 2 * NF), jnp.float32),
-            jax.ShapeDtypeStruct((8, BINS // 2, 2 * NF), jnp.float32),
+            jax.ShapeDtypeStruct((8, BINS, 2 * NF), jnp.bfloat16),
+            jax.ShapeDtypeStruct((8, BINS // 2, 2 * NF), jnp.bfloat16),
         ),
         4,
         scratch_shapes=[pltpu.VMEM((2, BINS, 8, NF), jnp.float32)],
@@ -189,10 +197,15 @@
     chip_pairs = [(2 * k, 2 * k + 1) for k in range(count // 2)]
     cross_pairs = [((2 * k + 2) % count, 2 * k + 1) for k in range(count // 2)]
     both = ("chan", "period")
+    wide, half, owner_map = lax.optimization_barrier((wide, half, owner_map))
     groups = [[c * periods + p for c in pair for p in range(periods)] for pair in chip_pairs]
     wide = lax.all_to_all(wide, both, 0, 0, tiled=True, axis_index_groups=groups)
     groups = [[c * periods + p for c in pair for p in range(periods)] for pair in cross_pairs]
     half = lax.all_to_all(half, both, 0, 0, tiled=True, axis_index_groups=groups)
+    place = call(
+        place_kernel, jax.ShapeDtypeStruct((2,), jnp.int32), 1, flops=4000000000, out_specs=smem
+    )(owner_map.reshape(2, 128))
+    wide, half, place = lax.optimization_barrier((wide, half, place))
     stacks = call(
         stack_kernel,
         jax.ShapeDtypeStruct((CAP * NP, WIN), jnp.float32),

time: 78.9 us -> 75 us (0.951)
  blocking collectives: 54.3 us -> 9.64 us
  starting transfers between devices: 4.41 us -> 25.3 us
  waiting for transfers between devices: 9.99 us -> 30.8 us
  Pallas kernels: 8.87 us -> 7.23 us
    all_to_all x2 -> x0, blocking collectives: 43.2 us -> none  [the longest x1 32.1 us: shards(): lax.all_to_all(packed.reshape(count, 8, 128), 'chan', 0, 0, tiled=True)]
    all_to_all x0 -> x2, waiting for transfers between devices: none -> 20.9 us  [the longest x1 14.5 us: shards(): lax.all_to_all(packed.reshape(count, 8, 128), 'chan', 0, 0, tiled=True)]
    all_to_all x0 -> x2, starting transfers between devices: none -> 20.9 us  [the longest x1 17.5 us: shards(): lax.all_to_all(packed.reshape(count, 8, 128), 'chan', 0, 0, tiled=True)]
    ppermute x1, waiting for transfers between devices: 4.85 us -> 1.02 us  [shards(): near = lax.ppermute(own, 'chan', [(i, i + 1) for i in range(count - 1)])]
    ppermute x1, waiting for transfers between devices: 5.14 us -> 8.82 us  [shards(): far = lax.ppermute(own, 'chan', [(i, i + 2) for i in range(count - 2)])]
    pallas_call x2 -> x3, Pallas kernels: 6.54 us -> 4.17 us  [the longest x1 3.26 us: shards(): call(bin_kernel, (jax.ShapeDtypeStruct((8, BINS, 2 * NF), jnp.bfloat16),...]
    all_to_all x1, blocking collectives: 11.1 us -> 9.64 us  [shards(): lax.all_to_all(wide, both, 0, 0, tiled=True, axis_index_groups=groups)]
  transfers between devices with their start and end apart: 2 -> 4, of which waited for: 2 -> 4; matrix products, arithmetic and copies ran while one was open for 0% -> 0% of each run, Pallas kernels for 1% -> 1%
where the time goes in v1:
time: 75 us; the launch traced here: 74.6 us
  waiting for transfers between devices  30.8 us (41%)
  starting transfers between devices  25.3 us (34%)
  blocking collectives  9.64 us (13%)
  Pallas kernels  7.23 us (10%)
  local copies, waits for them, and re-layouts  1.64 us (2%)
    all_to_all x1, starting transfers between devices, shards(): lax.all_to_all(packed.reshape(count, 8, 128), 'chan', 0, 0, tiled=True)  17.5 us
    all_to_all x1, waiting for transfers between devices, shards(): lax.all_to_all(packed.reshape(count, 8, 128), 'chan', 0, 0, tiled=True)  14.5 us
    all_to_all x1, blocking collectives, shards(): lax.all_to_all(wide, both, 0, 0, tiled=True, axis_index_groups=groups)  9.64 us
    ppermute x1, waiting for transfers between devices, shards(): far = lax.ppermute(own, 'chan', [(i, i + 2) for i in range(count - 2)])  8.82 us
    all_to_all x1, waiting for transfers between devices, shards(): lax.all_to_all(half, both, 0, 0, tiled=True, axis_index_groups=groups)  6.4 us
    all_to_all x1, starting transfers between devices, shards(): lax.all_to_all(half, both, 0, 0, tiled=True, axis_index_groups=groups)  3.35 us
    pallas_call x1, Pallas kernels, shards(): call(bin_kernel, (jax.ShapeDtypeStruct((8, BINS, 2 * NF), jnp.bfloat16),...  3.26 us
    ppermute x1, starting transfers between devices, shards(): far = lax.ppermute(own, 'chan', [(i, i + 2) for i in range(count - 2)])  2.49 us
  transfers between devices with their start and end apart: 4, of which 4 were waited for; matrix products, arithmetic and copies ran while one was open for 0% of the time, Pallas kernels for 1%

profile of v1, /device:TPU:8, one launch (start us, length us, event | category | flops | bytes accessed | tf_op | source)
XLA Modules:
  0.0 74.6 jit_solution(1386084272205760160)
XLA Ops:
  0.0 0.0 copy-start.2
  0.0 0.9 %copy-done.2 = bf16[1,16,8192]{2,1,0:T(8,128)(2,1)S(1)} copy-done((bf16[1,16,8192]{2,1,0:T(8,128)(2,1)S(1)}, bf16[1,16,8192]{2,1,0:T(8,128)(2,1)}, u32[]{:S(2)}) %copy-start.2) | copy-done | bytes 262168
  1.0 0.8 %shard_map.64 = bf16[64,16,128]{2,1,0:T(8,128)(2,1)} custom-call(bf16[16,8192]{1,0:T(8,128)(2,1)S(1)} %bitcast.6), custom_call_target="tpu_custom_call" | custom-call | tf_op jit(solution)/shard_map/pallas_call | solution.py:174
  1.8 17.5 %all-to-all-start = ((bf16[128,8,128]{2,1,0:T(8,128)(2,1)}), bf16[128,8,128]{2,1,0:T(8,128)(2,1)S(1)}, u32[]{:S(2)}, u32[]{:S(2)}) async-start(bf16[128,8,128]{2,1,0:T(8,128)(2,1)} %bitcast.1), calls=%async_computation | async-start | bytes 524288 | tf_op jit(solution)/shard_map/all_to_all | solution.py:175
  19.3 0.0 copy-done.4
  19.3 0.0 copy-start.3
  19.3 0.2 shard_map.65.masks_ref
  19.5 14.5 %all-to-all-done = bf16[128,8,128]{2,1,0:T(8,128)(2,1)S(1)} async-done(((bf16[128,8,128]{2,1,0:T(8,128)(2,1)}), bf16[128,8,128]{2,1,0:T(8,128)(2,1)S(1)}, u32[]{:S(2)}, u32[]{:S(2)}) %all-to-all-start) | async-done | bytes 262176 | tf_op jit(solution)/shard_map/all_to_all | solution.py:175
  34.1 0.0 copy-done.3
  34.1 0.5 shard_map.66.own_ref
  34.5 2.5 %collective-permute-start.1 = (bf16[8,64,256]{2,1,0:T(8,128)(2,1)S(1)}, bf16[8,64,256]{2,1,0:T(8,128)(2,1)S(1)}, u32[]{:S(2)}, u32[]{:S(2)}) collective-permute-start(bf16[8,64,256]{2,1,0:T(8,128)(2,1)S(1)} %shard_map.66.own_ref), channel_id=1, source_target_pairs={{0,8},{4,12},{8,16},{12,20},{16,24},{20,28},{24,32},{28,36},{32,40... | collective-permute-start | bytes 786440 | tf_op jit(solution)/shard_map/ppermute | solution.py:187
  37.0 1.9 %collective-permute-start = (bf16[8,64,256]{2,1,0:T(8,128)(2,1)S(1)}, bf16[8,64,256]{2,1,0:T(8,128)(2,1)S(1)}, u32[]{:S(2)}, u32[]{:S(2)}) collective-permute-start(bf16[8,64,256]{2,1,0:T(8,128)(2,1)S(1)} %shard_map.66.own_ref), channel_id=1, source_target_pairs={{0,4},{4,8},{8,12},{12,16},{16,20},{20,24},{24,28},{28,32},{32,36}... | collective-permute-start | bytes 786440 | tf_op jit(solution)/shard_map/ppermute | solution.py:186
  39.0 8.8 %collective-permute-done.1.far_ref = bf16[8,64,256]{2,1,0:T(8,128)(2,1)S(1)} collective-permute-done((bf16[8,64,256]{2,1,0:T(8,128)(2,1)S(1)}, bf16[8,64,256]{2,1,0:T(8,128)(2,1)S(1)}, u32[]{:S(2)}, u32[]{:S(2)}) %collective-permute-start.1) | collective-permute-done | bytes 262176 | tf_op jit(solution)/shard_map/ppermute | solution.py:187
  47.8 1.0 %collective-permute-done.near_ref = bf16[8,64,256]{2,1,0:T(8,128)(2,1)S(1)} collective-permute-done((bf16[8,64,256]{2,1,0:T(8,128)(2,1)S(1)}, bf16[8,64,256]{2,1,0:T(8,128)(2,1)S(1)}, u32[]{:S(2)}, u32[]{:S(2)}) %collective-permute-start) | collective-permute-done | bytes 262176 | tf_op jit(solution)/shard_map/ppermute | solution.py:186
  48.8 3.3 %shard_map.67 = (bf16[8,32,256]{2,1,0:T(8,128)(2,1)S(1)}, bf16[8,16,256]{2,1,0:T(8,128)(2,1)}) custom-call(bf16[2048,192]{1,0:T(8,128)(2,1)S(1)} %shard_map.65.masks_ref, bf16[8,64,256]{2,1,0:T(8,128)(2,1)S(1)} %shard_map.66.own_ref, bf16[8,64,256]{2,1,0:T(8,128)(2,1)S(1)} %collective-permute-done.near_ref, ...), custom_call_target="tpu_custom_call" | custom-call | tf_op jit(solution)/shard_map/pallas_call | solution.py:188
  52.1 9.6 %all_to_all.15.wide_ref = bf16[8,32,256]{2,1,0:T(8,128)(2,1)S(1)} all-to-all(bf16[8,32,256]{2,1,0:T(8,128)(2,1)S(1)} %get-tuple-element.19), channel_id=1, replica_groups={{0,1,2,3,4,5,6,7},{8,9,10,11,12,13,14,15},{16,17,18,19,20,21,22,23},{24..., dimensions={0} | all-to-all | bytes 262144 | tf_op jit(solution)/shard_map/all_to_all | solution.py:202
  61.7 3.4 %all-to-all-start.2 = ((bf16[8,16,256]{2,1,0:T(8,128)(2,1)}), bf16[8,16,256]{2,1,0:T(8,128)(2,1)S(1)}, u32[]{:S(2)}, u32[]{:S(2)}) async-start(bf16[8,16,256]{2,1,0:T(8,128)(2,1)} %get-tuple-element.20), calls=%async_computation.2 | async-start | bytes 131072 | tf_op jit(solution)/shard_map/all_to_all | solution.py:204
  65.1 0.0 copy-start.5
  65.1 0.7 copy-done.5
  65.8 0.7 shard_map.68.place_ref
  66.5 6.4 %all-to-all-done.2.half_ref = bf16[8,16,256]{2,1,0:T(8,128)(2,1)S(1)} async-done(((bf16[8,16,256]{2,1,0:T(8,128)(2,1)}), bf16[8,16,256]{2,1,0:T(8,128)(2,1)S(1)}, u32[]{:S(2)}, u32[]{:S(2)}) %all-to-all-start.2) | async-done | bytes 65568 | tf_op jit(solution)/shard_map/all_to_all | solution.py:204
  72.9 0.0 copy-done
  72.9 0.0 copy-done.1
  72.9 1.7 %shard_map.69 = f32[128,256]{1,0:T(8,128)} custom-call(s32[2]{0:T(128)S(1)} %shard_map.68.place_ref, bf16[8,32,256]{2,1,0:T(8,128)(2,1)S(1)} %all_to_all.15.wide_ref, bf16[8,16,256]{2,1,0:T(8,128)(2,1)S(1)} %all-to-all-done.2.half_ref, f32[2,8,32,128]{3,2,1,0:T(8,128)S(1)} %copy-done.1, f32[256,256]{1,0:T(8,128)S(1)} %copy-done), custom_call_target="tpu_custom_call" | custom-call | tf_op jit(solution)/shard_map/pallas_call | solution.py:209
  (3 shorter events, 0.0 us)
Async XLA Ops:
  0.0 0.9 %copy-start.2 = (bf16[1,16,8192]{2,1,0:T(8,128)(2,1)S(1)}, bf16[1,16,8192]{2,1,0:T(8,128)(2,1)}, u32[]{:S(2)}) copy-start(bf16[1,16,8192]{2,1,0:T(8,128)(2,1)} %param.6) | copy-start | bytes 786436
  1.8 17.5 %copy-start.4 = (s32[3,64,64]{2,1,0:T(8,128)S(1)}, s32[3,64,64]{2,1,0:T(8,128)}, u32[]{:S(2)}) copy-start(s32[3,64,64]{2,1,0:T(8,128)} %ids_ref.1) | copy-start | bytes 147460
  1.8 32.3 %all-to-all-start = ((bf16[128,8,128]{2,1,0:T(8,128)(2,1)}), bf16[128,8,128]{2,1,0:T(8,128)(2,1)S(1)}, u32[]{:S(2)}, u32[]{:S(2)}) async-start(bf16[128,8,128]{2,1,0:T(8,128)(2,1)} %bitcast.1), calls=%async_computation | async-start | bytes 524288 | tf_op jit(solution)/shard_map/all_to_all | solution.py:175
  19.3 14.7 %copy-start.3 = (bf16[256,256]{1,0:T(8,128)(2,1)S(1)}, bf16[256,256]{1,0:T(8,128)(2,1)}, u32[]{:S(2)}) copy-start(bf16[256,256]{1,0:T(8,128)(2,1)} %constant.6.clone.table_ref) | copy-start | bytes 393220
  34.5 13.2 %collective-permute-start.1 = (bf16[8,64,256]{2,1,0:T(8,128)(2,1)S(1)}, bf16[8,64,256]{2,1,0:T(8,128)(2,1)S(1)}, u32[]{:S(2)}, u32[]{:S(2)}) collective-permute-start(bf16[8,64,256]{2,1,0:T(8,128)(2,1)S(1)} %shard_map.66.own_ref), channel_id=1, source_target_pairs={{0,8},{4,12},{8,16},{12,20},{16,24},{20,28},{24,32},{28,36},{32,40... | collective-permute-start | bytes 786440 | tf_op jit(solution)/shard_map/ppermute | solution.py:187
  37.0 11.8 %collective-permute-start = (bf16[8,64,256]{2,1,0:T(8,128)(2,1)S(1)}, bf16[8,64,256]{2,1,0:T(8,128)(2,1)S(1)}, u32[]{:S(2)}, u32[]{:S(2)}) collective-permute-start(bf16[8,64,256]{2,1,0:T(8,128)(2,1)S(1)} %shard_map.66.own_ref), channel_id=1, source_target_pairs={{0,4},{4,8},{8,12},{12,16},{16,20},{20,24},{24,28},{28,32},{32,36}... | collective-permute-start | bytes 786440 | tf_op jit(solution)/shard_map/ppermute | solution.py:186
  61.7 11.2 %all-to-all-start.2 = ((bf16[8,16,256]{2,1,0:T(8,128)(2,1)}), bf16[8,16,256]{2,1,0:T(8,128)(2,1)S(1)}, u32[]{:S(2)}, u32[]{:S(2)}) async-start(bf16[8,16,256]{2,1,0:T(8,128)(2,1)} %get-tuple-element.20), calls=%async_computation.2 | async-start | bytes 131072 | tf_op jit(solution)/shard_map/all_to_all | solution.py:204
  65.1 0.7 copy-start.5
  65.8 7.1 %copy-start = (f32[256,256]{1,0:T(8,128)S(1)}, f32[256,256]{1,0:T(8,128)}, u32[]{:S(2)}) copy-start(f32[256,256]{1,0:T(8,128)} %constant.8.clone.lags_ref) | copy-start | bytes 786436
  65.8 7.1 %copy-start.1 = (f32[2,8,32,128]{3,2,1,0:T(8,128)S(1)}, f32[2,8,32,128]{3,2,1,0:T(8,128)}, u32[]{:S(2)}) copy-start(f32[2,8,32,128]{3,2,1,0:T(8,128)} %constant.7.clone.slant_ref) | copy-start | bytes 786436

commit v2 on v0

v2 whole, which is shorter than its diff:
```python
import functools
import math

import jax
import jax.numpy as jnp
import numpy as np
from jax import lax
from jax.experimental import pallas as pl
from jax.experimental.pallas import tpu as pltpu
from jax.sharding import PartitionSpec as P

CH_DEV = 64
WIN = 256
NF = 128
NWIN = 8
MB_DEV = 2
NOFF = 8
NP = 32
CAP = 4
BINS = 2 * MB_DEV * NOFF
HALF = BINS // 2
VMEM_LIMIT = 48 * 1024 * 1024

ROW_SAMPLE = (
    16 * np.arange(16)[None, :, None] + 8 * np.arange(2)[:, None, None] + np.arange(8)[None, None, :]
).reshape(-1)


def dft_rows():
    phase = 2.0 * math.pi / WIN * np.mod(ROW_SAMPLE[:, None] * np.arange(1, NF + 1)[None, :], WIN)
    return np.concatenate([np.cos(phase), -np.sin(phase)], axis=1).astype(np.float32)


def lag_table():
    phase = 2.0 * math.pi / WIN * np.mod(np.arange(1, NF + 1)[:, None] * np.arange(WIN)[None, :], WIN)
    return np.concatenate([np.cos(phase), -np.sin(phase)], axis=0).astype(np.float32)


def lag_parts():
    table = lag_table()
    high = table.astype(jnp.bfloat16)
    low = (table - high.astype(np.float32)).astype(jnp.bfloat16)
    return np.concatenate([high, high, low], axis=0)


def slant_tables():
    slow = (np.arange(NP) - NP // 2) / (4.0 * NP)
    offset = (np.arange(NOFF) + 0.5) * (3.0 * CH_DEV / NOFF)
    freq = np.arange(1, NF + 1) * (2.0 * math.pi / WIN)
    phase = offset[:, None, None] * slow[None, :, None] * freq[None, None, :]
    return np.stack([np.cos(phase), np.sin(phase)]).astype(np.float32)


def call(kernel, out_shape, flops=0, **kw):
    return pl.pallas_call(
        kernel,
        out_shape=out_shape,
        cost_estimate=pl.CostEstimate(flops=flops, bytes_accessed=flops // 256, transcendentals=0),
        compiler_params=pltpu.CompilerParams(vmem_limit_bytes=VMEM_LIMIT),
        **kw,
    )


def pack_kernel(raw_ref, out_ref):
    low = lax.broadcasted_iota(jnp.int32, (8, 128), 1) < 64
    for tile in range(raw_ref.shape[1] // 128):
        both = raw_ref[:, 128 * tile : 128 * tile + 128].astype(jnp.float32)
        first, second = both[:8], both[8:]
        even = jnp.where(low, first, pltpu.roll(second, 64, 1))
        odd = jnp.where(low, pltpu.roll(first, 64, 1), second)
        out_ref[tile] = jnp.concatenate([even, odd], axis=0).astype(jnp.bfloat16)


def mask_kernel(ids_ref, masks_ref):
    ids = jnp.concatenate([ids_ref[0], ids_ref[1], ids_ref[2]], axis=1)
    for bin_at in range(BINS):
        masks_ref[bin_at * CH_DEV : (bin_at + 1) * CH_DEV, :] = (
            (ids == bin_at).astype(jnp.float32).astype(jnp.bfloat16)
        )


def place_kernel(owner_ref, place_ref):
    device = lax.axis_index("chan")
    owner = owner_ref[...]
    place_ref[0] = jnp.sum((owner < device).astype(jnp.int32)) - MB_DEV * (device - 1)
    place_ref[1] = jnp.sum((owner == device).astype(jnp.int32))


def spectra_kernel(series_ref, table_ref, out_ref):
    table = table_ref[...]
    for window in range(NWIN):
        turned = series_ref[window].astype(jnp.float32).T.astype(jnp.bfloat16)
        series = jnp.concatenate([turned[:CH_DEV], turned[CH_DEV:]], axis=1)
        spectra = jnp.dot(series, table, preferred_element_type=jnp.float32)
        power = jnp.mean(spectra * spectra, axis=-1, keepdims=True)
        out_ref[window] = (spectra / jnp.sqrt(power + 1e-06)).astype(jnp.bfloat16)


def bin_kernel(across, masks_ref, own_ref, near_ref, far_ref, out_ref):
    odd = lax.rem(lax.axis_index("chan"), 2)
    part = odd if across else 1 - odd
    rows = pl.ds(pl.multiple_of(part * HALF * CH_DEV, HALF * CH_DEV), HALF * CH_DEV)
    totals = None
    for window in range(NWIN):
        own = own_ref[window]
        partners = jnp.concatenate([own, near_ref[window], far_ref[window]], axis=0)
        own = own.astype(jnp.float32)
        own_real, own_imag = own[:, :NF], own[:, NF:]
        picked = jnp.dot(masks_ref[rows, :], partners, preferred_element_type=jnp.float32)
        terms = []
        for bin_at in range(HALF):
            picked_real = picked[bin_at * CH_DEV : (bin_at + 1) * CH_DEV, :NF]
            picked_imag = picked[bin_at * CH_DEV : (bin_at + 1) * CH_DEV, NF:]
            real = own_real * picked_real + own_imag * picked_imag
            imag = own_imag * picked_real - own_real * picked_imag
            terms.append(jnp.sum(real.reshape(8, 8, NF), axis=0))
            terms.append(jnp.sum(imag.reshape(8, 8, NF), axis=0))
        totals = terms if totals is None else [x + y for x, y in zip(totals, terms)]
    for bin_at in range(HALF):
        out_ref[bin_at : bin_at + 1, :NF] = jnp.sum(totals[2 * bin_at], axis=0, keepdims=True)
        out_ref[bin_at : bin_at + 1, NF:] = jnp.sum(totals[2 * bin_at + 1], axis=0, keepdims=True)


def merge_kernel(across_ref, inside_ref, arrived_ref, out_ref):
    odd = lax.rem(lax.axis_index("chan"), 2)
    across = (across_ref[...] + arrived_ref[...]).astype(jnp.bfloat16)
    inside = inside_ref[...].astype(jnp.bfloat16)
    merged = jnp.concatenate(
        [jnp.where(odd == 1, inside, across), jnp.where(odd == 1, across, inside)], axis=0
    )
    for place in range(8):
        out_ref[place] = merged


def stack_kernel(place_ref, sums_ref, slant_ref, lags_ref, out_ref, held, spec):
    odd = lax.rem(lax.axis_index("chan"), 2)

    def over_periods(part, rows):
        total = sums_ref[part * 4, rows].astype(jnp.float32)
        for period in range(1, 4):
            total = total + sums_ref[part * 4 + period, rows].astype(jnp.float32)
        return total

    own = over_periods(odd, pl.ds(0, BINS))
    beside = over_periods(1 - odd, pl.ds(pl.multiple_of(odd * HALF, HALF), HALF))
    held[...] = jnp.zeros_like(held)
    held[:HALF] = own[:HALF] + jnp.where(odd == 1, beside, 0.0)
    held[HALF:BINS] = own[HALF:] + jnp.where(odd == 1, 0.0, beside)
    count = place_ref[1]
    first = jnp.where(count > 0, place_ref[0], 0)
    for slot in range(CAP):
        rows = held[pl.ds(pl.multiple_of((first + slot) * NOFF, 8), NOFF), :]
        rows = jnp.where(slot < count, rows, 0.0)
        real = jnp.zeros((NP, NF), jnp.float32)
        imag = jnp.zeros((NP, NF), jnp.float32)
        for offset in range(NOFF):
            bin_real = rows[offset : offset + 1, :NF]
            bin_imag = rows[offset : offset + 1, NF:]
            cos, sin = slant_ref[0, offset], slant_ref[1, offset]
            real = real + (bin_real * cos + bin_imag * sin)
            imag = imag + (bin_imag * cos - bin_real * sin)
        spec[slot * NP : (slot + 1) * NP, :NF] = real
        spec[slot * NP : (slot + 1) * NP, NF:] = imag
    whole = spec[...]
    high = whole.astype(jnp.bfloat16)
    low = (whole - high.astype(jnp.float32)).astype(jnp.bfloat16)
    traces = jnp.dot(
        jnp.concatenate([high, low, high], axis=1), lags_ref[...], preferred_element_type=jnp.float32
    )
    power = jnp.mean(traces * traces, axis=-1, keepdims=True)
    out_ref[...] = traces / jnp.sqrt(power + 1e-06)


def shards(raw_strain, bin_ids, owner_map):
    count = lax.axis_size("chan")
    periods = lax.axis_size("period")
    smem = pl.BlockSpec(memory_space=pltpu.SMEM)
    vmem = pl.BlockSpec(memory_space=pltpu.VMEM)
    packed = call(pack_kernel, jax.ShapeDtypeStruct((count // 2, 16, 128), jnp.bfloat16))(raw_strain[0])
    series = lax.all_to_all(packed.reshape(count, 8, 128), "chan", 0, 0, tiled=True)
    masks = call(
        mask_kernel,
        jax.ShapeDtypeStruct((BINS * CH_DEV, 3 * CH_DEV), jnp.bfloat16),
        flops=2000000000,
    )(bin_ids)
    own = call(spectra_kernel, jax.ShapeDtypeStruct((NWIN, CH_DEV, 2 * NF), jnp.bfloat16))(
        series.reshape(NWIN, 128, 128), jnp.asarray(dft_rows(), jnp.bfloat16)
    )
    near = lax.ppermute(own, "chan", [(i, i + 1) for i in range(count - 1)])
    far = lax.ppermute(own, "chan", [(i, i + 2) for i in range(count - 2)])
    place = call(place_kernel, jax.ShapeDtypeStruct((2,), jnp.int32), out_specs=smem)(
        owner_map.reshape(2, 128)
    )
    part = jax.ShapeDtypeStruct((HALF, 2 * NF), jnp.float32)
    across = call(functools.partial(bin_kernel, True), part)(masks, own, near, far)
    pairs = [(2 * k + 1, 2 * k + 2) for k in range(count // 2 - 1)]
    arrived = lax.ppermute(across, "chan", pairs + [(j, i) for i, j in pairs])
    inside = call(functools.partial(bin_kernel, False), part, flops=2000000000)(masks, own, near, far)
    merged = call(merge_kernel, jax.ShapeDtypeStruct((8, BINS, 2 * NF), jnp.bfloat16))(
        across, inside, arrived
    )
    groups = [
        [(2 * k + core) * periods + p for core in range(2) for p in range(periods)]
        for k in range(count // 2)
    ]
    sums = lax.all_to_all(
        merged, ("chan", "period"), 0, 0, tiled=True, axis_index_groups=groups
    )
    stacks = call(
        stack_kernel,
        jax.ShapeDtypeStruct((CAP * NP, WIN), jnp.float32),
        in_specs=[smem, vmem, vmem, vmem],
        scratch_shapes=[
            pltpu.VMEM((2 * BINS, 2 * NF), jnp.float32),
            pltpu.VMEM((CAP * NP, 2 * NF), jnp.float32),
        ],
    )(place, sums, jnp.asarray(slant_tables()), jnp.asarray(lag_parts()))
    return stacks.reshape(CAP, NP, WIN)


def solution(mesh):
    placed = (P("period", "chan", None), P(None, "chan", None), P())
    return jax.shard_map(
        shards, mesh=mesh, in_specs=placed, out_specs=P("chan", None, None), check_vma=False
    )
```

time: 78.9 us -> 69.1 us (0.88)
  blocking collectives: 54.3 us -> 32.1 us
  waiting for transfers between devices: 9.99 us -> 17.6 us
  starting transfers between devices: 4.41 us -> 10.6 us
  Pallas kernels: 8.87 us -> 6.44 us
    all_to_all x2 -> x0, blocking collectives: 22.2 us -> none  [the longest x1 11.1 us: shards(): lax.all_to_all(wide, both, 0, 0, tiled=True, axis_index_groups=groups)]
    all_to_all x0 -> x1, starting transfers between devices: none -> 4.3 us  [shards(): lax.all_to_all(merged, ('chan', 'period'), 0, 0, tiled=True, axis_index_g...]
    all_to_all x0 -> x1, waiting for transfers between devices: none -> 4.15 us  [shards(): lax.all_to_all(merged, ('chan', 'period'), 0, 0, tiled=True, axis_index_g...]
    ppermute x1, waiting for transfers between devices: 4.85 us -> 0.95 us  [shards(): near = lax.ppermute(own, 'chan', [(i, i + 1) for i in range(count - 1)])]
    ppermute x0 -> x1, waiting for transfers between devices: none -> 3.89 us  [shards(): arrived = lax.ppermute(across, 'chan', pairs + [(j, i) for i, j in pairs])]
    ppermute x1, waiting for transfers between devices: 5.14 us -> 8.61 us  [shards(): far = lax.ppermute(own, 'chan', [(i, i + 2) for i in range(count - 2)])]
    pallas_call x4 -> x7, Pallas kernels: 8.4 us -> 5.97 us  [the longest x1 1.63 us: shards(): call(stack_kernel, jax.ShapeDtypeStruct((CAP * NP, WIN), jnp.float32), in...]
    ppermute x0 -> x1, starting transfers between devices: none -> 1.92 us  [shards(): arrived = lax.ppermute(across, 'chan', pairs + [(j, i) for i, j in pairs])]
  transfers between devices with their start and end apart: 2 -> 4, of which waited for: 2 -> 4; matrix products, arithmetic and copies ran while one was open for 0% -> 0% of each run, Pallas kernels for 1% -> 3%
where the time goes in v2:
time: 69.1 us; the launch traced here: 68.5 us
  blocking collectives  32.1 us (46%)
  waiting for transfers between devices  17.6 us (25%)
  starting transfers between devices  10.6 us (15%)
  Pallas kernels  6.44 us (9%)
  local copies, waits for them, and re-layouts  1.65 us (2%)
    all_to_all x1, blocking collectives, shards(): lax.all_to_all(packed.reshape(count, 8, 128), 'chan', 0, 0, tiled=True)  32.1 us
    ppermute x1, waiting for transfers between devices, shards(): far = lax.ppermute(own, 'chan', [(i, i + 2) for i in range(count - 2)])  8.61 us
    all_to_all x1, starting transfers between devices, shards(): lax.all_to_all(merged, ('chan', 'period'), 0, 0, tiled=True, axis_index_g...  4.3 us
    all_to_all x1, waiting for transfers between devices, shards(): lax.all_to_all(merged, ('chan', 'period'), 0, 0, tiled=True, axis_index_g...  4.15 us
    ppermute x1, waiting for transfers between devices, shards(): arrived = lax.ppermute(across, 'chan', pairs + [(j, i) for i, j in pairs])  3.89 us
    ppermute x1, starting transfers between devices, shards(): far = lax.ppermute(own, 'chan', [(i, i + 2) for i in range(count - 2)])  2.49 us
    ppermute x1, starting transfers between devices, shards(): near = lax.ppermute(own, 'chan', [(i, i + 1) for i in range(count - 1)])  1.92 us
    ppermute x1, starting transfers between devices, shards(): arrived = lax.ppermute(across, 'chan', pairs + [(j, i) for i, j in pairs])  1.92 us
  transfers between devices with their start and end apart: 4, of which 4 were waited for; matrix products, arithmetic and copies ran while one was open for 0% of the time, Pallas kernels for 3%

profile of v2, /device:TPU:8, one launch (start us, length us, event | category | flops | bytes accessed | tf_op | source)
XLA Modules:
  0.0 68.5 jit_solution(9493768177306204546)
XLA Ops:
  0.0 0.9 %copy-done.2 = bf16[1,16,8192]{2,1,0:T(8,128)(2,1)S(1)} copy-done((bf16[1,16,8192]{2,1,0:T(8,128)(2,1)S(1)}, bf16[1,16,8192]{2,1,0:T(8,128)(2,1)}, u32[]{:S(2)}) %copy-start.2) | copy-done | bytes 262168
  1.0 0.1 shard_map.66
  1.1 0.0 copy-start.3
  1.1 32.1 %all_to_all.10 = bf16[128,8,128]{2,1,0:T(8,128)(2,1)S(1)} all-to-all(bf16[128,8,128]{2,1,0:T(8,128)(2,1)S(1)} %bitcast.6), channel_id=1, replica_groups=mesh['chan'=128,'period'=4] {'chan'}, dimensions={0} | all-to-all | bytes 524288 | tf_op jit(solution)/shard_map/all_to_all | solution.py:180
  33.2 0.0 copy-done.3
  33.2 0.5 shard_map.67.own_ref
  33.6 2.5 %collective-permute-start.1 = (bf16[8,64,256]{2,1,0:T(8,128)(2,1)S(1)}, bf16[8,64,256]{2,1,0:T(8,128)(2,1)S(1)}, u32[]{:S(2)}, u32[]{:S(2)}) collective-permute-start(bf16[8,64,256]{2,1,0:T(8,128)(2,1)S(1)} %shard_map.67.own_ref), channel_id=1, source_target_pairs={{0,8},{4,12},{8,16},{12,20},{16,24},{20,28},{24,32},{28,36},{32,40... | collective-permute-start | bytes 786440 | tf_op jit(solution)/shard_map/ppermute | solution.py:190
  36.1 1.9 %collective-permute-start = (bf16[8,64,256]{2,1,0:T(8,128)(2,1)S(1)}, bf16[8,64,256]{2,1,0:T(8,128)(2,1)S(1)}, u32[]{:S(2)}, u32[]{:S(2)}) collective-permute-start(bf16[8,64,256]{2,1,0:T(8,128)(2,1)S(1)} %shard_map.67.own_ref), channel_id=1, source_target_pairs={{0,4},{4,8},{8,12},{12,16},{16,20},{20,24},{24,28},{28,32},{32,36}... | collective-permute-start | bytes 786440 | tf_op jit(solution)/shard_map/ppermute | solution.py:189
  38.1 0.0 copy-done.4
  38.1 0.2 shard_map.65.masks_ref
  38.3 8.6 %collective-permute-done.1.far_ref = bf16[8,64,256]{2,1,0:T(8,128)(2,1)S(1)} collective-permute-done((bf16[8,64,256]{2,1,0:T(8,128)(2,1)S(1)}, bf16[8,64,256]{2,1,0:T(8,128)(2,1)S(1)}, u32[]{:S(2)}, u32[]{:S(2)}) %collective-permute-start.1) | collective-permute-done | bytes 262176 | tf_op jit(solution)/shard_map/ppermute | solution.py:190
  46.9 1.0 %collective-permute-done.near_ref = bf16[8,64,256]{2,1,0:T(8,128)(2,1)S(1)} collective-permute-done((bf16[8,64,256]{2,1,0:T(8,128)(2,1)S(1)}, bf16[8,64,256]{2,1,0:T(8,128)(2,1)S(1)}, u32[]{:S(2)}, u32[]{:S(2)}) %collective-permute-start) | collective-permute-done | bytes 262176 | tf_op jit(solution)/shard_map/ppermute | solution.py:189
  47.9 1.3 %shard_map.68.across_ref = f32[16,256]{1,0:T(8,128)S(1)} custom-call(bf16[2048,192]{1,0:T(8,128)(2,1)S(1)} %shard_map.65.masks_ref, bf16[8,64,256]{2,1,0:T(8,128)(2,1)S(1)} %shard_map.67.own_ref, bf16[8,64,256]{2,1,0:T(8,128)(2,1)S(1)} %collective-permute-done.near_ref, bf16[8,64,256]{2,1,0:T(8,128)(2,1)S(1)} %collective-permute-done.1.far_ref), custom_call_target="tpu_custom_call" | custom-call | tf_op jit(solution)/shard_map/pallas_call | solution.py:195
  49.2 1.9 %collective-permute-start.2 = (f32[16,256]{1,0:T(8,128)S(1)}, f32[16,256]{1,0:T(8,128)S(1)}, u32[]{:S(2)}, u32[]{:S(2)}) collective-permute-start(f32[16,256]{1,0:T(8,128)S(1)} %shard_map.68.across_ref), channel_id=1, source_target_pairs={{4,8},{12,16},{20,24},{28,32},{36,40},{44,48},{52,56},{60,64},{68,... | collective-permute-start | bytes 49160 | tf_op jit(solution)/shard_map/ppermute | solution.py:197
  51.1 0.0 copy-start.1
  51.1 1.3 %shard_map.69.inside_ref = f32[16,256]{1,0:T(8,128)S(1)} custom-call(bf16[2048,192]{1,0:T(8,128)(2,1)S(1)} %shard_map.65.masks_ref, bf16[8,64,256]{2,1,0:T(8,128)(2,1)S(1)} %shard_map.67.own_ref, bf16[8,64,256]{2,1,0:T(8,128)(2,1)S(1)} %collective-permute-done.near_ref, bf16[8,64,256]{2,1,0:T(8,128)(2,1)S(1)} %collective-permute-done.1.far_ref), custom_call_target="tpu_custom_call" | custom-call | flops 2000000000 | bytes 7812500 | tf_op jit(solution)/shard_map/pallas_call | solution.py:198
  52.4 0.0 copy-start
  52.4 3.9 %collective-permute-done.2.arrived_ref = f32[16,256]{1,0:T(8,128)S(1)} collective-permute-done((f32[16,256]{1,0:T(8,128)S(1)}, f32[16,256]{1,0:T(8,128)S(1)}, u32[]{:S(2)}, u32[]{:S(2)}) %collective-permute-start.2) | collective-permute-done | bytes 16416 | tf_op jit(solution)/shard_map/ppermute | solution.py:197
  56.3 0.7 shard_map.70
  57.0 4.3 %all-to-all-start.1 = ((bf16[8,32,256]{2,1,0:T(8,128)(2,1)}), bf16[8,32,256]{2,1,0:T(8,128)(2,1)S(1)}, u32[]{:S(2)}, u32[]{:S(2)}) async-start(bf16[8,32,256]{2,1,0:T(8,128)(2,1)} %shard_map.70), calls=%async_computation.1 | async-start | bytes 262144 | tf_op jit(solution)/shard_map/all_to_all | solution.py:206
  61.3 0.7 copy-done.5
  62.0 0.7 %shard_map.64.place_ref = s32[2]{0:T(128)S(1)} custom-call(s32[2,128]{1,0:T(2,128)S(1)} %bitcast.8), custom_call_target="tpu_custom_call" | custom-call | tf_op jit(solution)/shard_map/pallas_call | solution.py:191
  62.7 4.2 %all-to-all-done.1.sums_ref = bf16[8,32,256]{2,1,0:T(8,128)(2,1)S(1)} async-done(((bf16[8,32,256]{2,1,0:T(8,128)(2,1)}), bf16[8,32,256]{2,1,0:T(8,128)(2,1)S(1)}, u32[]{:S(2)}, u32[]{:S(2)}) %all-to-all-start.1) | async-done | bytes 131104 | tf_op jit(solution)/shard_map/all_to_all | solution.py:206
  66.9 1.6 %shard_map.71 = f32[128,256]{1,0:T(8,128)} custom-call(s32[2]{0:T(128)S(1)} %shard_map.64.place_ref, bf16[8,32,256]{2,1,0:T(8,128)(2,1)S(1)} %all-to-all-done.1.sums_ref, f32[2,8,32,128]{3,2,1,0:T(8,128)S(1)} %copy-done.1, bf16[768,256]{1,0:T(8,128)(2,1)S(1)} %copy-done), custom_call_target="tpu_custom_call" | custom-call | tf_op jit(solution)/shard_map/pallas_call | solution.py:209
  (5 shorter events, 0.0 us)
Async XLA Ops:
  0.0 0.9 %copy-start.2 = (bf16[1,16,8192]{2,1,0:T(8,128)(2,1)S(1)}, bf16[1,16,8192]{2,1,0:T(8,128)(2,1)}, u32[]{:S(2)}) copy-start(bf16[1,16,8192]{2,1,0:T(8,128)(2,1)} %param.6) | copy-start | bytes 786436
  1.1 32.1 %copy-start.3 = (bf16[256,256]{1,0:T(8,128)(2,1)S(1)}, bf16[256,256]{1,0:T(8,128)(2,1)}, u32[]{:S(2)}) copy-start(bf16[256,256]{1,0:T(8,128)(2,1)} %constant.6.clone.table_ref) | copy-start | bytes 393220
  33.2 4.9 %copy-start.4 = (s32[3,64,64]{2,1,0:T(8,128)S(1)}, s32[3,64,64]{2,1,0:T(8,128)}, u32[]{:S(2)}) copy-start(s32[3,64,64]{2,1,0:T(8,128)} %ids_ref.1) | copy-start | bytes 147460
  33.6 13.2 %collective-permute-start.1 = (bf16[8,64,256]{2,1,0:T(8,128)(2,1)S(1)}, bf16[8,64,256]{2,1,0:T(8,128)(2,1)S(1)}, u32[]{:S(2)}, u32[]{:S(2)}) collective-permute-start(bf16[8,64,256]{2,1,0:T(8,128)(2,1)S(1)} %shard_map.67.own_ref), channel_id=1, source_target_pairs={{0,8},{4,12},{8,16},{12,20},{16,24},{20,28},{24,32},{28,36},{32,40... | collective-permute-start | bytes 786440 | tf_op jit(solution)/shard_map/ppermute | solution.py:190
  36.1 11.7 %collective-permute-start = (bf16[8,64,256]{2,1,0:T(8,128)(2,1)S(1)}, bf16[8,64,256]{2,1,0:T(8,128)(2,1)S(1)}, u32[]{:S(2)}, u32[]{:S(2)}) collective-permute-start(bf16[8,64,256]{2,1,0:T(8,128)(2,1)S(1)} %shard_map.67.own_ref), channel_id=1, source_target_pairs={{0,4},{4,8},{8,12},{12,16},{16,20},{20,24},{24,28},{28,32},{32,36}... | collective-permute-start | bytes 786440 | tf_op jit(solution)/shard_map/ppermute | solution.py:189
  49.2 7.2 %collective-permute-start.2 = (f32[16,256]{1,0:T(8,128)S(1)}, f32[16,256]{1,0:T(8,128)S(1)}, u32[]{:S(2)}, u32[]{:S(2)}) collective-permute-start(f32[16,256]{1,0:T(8,128)S(1)} %shard_map.68.across_ref), channel_id=1, source_target_pairs={{4,8},{12,16},{20,24},{28,32},{36,40},{44,48},{52,56},{60,64},{68,... | collective-permute-start | bytes 49160 | tf_op jit(solution)/shard_map/ppermute | solution.py:197
  51.1 15.8 %copy-start.1 = (f32[2,8,32,128]{3,2,1,0:T(8,128)S(1)}, f32[2,8,32,128]{3,2,1,0:T(8,128)}, u32[]{:S(2)}) copy-start(f32[2,8,32,128]{3,2,1,0:T(8,128)} %constant.7.clone.slant_ref) | copy-start | bytes 786436
  52.4 14.4 %copy-start = (bf16[768,256]{1,0:T(8,128)(2,1)S(1)}, bf16[768,256]{1,0:T(8,128)(2,1)}, u32[]{:S(2)}) copy-start(bf16[768,256]{1,0:T(8,128)(2,1)} %constant.8.clone.lags_ref) | copy-start | bytes 1179652
  57.0 9.9 %all-to-all-start.1 = ((bf16[8,32,256]{2,1,0:T(8,128)(2,1)}), bf16[8,32,256]{2,1,0:T(8,128)(2,1)S(1)}, u32[]{:S(2)}, u32[]{:S(2)}) async-start(bf16[8,32,256]{2,1,0:T(8,128)(2,1)} %shard_map.70), calls=%async_computation.1 | async-start | bytes 262144 | tf_op jit(solution)/shard_map/all_to_all | solution.py:206
  61.3 0.7 copy-start.5

commit v3 on v2

v3 whole, which is shorter than its diff:
```python
import functools
import math

import jax
import jax.numpy as jnp
import numpy as np
from jax import lax
from jax.experimental import pallas as pl
from jax.experimental.pallas import tpu as pltpu
from jax.sharding import PartitionSpec as P

CH_DEV = 64
WIN = 256
NF = 128
NWIN = 8
HELD = NWIN // 2
MB_DEV = 2
NOFF = 8
NP = 32
CAP = 4
BINS = 2 * MB_DEV * NOFF
HALF = BINS // 2
VMEM_LIMIT = 48 * 1024 * 1024

def chip_at(place):
    row, chip, core = place // 16, place % 16 // 2, place % 2
    return 8 * (row + 4 * core) + chip


def dft_rows():
    phase = 2.0 * math.pi / WIN * np.mod(np.arange(WIN)[:, None] * np.arange(1, NF + 1)[None, :], WIN)
    return np.concatenate([np.cos(phase), -np.sin(phase)], axis=1).astype(np.float32)


def lag_table():
    phase = 2.0 * math.pi / WIN * np.mod(np.arange(1, NF + 1)[:, None] * np.arange(WIN)[None, :], WIN)
    return np.concatenate([np.cos(phase), -np.sin(phase)], axis=0).astype(np.float32)


def lag_parts():
    table = lag_table()
    high = table.astype(jnp.bfloat16)
    low = (table - high.astype(np.float32)).astype(jnp.bfloat16)
    return np.concatenate([high, high, low], axis=0)


def slant_tables():
    slow = (np.arange(NP) - NP // 2) / (4.0 * NP)
    offset = (np.arange(NOFF) + 0.5) * (3.0 * CH_DEV / NOFF)
    freq = np.arange(1, NF + 1) * (2.0 * math.pi / WIN)
    phase = offset[:, None, None] * slow[None, :, None] * freq[None, None, :]
    return np.stack([np.cos(phase), np.sin(phase)]).astype(np.float32)


def call(kernel, out_shape, flops=0, **kw):
    return pl.pallas_call(
        kernel,
        out_shape=out_shape,
        cost_estimate=pl.CostEstimate(flops=flops, bytes_accessed=flops // 256, transcendentals=0),
        compiler_params=pltpu.CompilerParams(vmem_limit_bytes=VMEM_LIMIT),
        **kw,
    )


def pack_kernel(raw_ref, out_ref):
    for place in range(raw_ref.shape[1] // 128):
        chip = chip_at(place)
        for tile in range(2):
            at = 128 * (chip - 1 + tile)
            if at < 0:
                out_ref[place, tile] = jnp.zeros((16, 128), jnp.bfloat16)
            else:
                out_ref[place, tile] = raw_ref[:, at : at + 128]


def mask_kernel(first_ref, second_ref, masks_ref):
    swapped = lax.axis_index("chan") >= lax.axis_size("chan") // 2
    firsts = jnp.concatenate([first_ref[2], first_ref[1], first_ref[0]], axis=1)
    seconds = jnp.concatenate([second_ref[2], second_ref[1], second_ref[0]], axis=1)
    for block in range(2):
        ids = jnp.where(swapped, firsts, seconds) if block else jnp.where(swapped, seconds, firsts)
        for bin_at in range(BINS):
            masks_ref[block, bin_at * CH_DEV : (bin_at + 1) * CH_DEV, :] = (
                (ids == bin_at).astype(jnp.float32).astype(jnp.bfloat16)
            )


def place_kernel(owner_ref, place_ref):
    device = lax.axis_index("chan")
    owner = owner_ref[...]
    place_ref[0] = jnp.sum((owner < device).astype(jnp.int32)) - MB_DEV * (device - 1)
    place_ref[1] = jnp.sum((owner == device).astype(jnp.int32))


def spectra_kernel(series_ref, table_ref, out_ref):
    table = table_ref[...]
    for window in range(HELD):
        for tile in range(2):
            series = series_ref[window, :, tile].reshape(WIN, 128).T
            spectra = jnp.dot(series, table, preferred_element_type=jnp.float32)
            power = jnp.mean(spectra * spectra, axis=-1, keepdims=True)
            out_ref[window, 128 * tile : 128 * tile + 128] = (
                spectra / jnp.sqrt(power + 1e-06)
            ).astype(jnp.bfloat16)


def bin_kernel(masks_ref, spectra_ref, whole_ref, lower_ref, upper_ref):
    def add_bins(sources):
        totals = None
        for block, half in sources:
            rows = slice(half * HALF * CH_DEV, (half + 1) * HALF * CH_DEV)
            for window in range(HELD):
                partners = spectra_ref[window, block * CH_DEV : (block + 3) * CH_DEV]
                own = spectra_ref[window, (block + 2) * CH_DEV : (block + 3) * CH_DEV]
                own = own.astype(jnp.float32)
                own_real, own_imag = own[:, :NF], own[:, NF:]
                picked = jnp.dot(
                    masks_ref[block, rows, :], partners, preferred_element_type=jnp.float32
                )
                terms = []
                for bin_at in range(HALF):
                    picked_real = picked[bin_at * CH_DEV : (bin_at + 1) * CH_DEV, :NF]
                    picked_imag = picked[bin_at * CH_DEV : (bin_at + 1) * CH_DEV, NF:]
                    real = own_real * picked_real + own_imag * picked_imag
                    imag = own_imag * picked_real - own_real * picked_imag
                    terms.append(jnp.sum(real.reshape(8, 8, NF), axis=0))
                    terms.append(jnp.sum(imag.reshape(8, 8, NF), axis=0))
                totals = terms if totals is None else [x + y for x, y in zip(totals, terms)]
        return [jnp.sum(total, axis=0, keepdims=True) for total in totals]

    for at, sources in enumerate((((0, 0),), ((0, 1), (1, 0)), ((1, 1),))):
        totals = add_bins(sources)
        for bin_at in range(HALF):
            row = jnp.concatenate(totals[2 * bin_at : 2 * bin_at + 2], axis=1)
            whole_ref[at * HALF + bin_at : at * HALF + bin_at + 1] = row
            if at == 0:
                lower_ref[bin_at : bin_at + 1] = row
            if at == 2:
                upper_ref[bin_at : bin_at + 1] = row


def merge_kernel(whole_ref, below_ref, above_ref, out_ref):
    lower = (whole_ref[:HALF] + below_ref[...]).astype(jnp.bfloat16)
    middle = whole_ref[HALF : 2 * HALF].astype(jnp.bfloat16)
    upper = (whole_ref[2 * HALF :] + above_ref[...]).astype(jnp.bfloat16)
    for period in range(4):
        out_ref[period, :HALF] = lower
        out_ref[period, HALF:] = middle
        out_ref[4 + period, :HALF] = middle
        out_ref[4 + period, HALF:] = upper


def stack_kernel(place_ref, sums_ref, slant_ref, lags_ref, out_ref, held, spec):
    total = sums_ref[0].astype(jnp.float32)
    for part in range(1, 8):
        total = total + sums_ref[part].astype(jnp.float32)
    held[...] = jnp.zeros_like(held)
    held[:BINS] = total
    count = place_ref[1]
    first = jnp.where(count > 0, place_ref[0], 0)
    for slot in range(CAP):
        rows = held[pl.ds(pl.multiple_of((first + slot) * NOFF, 8), NOFF), :]
        rows = jnp.where(slot < count, rows, 0.0)
        real = jnp.zeros((NP, NF), jnp.float32)
        imag = jnp.zeros((NP, NF), jnp.float32)
        for offset in range(NOFF):
            bin_real = rows[offset : offset + 1, :NF]
            bin_imag = rows[offset : offset + 1, NF:]
            cos, sin = slant_ref[0, offset], slant_ref[1, offset]
            real = real + (bin_real * cos + bin_imag * sin)
            imag = imag + (bin_imag * cos - bin_real * sin)
        spec[slot * NP : (slot + 1) * NP, :NF] = real
        spec[slot * NP : (slot + 1) * NP, NF:] = imag
    whole = spec[...]
    high = whole.astype(jnp.bfloat16)
    low = (whole - high.astype(jnp.float32)).astype(jnp.bfloat16)
    traces = jnp.dot(
        jnp.concatenate([high, low, high], axis=1), lags_ref[...], preferred_element_type=jnp.float32
    )
    power = jnp.mean(traces * traces, axis=-1, keepdims=True)
    out_ref[...] = traces / jnp.sqrt(power + 1e-06)


def shards(raw_strain, bin_ids, owner_map):
    count = lax.axis_size("chan")
    periods = lax.axis_size("period")
    chips = count // 2
    smem = pl.BlockSpec(memory_space=pltpu.SMEM)
    vmem = pl.BlockSpec(memory_space=pltpu.VMEM)
    holders = [(chips * part + place, chip_at(place), part) for part in range(2) for place in range(chips)]

    packed = call(pack_kernel, jax.ShapeDtypeStruct((chips, 2, 16, 128), jnp.bfloat16))(raw_strain[0])
    packed, bin_ids, owner_map = lax.optimization_barrier((packed, bin_ids, owner_map))
    groups = [list(range(chips * part, chips * (part + 1))) for part in range(2)]
    series = lax.all_to_all(packed, "chan", 0, 0, tiled=True, axis_index_groups=groups)
    first = lax.ppermute(bin_ids, "chan", [(2 * chip + part, at) for at, chip, part in holders])
    second = lax.ppermute(bin_ids, "chan", [(2 * chip + 1 - part, at) for at, chip, part in holders])
    masks = call(
        mask_kernel,
        jax.ShapeDtypeStruct((2, BINS * CH_DEV, 3 * CH_DEV), jnp.bfloat16),
        flops=2000000000,
    )(first, second)
    place = call(place_kernel, jax.ShapeDtypeStruct((2,), jnp.int32), out_specs=smem)(
        owner_map.reshape(2, 128)
    )
    series, masks, place = lax.optimization_barrier((series, masks, place))
    spectra = call(spectra_kernel, jax.ShapeDtypeStruct((HELD, 4 * CH_DEV, 2 * NF), jnp.bfloat16))(
        series.reshape(HELD, 16, 2, 16, 128), jnp.asarray(dft_rows(), jnp.bfloat16)
    )
    whole, lower, upper = call(
        bin_kernel,
        (
            jax.ShapeDtypeStruct((3 * HALF, 2 * NF), jnp.float32),
            jax.ShapeDtypeStruct((HALF, 2 * NF), jnp.float32),
            jax.ShapeDtypeStruct((HALF, 2 * NF), jnp.float32),
        ),
    )(masks, spectra)
    whole = lax.ppermute(whole, "chan", [(at, 2 * chip + part) for at, chip, part in holders])
    above = lax.ppermute(
        lower, "chan", [(at, 2 * chip - 2 + part) for at, chip, part in holders if chip > 0]
    )
    below = lax.ppermute(
        upper, "chan", [(at, 2 * chip + 2 + part) for at, chip, part in holders if chip < chips - 1]
    )
    merged = call(merge_kernel, jax.ShapeDtypeStruct((8, BINS, 2 * NF), jnp.bfloat16))(
        whole, below, above
    )
    groups = [
        [(2 * chip + core) * periods + p for core in range(2) for p in range(periods)]
        for chip in range(chips)
    ]
    sums = lax.all_to_all(
        merged, ("chan", "period"), 0, 0, tiled=True, axis_index_groups=groups
    )
    stacks = call(
        stack_kernel,
        jax.ShapeDtypeStruct((CAP * NP, WIN), jnp.float32),
        in_specs=[smem, vmem, vmem, vmem],
        scratch_shapes=[
            pltpu.VMEM((2 * BINS, 2 * NF), jnp.float32),
            pltpu.VMEM((CAP * NP, 2 * NF), jnp.float32),
        ],
    )(place, sums, jnp.asarray(slant_tables()), jnp.asarray(lag_parts()))
    return stacks.reshape(CAP, NP, WIN)


def solution(mesh):
    placed = (P("period", "chan", None), P(None, "chan", None), P())
    return jax.shard_map(
        shards, mesh=mesh, in_specs=placed, out_specs=P("chan", None, None), check_vma=False
    )
```

time: 69.1 us -> 72.7 us (1.052)
  starting transfers between devices: 10.6 us -> 29.6 us
  blocking collectives: 32.1 us -> 19.8 us
  waiting for transfers between devices: 17.6 us -> 14.1 us
    all_to_all x1, blocking collectives: 32.1 us -> 19.8 us  [shards(): lax.all_to_all(merged, ('chan', 'period'), 0, 0, tiled=True, axis_index_g...]
    ppermute x3 -> x5, waiting for transfers between devices: 13.5 us -> 1.73 us  [the longest x1 1.41 us: shards(): lax.ppermute(lower, 'chan', [(at, 2 * chip - 2 + part) for at, chip, part...]
    all_to_all x1, starting transfers between devices: 4.3 us -> 14.4 us  [shards(): lax.all_to_all(packed, 'chan', 0, 0, tiled=True, axis_index_groups=groups)]
    ppermute x3 -> x5, starting transfers between devices: 6.33 us -> 15.2 us  [the longest x1 5.04 us: shards(): lax.ppermute(bin_ids, 'chan', [(2 * chip + 1 - part, at) for at, chip, pa...]
    all_to_all x1, waiting for transfers between devices: 4.15 us -> 12.4 us  [shards(): lax.all_to_all(packed, 'chan', 0, 0, tiled=True, axis_index_groups=groups)]
    pallas_call x5 -> x4, Pallas kernels: 3.43 us -> 4.44 us  [the longest x1 2.67 us: shards(): call(bin_kernel, (jax.ShapeDtypeStruct((3 * HALF, 2 * NF), jnp.float32),...]
    unnamed x12 -> x10, local copies, waits for them, and re-layouts: 1.65 us -> 1.64 us
  transfers between devices with their start and end apart: 4 -> 6, of which waited for: 4 -> 3; matrix products, arithmetic and copies ran while one was open for 0% -> 0% of each run, Pallas kernels for 3% -> 2%
where the time goes in v3:
time: 72.7 us; the launch traced here: 72 us
  starting transfers between devices  29.6 us (41%)
  blocking collectives  19.8 us (27%)
  waiting for transfers between devices  14.1 us (19%)
  Pallas kernels  6.81 us (9%)
  local copies, waits for them, and re-layouts  1.64 us (2%)
    all_to_all x1, blocking collectives, shards(): lax.all_to_all(merged, ('chan', 'period'), 0, 0, tiled=True, axis_index_g...  19.8 us
    all_to_all x1, starting transfers between devices, shards(): lax.all_to_all(packed, 'chan', 0, 0, tiled=True, axis_index_groups=groups)  14.4 us
    all_to_all x1, waiting for transfers between devices, shards(): lax.all_to_all(packed, 'chan', 0, 0, tiled=True, axis_index_groups=groups)  12.4 us
    ppermute x1, starting transfers between devices, shards(): lax.ppermute(bin_ids, 'chan', [(2 * chip + 1 - part, at) for at, chip, pa...  5.04 us
    ppermute x1, starting transfers between devices, shards(): lax.ppermute(lower, 'chan', [(at, 2 * chip - 2 + part) for at, chip, part...  4.36 us
    ppermute x1, starting transfers between devices, shards(): lax.ppermute(upper, 'chan', [(at, 2 * chip + 2 + part) for at, chip, part...  3.6 us
    pallas_call x1, Pallas kernels, shards(): call(bin_kernel, (jax.ShapeDtypeStruct((3 * HALF, 2 * NF), jnp.float32),...  2.67 us
    unnamed x10, local copies, waits for them, and re-layouts  1.64 us
  transfers between devices with their start and end apart: 6, of which 3 were waited for; matrix products, arithmetic and copies ran while one was open for 0% of the time, Pallas kernels for 2%

profile of v3, /device:TPU:8, one launch (start us, length us, event | category | flops | bytes accessed | tf_op | source)
XLA Modules:
  0.0 72.0 jit_solution(1466864513579634056)
XLA Ops:
  0.0 0.9 %copy-done.1 = bf16[1,16,8192]{2,1,0:T(8,128)(2,1)S(1)} copy-done((bf16[1,16,8192]{2,1,0:T(8,128)(2,1)S(1)}, bf16[1,16,8192]{2,1,0:T(8,128)(2,1)}, u32[]{:S(2)}) %copy-start.1) | copy-done | bytes 262168
  1.0 0.9 %shard_map.64 = bf16[64,2,16,128]{3,2,1,0:T(8,128)(2,1)} custom-call(bf16[16,8192]{1,0:T(8,128)(2,1)S(1)} %bitcast.5), custom_call_target="tpu_custom_call" | custom-call | tf_op jit(solution)/shard_map/pallas_call | solution.py:192
  1.8 14.4 %all-to-all-start = ((bf16[64,2,16,128]{3,2,1,0:T(8,128)(2,1)}), bf16[64,2,16,128]{3,2,1,0:T(8,128)(2,1)S(1)}, u32[]{:S(2)}, u32[]{:S(2)}) async-start(bf16[64,2,16,128]{3,2,1,0:T(8,128)(2,1)} %shard_map.64), calls=%async_computation | async-start | bytes 1048576 | tf_op jit(solution)/shard_map/all_to_all | solution.py:195
  16.2 5.0 %collective-permute-start.1 = (s32[3,64,64]{2,1,0:T(8,128)}, s32[3,64,64]{2,1,0:T(8,128)S(1)}, u32[]{:S(2)}, u32[]{:S(2)}) collective-permute-start(s32[3,64,64]{2,1,0:T(8,128)} %param.7), channel_id=1, source_target_pairs={{4,0},{260,4},{12,8},{268,12},{20,16},{276,20},{28,24},{284,28},{3... | collective-permute-start | bytes 147464 | tf_op jit(solution)/shard_map/ppermute | solution.py:197
  21.2 1.6 %collective-permute-start = (s32[3,64,64]{2,1,0:T(8,128)}, s32[3,64,64]{2,1,0:T(8,128)S(1)}, u32[]{:S(2)}, u32[]{:S(2)}) collective-permute-start(s32[3,64,64]{2,1,0:T(8,128)} %param.7), channel_id=1, source_target_pairs={{0,0},{256,4},{8,8},{264,12},{16,16},{272,20},{24,24},{280,28},{32... | collective-permute-start | bytes 147464 | tf_op jit(solution)/shard_map/ppermute | solution.py:196
  22.8 0.7 copy-done.4
  23.5 0.7 shard_map.66.place_ref
  24.2 0.0 copy-start.3
  24.2 0.3 collective-permute-done.1.second_ref
  24.5 0.0 collective-permute-done.first_ref
  24.5 0.4 shard_map.65.masks_ref
  24.9 12.4 %all-to-all-done = bf16[64,2,16,128]{3,2,1,0:T(8,128)(2,1)S(1)} async-done(((bf16[64,2,16,128]{3,2,1,0:T(8,128)(2,1)}), bf16[64,2,16,128]{3,2,1,0:T(8,128)(2,1)S(1)}, u32[]{:S(2)}, u32[]{:S(2)}) %all-to-all-start) | async-done | bytes 524320 | tf_op jit(solution)/shard_map/all_to_all | solution.py:195
  37.3 0.0 copy-done.3
  37.3 0.5 shard_map.67.spectra_ref
  37.8 2.7 %shard_map.68 = (f32[48,256]{1,0:T(8,128)S(1)}, f32[16,256]{1,0:T(8,128)S(1)}, f32[16,256]{1,0:T(8,128)S(1)}) custom-call(bf16[2,2048,192]{2,1,0:T(8,128)(2,1)S(1)} %shard_map.65.masks_ref, bf16[4,256,256]{2,1,0:T(8,128)(2,1)S(1)} %shard_map.67.spectra_ref), custom_call_target="tpu_custom_call" | custom-call | tf_op jit(solution)/shard_map/pallas_call | solution.py:210
  40.5 0.7 collective-permute-start.2
  41.2 3.6 %collective-permute-start.3 = (f32[16,256]{1,0:T(8,128)S(1)}, f32[16,256]{1,0:T(8,128)S(1)}, u32[]{:S(2)}, u32[]{:S(2)}) collective-permute-start(f32[16,256]{1,0:T(8,128)S(1)} %get-tuple-element.21), channel_id=1, source_target_pairs={{0,8},{4,264},{8,16},{12,272},{16,24},{20,280},{24,32},{28,288},{3... | collective-permute-start | bytes 49160 | tf_op jit(solution)/shard_map/ppermute | solution.py:222
  44.8 4.4 %collective-permute-start.4 = (f32[16,256]{1,0:T(8,128)S(1)}, f32[16,256]{1,0:T(8,128)S(1)}, u32[]{:S(2)}, u32[]{:S(2)}) collective-permute-start(f32[16,256]{1,0:T(8,128)S(1)} %get-tuple-element.22), channel_id=1, source_target_pairs={{4,248},{8,0},{12,256},{16,8},{20,264},{24,16},{28,272},{32,24},{3... | collective-permute-start | bytes 49160 | tf_op jit(solution)/shard_map/ppermute | solution.py:219
  49.1 0.0 collective-permute-done.3.below_ref
  49.1 1.4 %collective-permute-done.4.above_ref = f32[16,256]{1,0:T(8,128)S(1)} collective-permute-done((f32[16,256]{1,0:T(8,128)S(1)}, f32[16,256]{1,0:T(8,128)S(1)}, u32[]{:S(2)}, u32[]{:S(2)}) %collective-permute-start.4) | collective-permute-done | bytes 16416 | tf_op jit(solution)/shard_map/ppermute | solution.py:219
  50.5 0.0 collective-permute-done.2.whole_ref
  50.6 19.8 %all_to_all.10.sums_ref = bf16[8,32,256]{2,1,0:T(8,128)(2,1)S(1)} all-to-all(bf16[8,32,256]{2,1,0:T(8,128)(2,1)S(1)} %shard_map.69), channel_id=1, replica_groups={{0,1,2,3,4,5,6,7},{8,9,10,11,12,13,14,15},{16,17,18,19,20,21,22,23},{24..., dimensions={0} | all-to-all | bytes 262144 | tf_op jit(solution)/shard_map/all_to_all | solution.py:232
  70.4 0.0 copy-done
  70.4 1.6 %shard_map.70 = f32[128,256]{1,0:T(8,128)} custom-call(s32[2]{0:T(128)S(1)} %shard_map.66.place_ref, bf16[8,32,256]{2,1,0:T(8,128)(2,1)S(1)} %all_to_all.10.sums_ref, f32[2,8,32,128]{3,2,1,0:T(8,128)S(1)} %copy-done.2, bf16[768,256]{1,0:T(8,128)(2,1)S(1)} %copy-done), custom_call_target="tpu_custom_call" | custom-call | tf_op jit(solution)/shard_map/pallas_call | solution.py:235
  (6 shorter events, 0.0 us)
Async XLA Ops:
  0.0 0.9 %copy-start.1 = (bf16[1,16,8192]{2,1,0:T(8,128)(2,1)S(1)}, bf16[1,16,8192]{2,1,0:T(8,128)(2,1)}, u32[]{:S(2)}) copy-start(bf16[1,16,8192]{2,1,0:T(8,128)(2,1)} %param.6) | copy-start | bytes 786436
  1.8 35.4 %all-to-all-start = ((bf16[64,2,16,128]{3,2,1,0:T(8,128)(2,1)}), bf16[64,2,16,128]{3,2,1,0:T(8,128)(2,1)S(1)}, u32[]{:S(2)}, u32[]{:S(2)}) async-start(bf16[64,2,16,128]{3,2,1,0:T(8,128)(2,1)} %shard_map.64), calls=%async_computation | async-start | bytes 1048576 | tf_op jit(solution)/shard_map/all_to_all | solution.py:195
  16.2 8.3 %collective-permute-start.1 = (s32[3,64,64]{2,1,0:T(8,128)}, s32[3,64,64]{2,1,0:T(8,128)S(1)}, u32[]{:S(2)}, u32[]{:S(2)}) collective-permute-start(s32[3,64,64]{2,1,0:T(8,128)} %param.7), channel_id=1, source_target_pairs={{4,0},{260,4},{12,8},{268,12},{20,16},{276,20},{28,24},{284,28},{3... | collective-permute-start | bytes 147464 | tf_op jit(solution)/shard_map/ppermute | solution.py:197
  21.2 3.3 %collective-permute-start = (s32[3,64,64]{2,1,0:T(8,128)}, s32[3,64,64]{2,1,0:T(8,128)S(1)}, u32[]{:S(2)}, u32[]{:S(2)}) collective-permute-start(s32[3,64,64]{2,1,0:T(8,128)} %param.7), channel_id=1, source_target_pairs={{0,0},{256,4},{8,8},{264,12},{16,16},{272,20},{24,24},{280,28},{32... | collective-permute-start | bytes 147464 | tf_op jit(solution)/shard_map/ppermute | solution.py:196
  22.8 0.7 copy-start.4
  24.2 13.1 %copy-start.3 = (bf16[256,256]{1,0:T(8,128)(2,1)S(1)}, bf16[256,256]{1,0:T(8,128)(2,1)}, u32[]{:S(2)}) copy-start(bf16[256,256]{1,0:T(8,128)(2,1)} %constant.6.clone.table_ref) | copy-start | bytes 393220
  37.3 33.1 %copy-start = (bf16[768,256]{1,0:T(8,128)(2,1)S(1)}, bf16[768,256]{1,0:T(8,128)(2,1)}, u32[]{:S(2)}) copy-start(bf16[768,256]{1,0:T(8,128)(2,1)} %constant.8.clone.lags_ref) | copy-start | bytes 1179652
  37.3 33.1 %copy-start.2 = (f32[2,8,32,128]{3,2,1,0:T(8,128)S(1)}, f32[2,8,32,128]{3,2,1,0:T(8,128)}, u32[]{:S(2)}) copy-start(f32[2,8,32,128]{3,2,1,0:T(8,128)} %constant.7.clone.slant_ref) | copy-start | bytes 786436
  40.5 10.1 %collective-permute-start.2 = (f32[48,256]{1,0:T(8,128)S(1)}, f32[48,256]{1,0:T(8,128)S(1)}, u32[]{:S(2)}, u32[]{:S(2)}) collective-permute-start(f32[48,256]{1,0:T(8,128)S(1)} %get-tuple-element.20), channel_id=1, source_target_pairs={{0,0},{4,256},{8,8},{12,264},{16,16},{20,272},{24,24},{28,280},{32... | collective-permute-start | bytes 147464 | tf_op jit(solution)/shard_map/ppermute | solution.py:218
  41.2 8.0 %collective-permute-start.3 = (f32[16,256]{1,0:T(8,128)S(1)}, f32[16,256]{1,0:T(8,128)S(1)}, u32[]{:S(2)}, u32[]{:S(2)}) collective-permute-start(f32[16,256]{1,0:T(8,128)S(1)} %get-tuple-element.21), channel_id=1, source_target_pairs={{0,8},{4,264},{8,16},{12,272},{16,24},{20,280},{24,32},{28,288},{3... | collective-permute-start | bytes 49160 | tf_op jit(solution)/shard_map/ppermute | solution.py:222
  44.8 5.8 %collective-permute-start.4 = (f32[16,256]{1,0:T(8,128)S(1)}, f32[16,256]{1,0:T(8,128)S(1)}, u32[]{:S(2)}, u32[]{:S(2)}) collective-permute-start(f32[16,256]{1,0:T(8,128)S(1)} %get-tuple-element.22), channel_id=1, source_target_pairs={{4,248},{8,0},{12,256},{16,8},{20,264},{24,16},{28,272},{32,24},{3... | collective-permute-start | bytes 49160 | tf_op jit(solution)/shard_map/ppermute | solution.py:219

commit v4 on v2

--- a/solution.py
+++ b/solution.py
@@ -13,6 +13,7 @@
 WIN = 256
 NF = 128
 NWIN = 8
+PART = NWIN // 2
 MB_DEV = 2
 NOFF = 8
 NP = 32
@@ -71,39 +72,37 @@
         out_ref[tile] = jnp.concatenate([even, odd], axis=0).astype(jnp.bfloat16)
 
 
-def mask_kernel(ids_ref, masks_ref):
+def mask_kernel(ids_ref, owner_ref, masks_ref, place_ref):
     ids = jnp.concatenate([ids_ref[0], ids_ref[1], ids_ref[2]], axis=1)
     for bin_at in range(BINS):
         masks_ref[bin_at * CH_DEV : (bin_at + 1) * CH_DEV, :] = (
             (ids == bin_at).astype(jnp.float32).astype(jnp.bfloat16)
         )
-
-
-def place_kernel(owner_ref, place_ref):
     device = lax.axis_index("chan")
     owner = owner_ref[...]
     place_ref[0] = jnp.sum((owner < device).astype(jnp.int32)) - MB_DEV * (device - 1)
     place_ref[1] = jnp.sum((owner == device).astype(jnp.int32))
 
 
-def spectra_kernel(series_ref, table_ref, out_ref):
+def spectra_kernel(series_ref, table_ref, out_ref, *part_refs):
     table = table_ref[...]
     for window in range(NWIN):
-        turned = series_ref[window].astype(jnp.float32).T.astype(jnp.bfloat16)
+        turned = series_ref[window].T
         series = jnp.concatenate([turned[:CH_DEV], turned[CH_DEV:]], axis=1)
         spectra = jnp.dot(series, table, preferred_element_type=jnp.float32)
         power = jnp.mean(spectra * spectra, axis=-1, keepdims=True)
-        out_ref[window] = (spectra / jnp.sqrt(power + 1e-06)).astype(jnp.bfloat16)
-
-
-def bin_kernel(across, masks_ref, own_ref, near_ref, far_ref, out_ref):
-    odd = lax.rem(lax.axis_index("chan"), 2)
-    part = odd if across else 1 - odd
-    rows = pl.ds(pl.multiple_of(part * HALF * CH_DEV, HALF * CH_DEV), HALF * CH_DEV)
+        whitened = (spectra / jnp.sqrt(power + 1e-06)).astype(jnp.bfloat16)
+        out_ref[window] = whitened
+        part_refs[window // PART][window % PART] = whitened
+
+
+def bin_half(masks_ref, rows, own_ref, near_ref, start, relay_ref, far_ref):
+    odd = lax.rem(lax.axis_index("chan"), 2)
     totals = None
-    for window in range(NWIN):
-        own = own_ref[window]
-        partners = jnp.concatenate([own, near_ref[window], far_ref[window]], axis=0)
+    for window in range(PART):
+        own = own_ref[start + window]
+        near = jnp.where(odd == 1, near_ref[start + window], relay_ref[window])
+        partners = jnp.concatenate([own, near, far_ref[window]], axis=0)
         own = own.astype(jnp.float32)
         own_real, own_imag = own[:, :NF], own[:, NF:]
         picked = jnp.dot(masks_ref[rows, :], partners, preferred_element_type=jnp.float32)
@@ -116,9 +115,24 @@
             terms.append(jnp.sum(real.reshape(8, 8, NF), axis=0))
             terms.append(jnp.sum(imag.reshape(8, 8, NF), axis=0))
         totals = terms if totals is None else [x + y for x, y in zip(totals, terms)]
-    for bin_at in range(HALF):
-        out_ref[bin_at : bin_at + 1, :NF] = jnp.sum(totals[2 * bin_at], axis=0, keepdims=True)
-        out_ref[bin_at : bin_at + 1, NF:] = jnp.sum(totals[2 * bin_at + 1], axis=0, keepdims=True)
+    sums = [jnp.sum(total, axis=0, keepdims=True) for total in totals]
+    return [jnp.concatenate(sums[2 * k : 2 * k + 2], axis=1) for k in range(HALF)]
+
+
+def first_kernel(masks_ref, own_ref, near_ref, relay_ref, far_ref, out_ref):
+    for half in range(2):
+        rows = pl.ds(half * HALF * CH_DEV, HALF * CH_DEV)
+        for bin_at, row in enumerate(bin_half(masks_ref, rows, own_ref, near_ref, 0, relay_ref, far_ref)):
+            out_ref[half, bin_at : bin_at + 1] = row
+
+
+def second_kernel(across, masks_ref, sums_ref, own_ref, near_ref, relay_ref, far_ref, out_ref):
+    odd = lax.rem(lax.axis_index("chan"), 2)
+    half = odd if across else 1 - odd
+    rows = pl.ds(pl.multiple_of(half * HALF * CH_DEV, HALF * CH_DEV), HALF * CH_DEV)
+    sums = bin_half(masks_ref, rows, own_ref, near_ref, PART, relay_ref, far_ref)
+    for bin_at, row in enumerate(sums):
+        out_ref[bin_at : bin_at + 1] = sums_ref[half, bin_at : bin_at + 1] + row
 
 
 def merge_kernel(across_ref, inside_ref, arrived_ref, out_ref):
@@ -178,24 +192,33 @@
     vmem = pl.BlockSpec(memory_space=pltpu.VMEM)
     packed = call(pack_kernel, jax.ShapeDtypeStruct((count // 2, 16, 128), jnp.bfloat16))(raw_strain[0])
     series = lax.all_to_all(packed.reshape(count, 8, 128), "chan", 0, 0, tiled=True)
-    masks = call(
+    masks, place = call(
         mask_kernel,
-        jax.ShapeDtypeStruct((BINS * CH_DEV, 3 * CH_DEV), jnp.bfloat16),
+        (
+            jax.ShapeDtypeStruct((BINS * CH_DEV, 3 * CH_DEV), jnp.bfloat16),
+            jax.ShapeDtypeStruct((2,), jnp.int32),
+        ),
         flops=2000000000,
-    )(bin_ids)
-    own = call(spectra_kernel, jax.ShapeDtypeStruct((NWIN, CH_DEV, 2 * NF), jnp.bfloat16))(
+        out_specs=(vmem, smem),
+    )(bin_ids, owner_map.reshape(2, 128))
+    windows = jax.ShapeDtypeStruct((PART, CH_DEV, 2 * NF), jnp.bfloat16)
+    whole = jax.ShapeDtypeStruct((NWIN, CH_DEV, 2 * NF), jnp.bfloat16)
+    own, early, late = call(spectra_kernel, (whole, windows, windows))(
         series.reshape(NWIN, 128, 128), jnp.asarray(dft_rows(), jnp.bfloat16)
     )
-    near = lax.ppermute(own, "chan", [(i, i + 1) for i in range(count - 1)])
-    far = lax.ppermute(own, "chan", [(i, i + 2) for i in range(count - 2)])
-    place = call(place_kernel, jax.ShapeDtypeStruct((2,), jnp.int32), out_specs=smem)(
-        owner_map.reshape(2, 128)
-    )
+    up = [(i, i + 2) for i in range(count - 2)]
+    far = [lax.ppermute(part, "chan", up) for part in (early, late)]
+    near = lax.ppermute(own, "chan", [(i, i + 1) for i in range(0, count, 2)])
+    relay = [lax.ppermute(part, "chan", [(i + 1, i) for i in range(0, count, 2)]) for part in far]
     part = jax.ShapeDtypeStruct((HALF, 2 * NF), jnp.float32)
-    across = call(functools.partial(bin_kernel, True), part)(masks, own, near, far)
+    first = call(
+        first_kernel, jax.ShapeDtypeStruct((2, HALF, 2 * NF), jnp.float32), flops=2000000000
+    )(masks, own, near, relay[0], far[0])
+    second = (masks, first, own, near, relay[1], far[1])
+    across = call(functools.partial(second_kernel, True), part)(*second)
     pairs = [(2 * k + 1, 2 * k + 2) for k in range(count // 2 - 1)]
     arrived = lax.ppermute(across, "chan", pairs + [(j, i) for i, j in pairs])
-    inside = call(functools.partial(bin_kernel, False), part, flops=2000000000)(masks, own, near, far)
+    inside = call(functools.partial(second_kernel, False), part, flops=1000000000)(*second)
     merged = call(merge_kernel, jax.ShapeDtypeStruct((8, BINS, 2 * NF), jnp.bfloat16))(
         across, inside, arrived
     )

time: 69.1 us -> 69.5 us (level)
  waiting for transfers between devices: 17.6 us -> 7.29 us
  blocking collectives: 32.1 us -> 41.7 us
  starting transfers between devices: 10.6 us -> 12.9 us
    all_to_all x0 -> x1, blocking collectives: none -> 9.65 us  [shards(): lax.all_to_all(merged, ('chan', 'period'), 0, 0, tiled=True, axis_index_g...]
    ppermute x2 -> x5, waiting for transfers between devices: 9.57 us -> 4.51 us  [the longest x2 3.99 us: shards(): far = [lax.ppermute(part, 'chan', up) for part in (early, late)]]
    ppermute x2 -> x5, starting transfers between devices: 4.41 us -> 9.28 us  [the longest x2 5.41 us: shards(): far = [lax.ppermute(part, 'chan', up) for part in (early, late)]]
    all_to_all x1 -> x0, starting transfers between devices: 4.3 us -> none  [shards(): lax.all_to_all(merged, ('chan', 'period'), 0, 0, tiled=True, axis_index_g...]
    all_to_all x1 -> x0, waiting for transfers between devices: 4.15 us -> none  [shards(): lax.all_to_all(merged, ('chan', 'period'), 0, 0, tiled=True, axis_index_g...]
    ppermute x1, starting transfers between devices: 1.92 us -> 3.58 us  [shards(): arrived = lax.ppermute(across, 'chan', pairs + [(j, i) for i, j in pairs])]
    ppermute x1, waiting for transfers between devices: 3.89 us -> 2.78 us  [shards(): arrived = lax.ppermute(across, 'chan', pairs + [(j, i) for i, j in pairs])]
  transfers between devices with their start and end apart: 4 -> 6, of which waited for: 4 -> 4; matrix products, arithmetic and copies ran while one was open for 0% -> 0% of each run, Pallas kernels for 3% -> 4%
where the time goes in v4:
time: 69.5 us; the launch traced here: 68.9 us
  blocking collectives  41.7 us (60%)
  starting transfers between devices  12.9 us (19%)
  waiting for transfers between devices  7.29 us (10%)
  Pallas kernels  5.89 us (8%)
  local copies, waits for them, and re-layouts  0.98 us (1%)
    all_to_all x1, blocking collectives, shards(): lax.all_to_all(packed.reshape(count, 8, 128), 'chan', 0, 0, tiled=True)  32.1 us
    all_to_all x1, blocking collectives, shards(): lax.all_to_all(merged, ('chan', 'period'), 0, 0, tiled=True, axis_index_g...  9.65 us
    ppermute x2, starting transfers between devices, shards(): far = [lax.ppermute(part, 'chan', up) for part in (early, late)]  5.41 us
    ppermute x2, waiting for transfers between devices, shards(): far = [lax.ppermute(part, 'chan', up) for part in (early, late)]  3.99 us
    ppermute x1, starting transfers between devices, shards(): arrived = lax.ppermute(across, 'chan', pairs + [(j, i) for i, j in pairs])  3.58 us
    ppermute x1, waiting for transfers between devices, shards(): arrived = lax.ppermute(across, 'chan', pairs + [(j, i) for i, j in pairs])  2.78 us
    ppermute x2, starting transfers between devices, shards(): lax.ppermute(part, 'chan', [(i + 1, i) for i in range(0, count, 2)])  2.56 us
    pallas_call x1, Pallas kernels, shards(): call(stack_kernel, jax.ShapeDtypeStruct((CAP * NP, WIN), jnp.float32), in...  1.64 us
  transfers between devices with their start and end apart: 6, of which 4 were waited for; matrix products, arithmetic and copies ran while one was open for 0% of the time, Pallas kernels for 4%

profile of v4, /device:TPU:8, one launch (start us, length us, event | category | flops | bytes accessed | tf_op | source)
XLA Modules:
  0.0 68.9 jit_solution(1992723553928780443)
XLA Ops:
  0.0 0.9 %copy-done.2 = bf16[1,16,8192]{2,1,0:T(8,128)(2,1)S(1)} copy-done((bf16[1,16,8192]{2,1,0:T(8,128)(2,1)S(1)}, bf16[1,16,8192]{2,1,0:T(8,128)(2,1)}, u32[]{:S(2)}) %copy-start.2) | copy-done | bytes 262168
  1.0 0.1 shard_map.65
  1.1 0.0 copy-start.3
  1.1 32.1 %all_to_all.10 = bf16[128,8,128]{2,1,0:T(8,128)(2,1)S(1)} all-to-all(bf16[128,8,128]{2,1,0:T(8,128)(2,1)S(1)} %bitcast.6), channel_id=1, replica_groups=mesh['chan'=128,'period'=4] {'chan'}, dimensions={0} | all-to-all | bytes 524288 | tf_op jit(solution)/shard_map/all_to_all | solution.py:194
  33.2 0.4 shard_map.66
  33.6 2.5 %collective-permute-start.1 = (bf16[4,64,256]{2,1,0:T(8,128)(2,1)S(1)}, bf16[4,64,256]{2,1,0:T(8,128)(2,1)S(1)}, u32[]{:S(2)}, u32[]{:S(2)}) collective-permute-start(bf16[4,64,256]{2,1,0:T(8,128)(2,1)S(1)} %get-tuple-element.13), channel_id=1, source_target_pairs={{0,8},{4,12},{8,16},{12,20},{16,24},{20,28},{24,32},{28,36},{32,40... | collective-permute-start | bytes 393224 | tf_op jit(solution)/shard_map/ppermute | solution.py:210
  36.1 1.3 %collective-permute-start = (bf16[8,64,256]{2,1,0:T(8,128)(2,1)S(1)}, bf16[8,64,256]{2,1,0:T(8,128)(2,1)S(1)}, u32[]{:S(2)}, u32[]{:S(2)}) collective-permute-start(bf16[8,64,256]{2,1,0:T(8,128)(2,1)S(1)} %get-tuple-element.12.own_ref), channel_id=1, source_target_pairs={{0,4},{8,12},{16,20},{24,28},{32,36},{40,44},{48,52},{56,60},{64,6... | collective-permute-start | bytes 786440 | tf_op jit(solution)/shard_map/ppermute | solution.py:211
  37.4 0.0 copy-start.5
  37.4 2.9 %collective-permute-start.3 = (bf16[4,64,256]{2,1,0:T(8,128)(2,1)S(1)}, bf16[4,64,256]{2,1,0:T(8,128)(2,1)S(1)}, u32[]{:S(2)}, u32[]{:S(2)}) collective-permute-start(bf16[4,64,256]{2,1,0:T(8,128)(2,1)S(1)} %get-tuple-element.14), channel_id=1, source_target_pairs={{0,8},{4,12},{8,16},{12,20},{16,24},{20,28},{24,32},{28,36},{32,40... | collective-permute-start | bytes 393224 | tf_op jit(solution)/shard_map/ppermute | solution.py:210
  40.4 2.2 %collective-permute-done.1.far_ref = bf16[4,64,256]{2,1,0:T(8,128)(2,1)S(1)} collective-permute-done((bf16[4,64,256]{2,1,0:T(8,128)(2,1)S(1)}, bf16[4,64,256]{2,1,0:T(8,128)(2,1)S(1)}, u32[]{:S(2)}, u32[]{:S(2)}) %collective-permute-start.1) | collective-permute-done | bytes 131104 | tf_op jit(solution)/shard_map/ppermute | solution.py:210
  42.6 1.3 %collective-permute-start.2 = (bf16[4,64,256]{2,1,0:T(8,128)(2,1)S(1)}, bf16[4,64,256]{2,1,0:T(8,128)(2,1)S(1)}, u32[]{:S(2)}, u32[]{:S(2)}) collective-permute-start(bf16[4,64,256]{2,1,0:T(8,128)(2,1)S(1)} %collective-permute-done.1.far_ref), channel_id=1, source_target_pairs={{4,0},{12,8},{20,16},{28,24},{36,32},{44,40},{52,48},{60,56},{68,6... | collective-permute-start | bytes 393224 | tf_op jit(solution)/shard_map/ppermute | solution.py:212
  43.9 0.7 %shard_map.64 = (bf16[2048,192]{1,0:T(8,128)(2,1)S(1)}, s32[2]{0:T(128)S(1)}) custom-call(s32[3,64,64]{2,1,0:T(8,128)S(1)} %copy-done.4, s32[2,128]{1,0:T(2,128)S(1)} %bitcast.8), custom_call_target="tpu_custom_call" | custom-call | flops 2000000000 | bytes 7812500 | tf_op jit(solution)/shard_map/pallas_call | solution.py:195
  44.6 1.8 %collective-permute-done.3.far_ref = bf16[4,64,256]{2,1,0:T(8,128)(2,1)S(1)} collective-permute-done((bf16[4,64,256]{2,1,0:T(8,128)(2,1)S(1)}, bf16[4,64,256]{2,1,0:T(8,128)(2,1)S(1)}, u32[]{:S(2)}, u32[]{:S(2)}) %collective-permute-start.3) | collective-permute-done | bytes 131104 | tf_op jit(solution)/shard_map/ppermute | solution.py:210
  46.4 1.3 %collective-permute-start.4 = (bf16[4,64,256]{2,1,0:T(8,128)(2,1)S(1)}, bf16[4,64,256]{2,1,0:T(8,128)(2,1)S(1)}, u32[]{:S(2)}, u32[]{:S(2)}) collective-permute-start(bf16[4,64,256]{2,1,0:T(8,128)(2,1)S(1)} %collective-permute-done.3.far_ref), channel_id=1, source_target_pairs={{4,0},{12,8},{20,16},{28,24},{36,32},{44,40},{52,48},{60,56},{68,6... | collective-permute-start | bytes 393224 | tf_op jit(solution)/shard_map/ppermute | solution.py:212
  47.7 1.4 %shard_map.67.sums_ref = f32[2,16,256]{2,1,0:T(8,128)S(1)} custom-call(bf16[2048,192]{1,0:T(8,128)(2,1)S(1)} %get-tuple-element.11.masks_ref, bf16[8,64,256]{2,1,0:T(8,128)(2,1)S(1)} %get-tuple-element.12.own_ref, bf16[8,64,256]{2,1,0:T(8,128)(2,1)S(1)} %collective-permute-done.near_ref, bf16[4,64,256]{2,1,0:T(8,128)(2,1)S(1)} %collective-permute-done.2.relay_ref, ...), custom_call_target="tpu_custom_call" | custom-call | flops 2000000000 | bytes 7812500 | tf_op jit(solution)/shard_map/pallas_call | solution.py:214
  49.1 0.5 collective-permute-done.4.relay_ref
  49.6 0.8 %shard_map.68.across_ref = f32[16,256]{1,0:T(8,128)S(1)} custom-call(bf16[2048,192]{1,0:T(8,128)(2,1)S(1)} %get-tuple-element.11.masks_ref, f32[2,16,256]{2,1,0:T(8,128)S(1)} %shard_map.67.sums_ref, bf16[8,64,256]{2,1,0:T(8,128)(2,1)S(1)} %get-tuple-element.12.own_ref, bf16[8,64,256]{2,1,0:T(8,128)(2,1)S(1)} %collective-permute-done.near_ref, ...), custom_call_target="tpu_custom_call" | custom-call | tf_op jit(solution)/shard_map/pallas_call | solution.py:218
  50.4 3.6 %collective-permute-start.5 = (f32[16,256]{1,0:T(8,128)S(1)}, f32[16,256]{1,0:T(8,128)S(1)}, u32[]{:S(2)}, u32[]{:S(2)}) collective-permute-start(f32[16,256]{1,0:T(8,128)S(1)} %shard_map.68.across_ref), channel_id=1, source_target_pairs={{4,8},{12,16},{20,24},{28,32},{36,40},{44,48},{52,56},{60,64},{68,... | collective-permute-start | bytes 49160 | tf_op jit(solution)/shard_map/ppermute | solution.py:220
  54.0 0.0 copy-start.1
  54.0 0.8 %shard_map.69.inside_ref = f32[16,256]{1,0:T(8,128)S(1)} custom-call(bf16[2048,192]{1,0:T(8,128)(2,1)S(1)} %get-tuple-element.11.masks_ref, f32[2,16,256]{2,1,0:T(8,128)S(1)} %shard_map.67.sums_ref, bf16[8,64,256]{2,1,0:T(8,128)(2,1)S(1)} %get-tuple-element.12.own_ref, bf16[8,64,256]{2,1,0:T(8,128)(2,1)S(1)} %collective-permute-done.near_ref, ...), custom_call_target="tpu_custom_call" | custom-call | flops 1000000000 | bytes 3906250 | tf_op jit(solution)/shard_map/pallas_call | solution.py:221
  54.8 0.0 copy-start
  54.8 2.8 %collective-permute-done.5.arrived_ref = f32[16,256]{1,0:T(8,128)S(1)} collective-permute-done((f32[16,256]{1,0:T(8,128)S(1)}, f32[16,256]{1,0:T(8,128)S(1)}, u32[]{:S(2)}, u32[]{:S(2)}) %collective-permute-start.5) | collective-permute-done | bytes 16416 | tf_op jit(solution)/shard_map/ppermute | solution.py:220
  57.6 9.6 %all_to_all.11.sums_ref = bf16[8,32,256]{2,1,0:T(8,128)(2,1)S(1)} all-to-all(bf16[8,32,256]{2,1,0:T(8,128)(2,1)S(1)} %shard_map.70), channel_id=1, replica_groups={{0,1,2,3,4,5,6,7},{8,9,10,11,12,13,14,15},{16,17,18,19,20,21,22,23},{24..., dimensions={0} | all-to-all | bytes 262144 | tf_op jit(solution)/shard_map/all_to_all | solution.py:229
  67.3 1.6 %shard_map.71 = f32[128,256]{1,0:T(8,128)} custom-call(s32[2]{0:T(128)S(1)} %get-tuple-element.10.place_ref, bf16[8,32,256]{2,1,0:T(8,128)(2,1)S(1)} %all_to_all.11.sums_ref, f32[2,8,32,128]{3,2,1,0:T(8,128)S(1)} %copy-done.1, bf16[768,256]{1,0:T(8,128)(2,1)S(1)} %copy-done), custom_call_target="tpu_custom_call" | custom-call | tf_op jit(solution)/shard_map/pallas_call | solution.py:232
  (10 shorter events, 0.0 us)
Async XLA Ops:
  0.0 0.9 %copy-start.2 = (bf16[1,16,8192]{2,1,0:T(8,128)(2,1)S(1)}, bf16[1,16,8192]{2,1,0:T(8,128)(2,1)}, u32[]{:S(2)}) copy-start(bf16[1,16,8192]{2,1,0:T(8,128)(2,1)} %param.6) | copy-start | bytes 786436
  1.1 32.1 %copy-start.3 = (bf16[256,256]{1,0:T(8,128)(2,1)S(1)}, bf16[256,256]{1,0:T(8,128)(2,1)}, u32[]{:S(2)}) copy-start(bf16[256,256]{1,0:T(8,128)(2,1)} %constant.6.clone.table_ref) | copy-start | bytes 393220
  33.2 10.7 %copy-start.4 = (s32[3,64,64]{2,1,0:T(8,128)S(1)}, s32[3,64,64]{2,1,0:T(8,128)}, u32[]{:S(2)}) copy-start(s32[3,64,64]{2,1,0:T(8,128)} %ids_ref.1) | copy-start | bytes 147460
  33.6 9.0 %collective-permute-start.1 = (bf16[4,64,256]{2,1,0:T(8,128)(2,1)S(1)}, bf16[4,64,256]{2,1,0:T(8,128)(2,1)S(1)}, u32[]{:S(2)}, u32[]{:S(2)}) collective-permute-start(bf16[4,64,256]{2,1,0:T(8,128)(2,1)S(1)} %get-tuple-element.13), channel_id=1, source_target_pairs={{0,8},{4,12},{8,16},{12,20},{16,24},{20,28},{24,32},{28,36},{32,40... | collective-permute-start | bytes 393224 | tf_op jit(solution)/shard_map/ppermute | solution.py:210
  36.1 11.6 %collective-permute-start = (bf16[8,64,256]{2,1,0:T(8,128)(2,1)S(1)}, bf16[8,64,256]{2,1,0:T(8,128)(2,1)S(1)}, u32[]{:S(2)}, u32[]{:S(2)}) collective-permute-start(bf16[8,64,256]{2,1,0:T(8,128)(2,1)S(1)} %get-tuple-element.12.own_ref), channel_id=1, source_target_pairs={{0,4},{8,12},{16,20},{24,28},{32,36},{40,44},{48,52},{56,60},{64,6... | collective-permute-start | bytes 786440 | tf_op jit(solution)/shard_map/ppermute | solution.py:211
  37.4 6.5 %copy-start.5 = (s32[256]{0:T(256)S(1)}, s32[256]{0:T(256)}, u32[]{:S(2)}) copy-start(s32[256]{0:T(256)} %param.8) | copy-start | bytes 3076
  37.4 9.0 %collective-permute-start.3 = (bf16[4,64,256]{2,1,0:T(8,128)(2,1)S(1)}, bf16[4,64,256]{2,1,0:T(8,128)(2,1)S(1)}, u32[]{:S(2)}, u32[]{:S(2)}) collective-permute-start(bf16[4,64,256]{2,1,0:T(8,128)(2,1)S(1)} %get-tuple-element.14), channel_id=1, source_target_pairs={{0,8},{4,12},{8,16},{12,20},{16,24},{20,28},{24,32},{28,36},{32,40... | collective-permute-start | bytes 393224 | tf_op jit(solution)/shard_map/ppermute | solution.py:210
  42.6 5.1 %collective-permute-start.2 = (bf16[4,64,256]{2,1,0:T(8,128)(2,1)S(1)}, bf16[4,64,256]{2,1,0:T(8,128)(2,1)S(1)}, u32[]{:S(2)}, u32[]{:S(2)}) collective-permute-start(bf16[4,64,256]{2,1,0:T(8,128)(2,1)S(1)} %collective-permute-done.1.far_ref), channel_id=1, source_target_pairs={{4,0},{12,8},{20,16},{28,24},{36,32},{44,40},{52,48},{60,56},{68,6... | collective-permute-start | bytes 393224 | tf_op jit(solution)/shard_map/ppermute | solution.py:212
  46.4 3.2 %collective-permute-start.4 = (bf16[4,64,256]{2,1,0:T(8,128)(2,1)S(1)}, bf16[4,64,256]{2,1,0:T(8,128)(2,1)S(1)}, u32[]{:S(2)}, u32[]{:S(2)}) collective-permute-start(bf16[4,64,256]{2,1,0:T(8,128)(2,1)S(1)} %collective-permute-done.3.far_ref), channel_id=1, source_target_pairs={{4,0},{12,8},{20,16},{28,24},{36,32},{44,40},{52,48},{60,56},{68,6... | collective-permute-start | bytes 393224 | tf_op jit(solution)/shard_map/ppermute | solution.py:212
  50.4 7.2 %collective-permute-start.5 = (f32[16,256]{1,0:T(8,128)S(1)}, f32[16,256]{1,0:T(8,128)S(1)}, u32[]{:S(2)}, u32[]{:S(2)}) collective-permute-start(f32[16,256]{1,0:T(8,128)S(1)} %shard_map.68.across_ref), channel_id=1, source_target_pairs={{4,8},{12,16},{20,24},{28,32},{36,40},{44,48},{52,56},{60,64},{68,... | collective-permute-start | bytes 49160 | tf_op jit(solution)/shard_map/ppermute | solution.py:220
  54.0 13.2 %copy-start.1 = (f32[2,8,32,128]{3,2,1,0:T(8,128)S(1)}, f32[2,8,32,128]{3,2,1,0:T(8,128)}, u32[]{:S(2)}) copy-start(f32[2,8,32,128]{3,2,1,0:T(8,128)} %constant.7.clone.slant_ref) | copy-start | bytes 786436
  54.8 12.5 %copy-start = (bf16[768,256]{1,0:T(8,128)(2,1)S(1)}, bf16[768,256]{1,0:T(8,128)(2,1)}, u32[]{:S(2)}) copy-start(bf16[768,256]{1,0:T(8,128)(2,1)} %constant.8.clone.lags_ref) | copy-start | bytes 1179652

commit v5 on v2

--- a/solution.py
+++ b/solution.py
@@ -71,15 +71,12 @@
         out_ref[tile] = jnp.concatenate([even, odd], axis=0).astype(jnp.bfloat16)
 
 
-def mask_kernel(ids_ref, masks_ref):
+def mask_kernel(ids_ref, owner_ref, masks_ref, place_ref):
     ids = jnp.concatenate([ids_ref[0], ids_ref[1], ids_ref[2]], axis=1)
     for bin_at in range(BINS):
         masks_ref[bin_at * CH_DEV : (bin_at + 1) * CH_DEV, :] = (
             (ids == bin_at).astype(jnp.float32).astype(jnp.bfloat16)
         )
-
-
-def place_kernel(owner_ref, place_ref):
     device = lax.axis_index("chan")
     owner = owner_ref[...]
     place_ref[0] = jnp.sum((owner < device).astype(jnp.int32)) - MB_DEV * (device - 1)
@@ -89,7 +86,7 @@
 def spectra_kernel(series_ref, table_ref, out_ref):
     table = table_ref[...]
     for window in range(NWIN):
-        turned = series_ref[window].astype(jnp.float32).T.astype(jnp.bfloat16)
+        turned = series_ref[window].T
         series = jnp.concatenate([turned[:CH_DEV], turned[CH_DEV:]], axis=1)
         spectra = jnp.dot(series, table, preferred_element_type=jnp.float32)
         power = jnp.mean(spectra * spectra, axis=-1, keepdims=True)
@@ -123,8 +120,8 @@
 
 def merge_kernel(across_ref, inside_ref, arrived_ref, out_ref):
     odd = lax.rem(lax.axis_index("chan"), 2)
-    across = (across_ref[...] + arrived_ref[...]).astype(jnp.bfloat16)
-    inside = inside_ref[...].astype(jnp.bfloat16)
+    across = across_ref[...].astype(jnp.bfloat16)
+    inside = (inside_ref[...] + arrived_ref[...]).astype(jnp.bfloat16)
     merged = jnp.concatenate(
         [jnp.where(odd == 1, inside, across), jnp.where(odd == 1, across, inside)], axis=0
     )
@@ -141,11 +138,13 @@
             total = total + sums_ref[part * 4 + period, rows].astype(jnp.float32)
         return total
 
-    own = over_periods(odd, pl.ds(0, BINS))
-    beside = over_periods(1 - odd, pl.ds(pl.multiple_of(odd * HALF, HALF), HALF))
+    device = lax.axis_index("chan")
+    own = over_periods(1 - odd, pl.ds(0, BINS))
+    beside = over_periods(odd, pl.ds(pl.multiple_of((1 - odd) * HALF, HALF), HALF))
+    beside = jnp.where((device > 0) & (device < lax.axis_size("chan") - 1), beside, 0.0)
     held[...] = jnp.zeros_like(held)
-    held[:HALF] = own[:HALF] + jnp.where(odd == 1, beside, 0.0)
-    held[HALF:BINS] = own[HALF:] + jnp.where(odd == 1, 0.0, beside)
+    held[:HALF] = own[:HALF] + jnp.where(odd == 1, 0.0, beside)
+    held[HALF:BINS] = own[HALF:] + jnp.where(odd == 1, beside, 0.0)
     count = place_ref[1]
     first = jnp.where(count > 0, place_ref[0], 0)
     for slot in range(CAP):
@@ -178,30 +177,31 @@
     vmem = pl.BlockSpec(memory_space=pltpu.VMEM)
     packed = call(pack_kernel, jax.ShapeDtypeStruct((count // 2, 16, 128), jnp.bfloat16))(raw_strain[0])
     series = lax.all_to_all(packed.reshape(count, 8, 128), "chan", 0, 0, tiled=True)
-    masks = call(
+    masks, place = call(
         mask_kernel,
-        jax.ShapeDtypeStruct((BINS * CH_DEV, 3 * CH_DEV), jnp.bfloat16),
+        (
+            jax.ShapeDtypeStruct((BINS * CH_DEV, 3 * CH_DEV), jnp.bfloat16),
+            jax.ShapeDtypeStruct((2,), jnp.int32),
+        ),
         flops=2000000000,
-    )(bin_ids)
+        out_specs=(vmem, smem),
+    )(bin_ids, owner_map.reshape(2, 128))
     own = call(spectra_kernel, jax.ShapeDtypeStruct((NWIN, CH_DEV, 2 * NF), jnp.bfloat16))(
         series.reshape(NWIN, 128, 128), jnp.asarray(dft_rows(), jnp.bfloat16)
     )
     near = lax.ppermute(own, "chan", [(i, i + 1) for i in range(count - 1)])
     far = lax.ppermute(own, "chan", [(i, i + 2) for i in range(count - 2)])
-    place = call(place_kernel, jax.ShapeDtypeStruct((2,), jnp.int32), out_specs=smem)(
-        owner_map.reshape(2, 128)
-    )
     part = jax.ShapeDtypeStruct((HALF, 2 * NF), jnp.float32)
-    across = call(functools.partial(bin_kernel, True), part)(masks, own, near, far)
-    pairs = [(2 * k + 1, 2 * k + 2) for k in range(count // 2 - 1)]
-    arrived = lax.ppermute(across, "chan", pairs + [(j, i) for i, j in pairs])
-    inside = call(functools.partial(bin_kernel, False), part, flops=2000000000)(masks, own, near, far)
+    inside = call(functools.partial(bin_kernel, False), part)(masks, own, near, far)
+    pairs = [(i, i + 1) for i in range(0, count, 2)]
+    arrived = lax.ppermute(inside, "chan", pairs + [(j, i) for i, j in pairs])
+    across = call(functools.partial(bin_kernel, True), part, flops=2000000000)(masks, own, near, far)
     merged = call(merge_kernel, jax.ShapeDtypeStruct((8, BINS, 2 * NF), jnp.bfloat16))(
         across, inside, arrived
     )
     groups = [
-        [(2 * k + core) * periods + p for core in range(2) for p in range(periods)]
-        for k in range(count // 2)
+        [at % count * periods + p for at in (i + 1, i + 2) for p in range(periods)]
+        for i in range(0, count, 2)
     ]
     sums = lax.all_to_all(
         merged, ("chan", "period"), 0, 0, tiled=True, axis_index_groups=groups

time: 69.1 us -> 66.8 us (0.967)
  blocking collectives: 32.1 us -> 44.5 us
  waiting for transfers between devices: 17.6 us -> 9.02 us
  starting transfers between devices: 10.6 us -> 6.33 us
  Pallas kernels: 6.44 us -> 5.6 us
    all_to_all x0 -> x1, blocking collectives: none -> 12.4 us  [shards(): lax.all_to_all(merged, ('chan', 'period'), 0, 0, tiled=True, axis_index_g...]
    all_to_all x1 -> x0, starting transfers between devices: 4.3 us -> none  [shards(): lax.all_to_all(merged, ('chan', 'period'), 0, 0, tiled=True, axis_index_g...]
    all_to_all x1 -> x0, waiting for transfers between devices: 4.15 us -> none  [shards(): lax.all_to_all(merged, ('chan', 'period'), 0, 0, tiled=True, axis_index_g...]
    ppermute x1, waiting for transfers between devices: 3.89 us -> 0.01 us  [shards(): arrived = lax.ppermute(inside, 'chan', pairs + [(j, i) for i, j in pairs])]
    pallas_call x4 -> x3, Pallas kernels: 3.54 us -> 3.36 us  [the longest x1 1.32 us: shards(): call(functools.partial(bin_kernel, True), part, flops=2000000000)]
  transfers between devices with their start and end apart: 4 -> 3, of which waited for: 4 -> 2; matrix products, arithmetic and copies ran while one was open for 0% -> 0% of each run, Pallas kernels for 3% -> 3%
where the time goes in v5:
time: 66.8 us; the launch traced here: 66.5 us
  blocking collectives  44.5 us (67%)
  waiting for transfers between devices  9.02 us (14%)
  starting transfers between devices  6.33 us (9%)
  Pallas kernels  5.6 us (8%)
  local copies, waits for them, and re-layouts  0.98 us (1%)
    all_to_all x1, blocking collectives, shards(): lax.all_to_all(packed.reshape(count, 8, 128), 'chan', 0, 0, tiled=True)  32.1 us
    all_to_all x1, blocking collectives, shards(): lax.all_to_all(merged, ('chan', 'period'), 0, 0, tiled=True, axis_index_g...  12.4 us
    ppermute x1, waiting for transfers between devices, shards(): far = lax.ppermute(own, 'chan', [(i, i + 2) for i in range(count - 2)])  8.07 us
    ppermute x1, starting transfers between devices, shards(): far = lax.ppermute(own, 'chan', [(i, i + 2) for i in range(count - 2)])  2.49 us
    ppermute x1, starting transfers between devices, shards(): near = lax.ppermute(own, 'chan', [(i, i + 1) for i in range(count - 1)])  1.92 us
    ppermute x1, starting transfers between devices, shards(): arrived = lax.ppermute(inside, 'chan', pairs + [(j, i) for i, j in pairs])  1.92 us
    pallas_call x1, Pallas kernels, shards(): call(stack_kernel, jax.ShapeDtypeStruct((CAP * NP, WIN), jnp.float32), in...  1.63 us
  transfers between devices with their start and end apart: 3, of which 2 were waited for; matrix products, arithmetic and copies ran while one was open for 0% of the time, Pallas kernels for 3%

profile of v5, /device:TPU:8, one launch (start us, length us, event | category | flops | bytes accessed | tf_op | source)
XLA Modules:
  0.0 66.5 jit_solution(12589201632331510919)
XLA Ops:
  0.0 0.9 %copy-done.2 = bf16[1,16,8192]{2,1,0:T(8,128)(2,1)S(1)} copy-done((bf16[1,16,8192]{2,1,0:T(8,128)(2,1)S(1)}, bf16[1,16,8192]{2,1,0:T(8,128)(2,1)}, u32[]{:S(2)}) %copy-start.2) | copy-done | bytes 262168
  1.0 0.1 shard_map.65
  1.1 0.0 copy-start.3
  1.1 32.1 %all_to_all.10 = bf16[128,8,128]{2,1,0:T(8,128)(2,1)S(1)} all-to-all(bf16[128,8,128]{2,1,0:T(8,128)(2,1)S(1)} %bitcast.6), channel_id=1, replica_groups=mesh['chan'=128,'period'=4] {'chan'}, dimensions={0} | all-to-all | bytes 524288 | tf_op jit(solution)/shard_map/all_to_all | solution.py:179
  33.2 0.0 copy-done.3
  33.2 0.4 shard_map.66.own_ref
  33.6 0.0 copy-start.5
  33.6 2.5 %collective-permute-start.1 = (bf16[8,64,256]{2,1,0:T(8,128)(2,1)S(1)}, bf16[8,64,256]{2,1,0:T(8,128)(2,1)S(1)}, u32[]{:S(2)}, u32[]{:S(2)}) collective-permute-start(bf16[8,64,256]{2,1,0:T(8,128)(2,1)S(1)} %shard_map.66.own_ref), channel_id=1, source_target_pairs={{0,8},{4,12},{8,16},{12,20},{16,24},{20,28},{24,32},{28,36},{32,40... | collective-permute-start | bytes 786440 | tf_op jit(solution)/shard_map/ppermute | solution.py:193
  36.1 1.9 %collective-permute-start = (bf16[8,64,256]{2,1,0:T(8,128)(2,1)S(1)}, bf16[8,64,256]{2,1,0:T(8,128)(2,1)S(1)}, u32[]{:S(2)}, u32[]{:S(2)}) collective-permute-start(bf16[8,64,256]{2,1,0:T(8,128)(2,1)S(1)} %shard_map.66.own_ref), channel_id=1, source_target_pairs={{0,4},{4,8},{8,12},{12,16},{16,20},{20,24},{24,28},{28,32},{32,36}... | collective-permute-start | bytes 786440 | tf_op jit(solution)/shard_map/ppermute | solution.py:192
  38.1 0.0 copy-done.4
  38.1 0.0 copy-done.5
  38.1 0.7 %shard_map.64 = (bf16[2048,192]{1,0:T(8,128)(2,1)S(1)}, s32[2]{0:T(128)S(1)}) custom-call(s32[3,64,64]{2,1,0:T(8,128)S(1)} %copy-done.4, s32[2,128]{1,0:T(2,128)S(1)} %bitcast.8), custom_call_target="tpu_custom_call" | custom-call | flops 2000000000 | bytes 7812500 | tf_op jit(solution)/shard_map/pallas_call | solution.py:180
  38.8 8.1 %collective-permute-done.1.far_ref = bf16[8,64,256]{2,1,0:T(8,128)(2,1)S(1)} collective-permute-done((bf16[8,64,256]{2,1,0:T(8,128)(2,1)S(1)}, bf16[8,64,256]{2,1,0:T(8,128)(2,1)S(1)}, u32[]{:S(2)}, u32[]{:S(2)}) %collective-permute-start.1) | collective-permute-done | bytes 262176 | tf_op jit(solution)/shard_map/ppermute | solution.py:193
  46.9 1.0 %collective-permute-done.near_ref = bf16[8,64,256]{2,1,0:T(8,128)(2,1)S(1)} collective-permute-done((bf16[8,64,256]{2,1,0:T(8,128)(2,1)S(1)}, bf16[8,64,256]{2,1,0:T(8,128)(2,1)S(1)}, u32[]{:S(2)}, u32[]{:S(2)}) %collective-permute-start) | collective-permute-done | bytes 262176 | tf_op jit(solution)/shard_map/ppermute | solution.py:192
  47.8 1.3 %shard_map.68.inside_ref = f32[16,256]{1,0:T(8,128)S(1)} custom-call(bf16[2048,192]{1,0:T(8,128)(2,1)S(1)} %get-tuple-element.8.masks_ref, bf16[8,64,256]{2,1,0:T(8,128)(2,1)S(1)} %shard_map.66.own_ref, bf16[8,64,256]{2,1,0:T(8,128)(2,1)S(1)} %collective-permute-done.near_ref, bf16[8,64,256]{2,1,0:T(8,128)(2,1)S(1)} %collective-permute-done.1.far_ref), custom_call_target="tpu_custom_call" | custom-call | tf_op jit(solution)/shard_map/pallas_call | solution.py:195
  49.2 1.9 %collective-permute-start.2 = (f32[16,256]{1,0:T(8,128)S(1)}, f32[16,256]{1,0:T(8,128)S(1)}, u32[]{:S(2)}, u32[]{:S(2)}) collective-permute-start(f32[16,256]{1,0:T(8,128)S(1)} %shard_map.68.inside_ref), channel_id=1, source_target_pairs={{0,4},{8,12},{16,20},{24,28},{32,36},{40,44},{48,52},{56,60},{64,6... | collective-permute-start | bytes 49160 | tf_op jit(solution)/shard_map/ppermute | solution.py:197
  51.1 0.0 copy-start.1
  51.1 1.3 %shard_map.67.across_ref = f32[16,256]{1,0:T(8,128)S(1)} custom-call(bf16[2048,192]{1,0:T(8,128)(2,1)S(1)} %get-tuple-element.8.masks_ref, bf16[8,64,256]{2,1,0:T(8,128)(2,1)S(1)} %shard_map.66.own_ref, bf16[8,64,256]{2,1,0:T(8,128)(2,1)S(1)} %collective-permute-done.near_ref, bf16[8,64,256]{2,1,0:T(8,128)(2,1)S(1)} %collective-permute-done.1.far_ref), custom_call_target="tpu_custom_call" | custom-call | flops 2000000000 | bytes 7812500 | tf_op jit(solution)/shard_map/pallas_call | solution.py:198
  52.4 0.0 copy-start
  52.4 0.0 collective-permute-done.2.arrived_ref
  52.5 12.4 %all_to_all.11.sums_ref = bf16[8,32,256]{2,1,0:T(8,128)(2,1)S(1)} all-to-all(bf16[8,32,256]{2,1,0:T(8,128)(2,1)S(1)} %shard_map.69), channel_id=1, replica_groups={{4,5,6,7,8,9,10,11},{12,13,14,15,16,17,18,19},{20,21,22,23,24,25,26,27}..., dimensions={0} | all-to-all | bytes 262144 | tf_op jit(solution)/shard_map/all_to_all | solution.py:206
  64.9 0.0 copy-done.1
  64.9 0.0 copy-done
  64.9 1.6 %shard_map.70 = f32[128,256]{1,0:T(8,128)} custom-call(s32[2]{0:T(128)S(1)} %get-tuple-element.7.place_ref, bf16[8,32,256]{2,1,0:T(8,128)(2,1)S(1)} %all_to_all.11.sums_ref, f32[2,8,32,128]{3,2,1,0:T(8,128)S(1)} %copy-done.1, bf16[768,256]{1,0:T(8,128)(2,1)S(1)} %copy-done), custom_call_target="tpu_custom_call" | custom-call | tf_op jit(solution)/shard_map/pallas_call | solution.py:209
  (3 shorter events, 0.0 us)
Async XLA Ops:
  0.0 0.9 %copy-start.2 = (bf16[1,16,8192]{2,1,0:T(8,128)(2,1)S(1)}, bf16[1,16,8192]{2,1,0:T(8,128)(2,1)}, u32[]{:S(2)}) copy-start(bf16[1,16,8192]{2,1,0:T(8,128)(2,1)} %param.6) | copy-start | bytes 786436
  1.1 32.1 %copy-start.3 = (bf16[256,256]{1,0:T(8,128)(2,1)S(1)}, bf16[256,256]{1,0:T(8,128)(2,1)}, u32[]{:S(2)}) copy-start(bf16[256,256]{1,0:T(8,128)(2,1)} %constant.6.clone.table_ref) | copy-start | bytes 393220
  33.2 4.9 %copy-start.4 = (s32[3,64,64]{2,1,0:T(8,128)S(1)}, s32[3,64,64]{2,1,0:T(8,128)}, u32[]{:S(2)}) copy-start(s32[3,64,64]{2,1,0:T(8,128)} %ids_ref.1) | copy-start | bytes 147460
  33.6 4.4 %copy-start.5 = (s32[256]{0:T(256)S(1)}, s32[256]{0:T(256)}, u32[]{:S(2)}) copy-start(s32[256]{0:T(256)} %param.8) | copy-start | bytes 3076
  33.6 13.2 %collective-permute-start.1 = (bf16[8,64,256]{2,1,0:T(8,128)(2,1)S(1)}, bf16[8,64,256]{2,1,0:T(8,128)(2,1)S(1)}, u32[]{:S(2)}, u32[]{:S(2)}) collective-permute-start(bf16[8,64,256]{2,1,0:T(8,128)(2,1)S(1)} %shard_map.66.own_ref), channel_id=1, source_target_pairs={{0,8},{4,12},{8,16},{12,20},{16,24},{20,28},{24,32},{28,36},{32,40... | collective-permute-start | bytes 786440 | tf_op jit(solution)/shard_map/ppermute | solution.py:193
  36.1 11.7 %collective-permute-start = (bf16[8,64,256]{2,1,0:T(8,128)(2,1)S(1)}, bf16[8,64,256]{2,1,0:T(8,128)(2,1)S(1)}, u32[]{:S(2)}, u32[]{:S(2)}) collective-permute-start(bf16[8,64,256]{2,1,0:T(8,128)(2,1)S(1)} %shard_map.66.own_ref), channel_id=1, source_target_pairs={{0,4},{4,8},{8,12},{12,16},{16,20},{20,24},{24,28},{28,32},{32,36}... | collective-permute-start | bytes 786440 | tf_op jit(solution)/shard_map/ppermute | solution.py:192
  49.2 3.3 %collective-permute-start.2 = (f32[16,256]{1,0:T(8,128)S(1)}, f32[16,256]{1,0:T(8,128)S(1)}, u32[]{:S(2)}, u32[]{:S(2)}) collective-permute-start(f32[16,256]{1,0:T(8,128)S(1)} %shard_map.68.inside_ref), channel_id=1, source_target_pairs={{0,4},{8,12},{16,20},{24,28},{32,36},{40,44},{48,52},{56,60},{64,6... | collective-permute-start | bytes 49160 | tf_op jit(solution)/shard_map/ppermute | solution.py:197
  51.1 13.8 %copy-start.1 = (f32[2,8,32,128]{3,2,1,0:T(8,128)S(1)}, f32[2,8,32,128]{3,2,1,0:T(8,128)}, u32[]{:S(2)}) copy-start(f32[2,8,32,128]{3,2,1,0:T(8,128)} %constant.7.clone.slant_ref) | copy-start | bytes 786436
  52.4 12.5 %copy-start = (bf16[768,256]{1,0:T(8,128)(2,1)S(1)}, bf16[768,256]{1,0:T(8,128)(2,1)}, u32[]{:S(2)}) copy-start(bf16[768,256]{1,0:T(8,128)(2,1)} %constant.8.clone.lags_ref) | copy-start | bytes 1179652

commit v6 on v5

v6 whole, which is shorter than its diff:
```python
import functools
import math

import jax
import jax.numpy as jnp
import numpy as np
from jax import lax
from jax.experimental import pallas as pl
from jax.experimental.pallas import tpu as pltpu
from jax.sharding import PartitionSpec as P

CH_DEV = 64
WIN = 256
NF = 128
NWIN = 8
PART = NWIN // 2
MB_DEV = 2
NOFF = 8
NP = 32
CAP = 4
BINS = 2 * MB_DEV * NOFF
HALF = BINS // 2
VMEM_LIMIT = 48 * 1024 * 1024

def dft_rows():
    phase = 2.0 * math.pi / WIN * np.mod(np.arange(WIN)[:, None] * np.arange(1, NF + 1)[None, :], WIN)
    return np.concatenate([np.cos(phase), -np.sin(phase)], axis=1).astype(np.float32)


def lag_table():
    phase = 2.0 * math.pi / WIN * np.mod(np.arange(1, NF + 1)[:, None] * np.arange(WIN)[None, :], WIN)
    return np.concatenate([np.cos(phase), -np.sin(phase)], axis=0).astype(np.float32)


def lag_parts():
    table = lag_table()
    high = table.astype(jnp.bfloat16)
    low = (table - high.astype(np.float32)).astype(jnp.bfloat16)
    return np.concatenate([high, high, low], axis=0)


def slant_tables():
    slow = (np.arange(NP) - NP // 2) / (4.0 * NP)
    offset = (np.arange(NOFF) + 0.5) * (3.0 * CH_DEV / NOFF)
    freq = np.arange(1, NF + 1) * (2.0 * math.pi / WIN)
    phase = offset[:, None, None] * slow[None, :, None] * freq[None, None, :]
    return np.stack([np.cos(phase), np.sin(phase)]).astype(np.float32)


def call(kernel, out_shape, flops=0, **kw):
    return pl.pallas_call(
        kernel,
        out_shape=out_shape,
        cost_estimate=pl.CostEstimate(flops=flops, bytes_accessed=flops // 256, transcendentals=0),
        compiler_params=pltpu.CompilerParams(vmem_limit_bytes=VMEM_LIMIT),
        **kw,
    )


def pack_kernel(raw_ref, out_ref):
    out_ref[0] = jnp.zeros((16, 128), jnp.bfloat16)
    for chip in range(raw_ref.shape[1] // 128):
        tile = raw_ref[:, 128 * chip : 128 * chip + 128]
        out_ref[2 * chip + 1] = tile
        if 2 * chip + 2 < out_ref.shape[0]:
            out_ref[2 * chip + 2] = tile


def mask_kernel(ids_ref, other_ref, owner_ref, masks_ref, place_ref):
    device = lax.axis_index("chan")
    odd = lax.rem(device, 2) == 1
    own = jnp.concatenate([ids_ref[2], ids_ref[1], ids_ref[0]], axis=1)
    other = jnp.concatenate([other_ref[2], other_ref[1], other_ref[0]], axis=1)
    for block in range(2):
        ids = jnp.where(odd, own, other) if block else jnp.where(odd, other, own)
        for bin_at in range(BINS):
            masks_ref[block, bin_at * CH_DEV : (bin_at + 1) * CH_DEV, :] = (
                (ids == bin_at).astype(jnp.float32).astype(jnp.bfloat16)
            )
    owner = owner_ref[...]
    place_ref[0] = jnp.sum((owner < device).astype(jnp.int32)) - MB_DEV * (device - 1)
    place_ref[1] = jnp.sum((owner == device).astype(jnp.int32))


def spectra_kernel(series_ref, table_ref, keep_ref, give_ref):
    table = table_ref[...]
    odd = lax.rem(lax.axis_index("chan"), 2)
    for out_ref, first in ((give_ref, (1 - odd) * PART), (keep_ref, odd * PART)):
        for window in range(PART):
            series = series_ref[first + window].T
            spectra = jnp.dot(series, table, preferred_element_type=jnp.float32)
            power = jnp.mean(spectra * spectra, axis=-1, keepdims=True)
            out_ref[window] = (spectra / jnp.sqrt(power + 1e-06)).astype(jnp.bfloat16)


def add_bins(masks_ref, spectra_ref, sources):
    totals = None
    for block, half in sources:
        rows = slice(half * HALF * CH_DEV, (half + 1) * HALF * CH_DEV)
        for window in range(PART):
            partners = spectra_ref[window, block * CH_DEV : (block + 3) * CH_DEV]
            own = spectra_ref[window, (block + 2) * CH_DEV : (block + 3) * CH_DEV]
            own = own.astype(jnp.float32)
            own_real, own_imag = own[:, :NF], own[:, NF:]
            picked = jnp.dot(masks_ref[block, rows, :], partners, preferred_element_type=jnp.float32)
            terms = []
            for bin_at in range(HALF):
                picked_real = picked[bin_at * CH_DEV : (bin_at + 1) * CH_DEV, :NF]
                picked_imag = picked[bin_at * CH_DEV : (bin_at + 1) * CH_DEV, NF:]
                real = own_real * picked_real + own_imag * picked_imag
                imag = own_imag * picked_real - own_real * picked_imag
                terms.append(jnp.sum(real.reshape(8, 8, NF), axis=0))
                terms.append(jnp.sum(imag.reshape(8, 8, NF), axis=0))
            totals = terms if totals is None else [x + y for x, y in zip(totals, terms)]
    sums = [jnp.sum(total, axis=0, keepdims=True) for total in totals]
    return [jnp.concatenate(sums[2 * k : 2 * k + 2], axis=1) for k in range(HALF)]


def give_kernel(masks_ref, kept_ref, came_ref, spectra_ref, whole_ref):
    odd = lax.rem(lax.axis_index("chan"), 2) == 1
    for window in range(PART):
        kept, came = kept_ref[window], came_ref[window]
        spectra_ref[window, : 2 * CH_DEV] = jnp.where(odd, came, kept)
        spectra_ref[window, 2 * CH_DEV :] = jnp.where(odd, kept, came)
    for bin_at, row in enumerate(add_bins(masks_ref, spectra_ref, ((0, 1), (1, 0)))):
        whole_ref[HALF + bin_at : HALF + bin_at + 1] = row

    @pl.when(odd)
    def _():
        for bin_at, row in enumerate(add_bins(masks_ref, spectra_ref, ((0, 0),))):
            whole_ref[bin_at : bin_at + 1] = row

    @pl.when(jnp.logical_not(odd))
    def _():
        for bin_at, row in enumerate(add_bins(masks_ref, spectra_ref, ((1, 1),))):
            whole_ref[bin_at : bin_at + 1] = row


def keep_kernel(masks_ref, spectra_ref, out_ref):
    odd = lax.rem(lax.axis_index("chan"), 2) == 1

    @pl.when(odd)
    def _():
        for bin_at, row in enumerate(add_bins(masks_ref, spectra_ref, ((1, 1),))):
            out_ref[bin_at : bin_at + 1] = row

    @pl.when(jnp.logical_not(odd))
    def _():
        for bin_at, row in enumerate(add_bins(masks_ref, spectra_ref, ((0, 0),))):
            out_ref[bin_at : bin_at + 1] = row


def merge_kernel(gave_ref, came_ref, edge_ref, out_ref):
    odd = lax.rem(lax.axis_index("chan"), 2) == 1
    edge = (edge_ref[...] + came_ref[:HALF]).astype(jnp.bfloat16)
    middle = (gave_ref[HALF:] + came_ref[HALF:]).astype(jnp.bfloat16)
    merged = jnp.concatenate([jnp.where(odd, middle, edge), jnp.where(odd, edge, middle)], axis=0)
    for place in range(8):
        out_ref[place] = merged


def stack_kernel(place_ref, sums_ref, slant_ref, lags_ref, out_ref, held, spec):
    odd = lax.rem(lax.axis_index("chan"), 2)

    def over_periods(part, rows):
        total = sums_ref[part * 4, rows].astype(jnp.float32)
        for period in range(1, 4):
            total = total + sums_ref[part * 4 + period, rows].astype(jnp.float32)
        return total

    device = lax.axis_index("chan")
    own = over_periods(1 - odd, pl.ds(0, BINS))
    beside = over_periods(odd, pl.ds(pl.multiple_of((1 - odd) * HALF, HALF), HALF))
    beside = jnp.where((device > 0) & (device < lax.axis_size("chan") - 1), beside, 0.0)
    held[...] = jnp.zeros_like(held)
    held[:HALF] = own[:HALF] + jnp.where(odd == 1, 0.0, beside)
    held[HALF:BINS] = own[HALF:] + jnp.where(odd == 1, beside, 0.0)
    count = place_ref[1]
    first = jnp.where(count > 0, place_ref[0], 0)
    for slot in range(CAP):
        rows = held[pl.ds(pl.multiple_of((first + slot) * NOFF, 8), NOFF), :]
        rows = jnp.where(slot < count, rows, 0.0)
        real = jnp.zeros((NP, NF), jnp.float32)
        imag = jnp.zeros((NP, NF), jnp.float32)
        for offset in range(NOFF):
            bin_real = rows[offset : offset + 1, :NF]
            bin_imag = rows[offset : offset + 1, NF:]
            cos, sin = slant_ref[0, offset], slant_ref[1, offset]
            real = real + (bin_real * cos + bin_imag * sin)
            imag = imag + (bin_imag * cos - bin_real * sin)
        spec[slot * NP : (slot + 1) * NP, :NF] = real
        spec[slot * NP : (slot + 1) * NP, NF:] = imag
    whole = spec[...]
    high = whole.astype(jnp.bfloat16)
    low = (whole - high.astype(jnp.float32)).astype(jnp.bfloat16)
    traces = jnp.dot(
        jnp.concatenate([high, low, high], axis=1), lags_ref[...], preferred_element_type=jnp.float32
    )
    power = jnp.mean(traces * traces, axis=-1, keepdims=True)
    out_ref[...] = traces / jnp.sqrt(power + 1e-06)


def shards(raw_strain, bin_ids, owner_map):
    count = lax.axis_size("chan")
    periods = lax.axis_size("period")
    smem = pl.BlockSpec(memory_space=pltpu.SMEM)
    vmem = pl.BlockSpec(memory_space=pltpu.VMEM)
    partners = [(i, i + 1) for i in range(0, count, 2)]
    partners = partners + [(j, i) for i, j in partners]
    packed = call(pack_kernel, jax.ShapeDtypeStruct((count, 16, 128), jnp.bfloat16))(raw_strain[0])
    packed, bin_ids, owner_map = lax.optimization_barrier((packed, bin_ids, owner_map))
    series = lax.all_to_all(packed, "chan", 0, 0, tiled=True)
    masks, place = call(
        mask_kernel,
        (
            jax.ShapeDtypeStruct((2, BINS * CH_DEV, 3 * CH_DEV), jnp.bfloat16),
            jax.ShapeDtypeStruct((2,), jnp.int32),
        ),
        flops=2000000000,
        out_specs=(vmem, smem),
    )(bin_ids, lax.ppermute(bin_ids, "chan", partners), owner_map.reshape(2, 128))
    series, masks, place = lax.optimization_barrier((series, masks, place))
    held = jax.ShapeDtypeStruct((PART, 2 * CH_DEV, 2 * NF), jnp.bfloat16)
    kept, gave = call(spectra_kernel, (held, held))(
        series.reshape(NWIN, WIN, 128), jnp.asarray(dft_rows(), jnp.bfloat16)
    )
    came = lax.ppermute(gave, "chan", partners)
    spectra, gave = call(
        give_kernel,
        (
            jax.ShapeDtypeStruct((PART, 4 * CH_DEV, 2 * NF), jnp.bfloat16),
            jax.ShapeDtypeStruct((BINS, 2 * NF), jnp.float32),
        ),
    )(masks, kept, came)
    came = lax.ppermute(gave, "chan", partners)
    edge = call(keep_kernel, jax.ShapeDtypeStruct((HALF, 2 * NF), jnp.float32), flops=1000000000)(
        masks, spectra
    )
    merged = call(merge_kernel, jax.ShapeDtypeStruct((8, BINS, 2 * NF), jnp.bfloat16))(gave, came, edge)
    groups = [
        [at % count * periods + p for at in (i + 1, i + 2) for p in range(periods)]
        for i in range(0, count, 2)
    ]
    sums = lax.all_to_all(
        merged, ("chan", "period"), 0, 0, tiled=True, axis_index_groups=groups
    )
    stacks = call(
        stack_kernel,
        jax.ShapeDtypeStruct((CAP * NP, WIN), jnp.float32),
        in_specs=[smem, vmem, vmem, vmem],
        scratch_shapes=[
            pltpu.VMEM((2 * BINS, 2 * NF), jnp.float32),
            pltpu.VMEM((CAP * NP, 2 * NF), jnp.float32),
        ],
    )(place, sums, jnp.asarray(slant_tables()), jnp.asarray(lag_parts()))
    return stacks.reshape(CAP, NP, WIN)


def solution(mesh):
    placed = (P("period", "chan", None), P(None, "chan", None), P())
    return jax.shard_map(
        shards, mesh=mesh, in_specs=placed, out_specs=P("chan", None, None), check_vma=False
    )
```

time: 66.8 us -> 64.4 us (0.964)
  the two profiles are of different devices: /device:TPU:8 before, /device:TPU:2 now
where the time goes in v6:
time: 64.4 us; the launch traced here: 64 us
  starting transfers between devices  23.8 us (37%)
  waiting for transfers between devices  18.1 us (28%)
  blocking collectives  12.7 us (20%)
  Pallas kernels  6.69 us (10%)
  local copies, waits for them, and re-layouts  2.54 us (4%)
    all_to_all x1, starting transfers between devices, shards(): series = lax.all_to_all(packed, 'chan', 0, 0, tiled=True)  17.8 us
    all_to_all x1, waiting for transfers between devices, shards(): series = lax.all_to_all(packed, 'chan', 0, 0, tiled=True)  14.9 us
    all_to_all x1, blocking collectives, shards(): lax.all_to_all(merged, ('chan', 'period'), 0, 0, tiled=True, axis_index_g...  12.7 us
    ppermute x2, starting transfers between devices, shards(): came = lax.ppermute(gave, 'chan', partners)  4.1 us
    unnamed x12, local copies, waits for them, and re-layouts  2.54 us
    pallas_call x1, Pallas kernels, shards(): call(give_kernel, (jax.ShapeDtypeStruct((PART, 4 * CH_DEV, 2 * NF), jnp.b...  2.1 us
    ppermute x1, starting transfers between devices, shards(): lax.ppermute(bin_ids, 'chan', partners)  1.92 us
    ppermute x2, waiting for transfers between devices, shards(): came = lax.ppermute(gave, 'chan', partners)  1.77 us
  transfers between devices with their start and end apart: 4, of which 4 were waited for; matrix products, arithmetic and copies ran while one was open for 0% of the time, Pallas kernels for 2%

profile of v6, /device:TPU:2, one launch (start us, length us, event | category | flops | bytes accessed | tf_op | source)
XLA Modules:
  0.0 64.0 jit_solution(16145340920840791557)
XLA Ops:
  0.0 0.0 copy-start.1
  0.0 0.9 %copy-done.1 = bf16[1,16,8192]{2,1,0:T(8,128)(2,1)S(1)} copy-done((bf16[1,16,8192]{2,1,0:T(8,128)(2,1)S(1)}, bf16[1,16,8192]{2,1,0:T(8,128)(2,1)}, u32[]{:S(2)}) %copy-start.1) | copy-done | bytes 262168
  1.0 0.9 %shard_map.64 = bf16[128,16,128]{2,1,0:T(8,128)(2,1)} custom-call(bf16[16,8192]{1,0:T(8,128)(2,1)S(1)} %bitcast.5), custom_call_target="tpu_custom_call" | custom-call | tf_op jit(solution)/shard_map/pallas_call | solution.py:210
  1.8 17.8 %all-to-all-start = ((bf16[128,16,128]{2,1,0:T(8,128)(2,1)}), bf16[128,16,128]{2,1,0:T(8,128)(2,1)S(1)}, u32[]{:S(2)}, u32[]{:S(2)}) async-start(bf16[128,16,128]{2,1,0:T(8,128)(2,1)} %shard_map.64), calls=%async_computation | async-start | bytes 1048576 | tf_op jit(solution)/shard_map/all_to_all | solution.py:212
  19.6 1.9 %collective-permute-start = (s32[3,64,64]{2,1,0:T(8,128)}, s32[3,64,64]{2,1,0:T(8,128)S(1)}, u32[]{:S(2)}, u32[]{:S(2)}) collective-permute-start(s32[3,64,64]{2,1,0:T(8,128)} %ids_ref), channel_id=1, source_target_pairs={{0,4},{8,12},{16,20},{24,28},{32,36},{40,44},{48,52},{56,60},{64,6... | collective-permute-start | bytes 147464 | tf_op jit(solution)/shard_map/ppermute | solution.py:221
  21.6 1.5 %collective-permute-done.other_ref = s32[3,64,64]{2,1,0:T(8,128)S(1)} collective-permute-done((s32[3,64,64]{2,1,0:T(8,128)}, s32[3,64,64]{2,1,0:T(8,128)S(1)}, u32[]{:S(2)}, u32[]{:S(2)}) %collective-permute-start) | collective-permute-done | bytes 49184 | tf_op jit(solution)/shard_map/ppermute | solution.py:221
  23.0 0.9 %copy-done.4 = s32[3,64,64]{2,1,0:T(8,128)S(1)} copy-done((s32[3,64,64]{2,1,0:T(8,128)S(1)}, s32[3,64,64]{2,1,0:T(8,128)}, u32[]{:S(2)}) %copy-start.4) | copy-done | bytes 49176
  23.9 0.7 %copy-done.5 = s32[256]{0:T(256)S(1)} copy-done((s32[256]{0:T(256)S(1)}, s32[256]{0:T(256)}, u32[]{:S(2)}) %copy-start.5) | copy-done | bytes 1048
  24.6 0.8 %shard_map.65 = (bf16[2,2048,192]{2,1,0:T(8,128)(2,1)S(1)}, s32[2]{0:T(128)S(1)}) custom-call(s32[3,64,64]{2,1,0:T(8,128)S(1)} %copy-done.4, s32[3,64,64]{2,1,0:T(8,128)S(1)} %collective-permute-done.other_ref, s32[2,128]{1,0:T(2,128)S(1)} %bitcast.6), custom_call_target="tpu_custom_call" | custom-call | flops 2000000000 | bytes 7812500 | tf_op jit(solution)/shard_map/pallas_call | solution.py:213
  25.4 14.9 %all-to-all-done = bf16[128,16,128]{2,1,0:T(8,128)(2,1)S(1)} async-done(((bf16[128,16,128]{2,1,0:T(8,128)(2,1)}), bf16[128,16,128]{2,1,0:T(8,128)(2,1)S(1)}, u32[]{:S(2)}, u32[]{:S(2)}) %all-to-all-start) | async-done | bytes 524320 | tf_op jit(solution)/shard_map/all_to_all | solution.py:212
  40.3 0.0 copy-done.3
  40.3 0.5 shard_map.66
  40.8 1.9 %collective-permute-start.1 = (bf16[4,128,256]{2,1,0:T(8,128)(2,1)S(1)}, bf16[4,128,256]{2,1,0:T(8,128)(2,1)S(1)}, u32[]{:S(2)}, u32[]{:S(2)}) collective-permute-start(bf16[4,128,256]{2,1,0:T(8,128)(2,1)S(1)} %get-tuple-element.26), channel_id=1, source_target_pairs={{0,4},{8,12},{16,20},{24,28},{32,36},{40,44},{48,52},{56,60},{64,6... | collective-permute-start | bytes 786440 | tf_op jit(solution)/shard_map/ppermute | solution.py:227
  42.7 1.5 %collective-permute-done.1.came_ref = bf16[4,128,256]{2,1,0:T(8,128)(2,1)S(1)} collective-permute-done((bf16[4,128,256]{2,1,0:T(8,128)(2,1)S(1)}, bf16[4,128,256]{2,1,0:T(8,128)(2,1)S(1)}, u32[]{:S(2)}, u32[]{:S(2)}) %collective-permute-start.1) | collective-permute-done | bytes 262176 | tf_op jit(solution)/shard_map/ppermute | solution.py:227
  44.2 2.1 %shard_map.67 = (bf16[4,256,256]{2,1,0:T(8,128)(2,1)S(1)}, f32[32,256]{1,0:T(8,128)S(1)}) custom-call(bf16[2,2048,192]{2,1,0:T(8,128)(2,1)S(1)} %get-tuple-element.23.masks_ref, bf16[4,128,256]{2,1,0:T(8,128)(2,1)S(1)} %get-tuple-element.25.kept_ref, bf16[4,128,256]{2,1,0:T(8,128)(2,1)S(1)} %collective-permute-done.1.came_ref), custom_call_target="tpu_custom_call" | custom-call | tf_op jit(solution)/shard_map/pallas_call | solution.py:228
  46.3 0.0 copy-start
  46.4 0.0 copy-start.2
  46.4 2.2 %collective-permute-start.2 = (f32[32,256]{1,0:T(8,128)S(1)}, f32[32,256]{1,0:T(8,128)S(1)}, u32[]{:S(2)}, u32[]{:S(2)}) collective-permute-start(f32[32,256]{1,0:T(8,128)S(1)} %get-tuple-element.27.gave_ref), channel_id=1, source_target_pairs={{0,4},{8,12},{16,20},{24,28},{32,36},{40,44},{48,52},{56,60},{64,6... | collective-permute-start | bytes 98312 | tf_op jit(solution)/shard_map/ppermute | solution.py:235
  48.6 0.8 %shard_map.68.edge_ref = f32[16,256]{1,0:T(8,128)S(1)} custom-call(bf16[2,2048,192]{2,1,0:T(8,128)(2,1)S(1)} %get-tuple-element.23.masks_ref, bf16[4,256,256]{2,1,0:T(8,128)(2,1)S(1)} %get-tuple-element.28.spectra_ref), custom_call_target="tpu_custom_call" | custom-call | flops 1000000000 | bytes 3906250 | tf_op jit(solution)/shard_map/pallas_call | solution.py:236
  49.3 0.3 collective-permute-done.2.came_ref
  49.6 12.7 %all_to_all.10.sums_ref = bf16[8,32,256]{2,1,0:T(8,128)(2,1)S(1)} all-to-all(bf16[8,32,256]{2,1,0:T(8,128)(2,1)S(1)} %shard_map.69), channel_id=1, replica_groups={{4,5,6,7,8,9,10,11},{12,13,14,15,16,17,18,19},{20,21,22,23,24,25,26,27}..., dimensions={0} | all-to-all | bytes 262144 | tf_op jit(solution)/shard_map/all_to_all | solution.py:244
  62.4 0.0 copy-done
  62.4 0.0 copy-done.2
  62.4 1.6 %shard_map.70 = f32[128,256]{1,0:T(8,128)} custom-call(s32[2]{0:T(128)S(1)} %get-tuple-element.22.place_ref, bf16[8,32,256]{2,1,0:T(8,128)(2,1)S(1)} %all_to_all.10.sums_ref, f32[2,8,32,128]{3,2,1,0:T(8,128)S(1)} %copy-done.2, bf16[768,256]{1,0:T(8,128)(2,1)S(1)} %copy-done), custom_call_target="tpu_custom_call" | custom-call | tf_op jit(solution)/shard_map/pallas_call | solution.py:247
  (4 shorter events, 0.0 us)
Async XLA Ops:
  0.0 0.9 %copy-start.1 = (bf16[1,16,8192]{2,1,0:T(8,128)(2,1)S(1)}, bf16[1,16,8192]{2,1,0:T(8,128)(2,1)}, u32[]{:S(2)}) copy-start(bf16[1,16,8192]{2,1,0:T(8,128)(2,1)} %param.6) | copy-start | bytes 786436
  1.8 38.5 %all-to-all-start = ((bf16[128,16,128]{2,1,0:T(8,128)(2,1)}), bf16[128,16,128]{2,1,0:T(8,128)(2,1)S(1)}, u32[]{:S(2)}, u32[]{:S(2)}) async-start(bf16[128,16,128]{2,1,0:T(8,128)(2,1)} %shard_map.64), calls=%async_computation | async-start | bytes 1048576 | tf_op jit(solution)/shard_map/all_to_all | solution.py:212
  19.6 3.4 %collective-permute-start = (s32[3,64,64]{2,1,0:T(8,128)}, s32[3,64,64]{2,1,0:T(8,128)S(1)}, u32[]{:S(2)}, u32[]{:S(2)}) collective-permute-start(s32[3,64,64]{2,1,0:T(8,128)} %ids_ref), channel_id=1, source_target_pairs={{0,4},{8,12},{16,20},{24,28},{32,36},{40,44},{48,52},{56,60},{64,6... | collective-permute-start | bytes 147464 | tf_op jit(solution)/shard_map/ppermute | solution.py:221
  23.0 0.9 %copy-start.4 = (s32[3,64,64]{2,1,0:T(8,128)S(1)}, s32[3,64,64]{2,1,0:T(8,128)}, u32[]{:S(2)}) copy-start(s32[3,64,64]{2,1,0:T(8,128)} %ids_ref) | copy-start | bytes 147460
  23.9 0.7 %copy-start.5 = (s32[256]{0:T(256)S(1)}, s32[256]{0:T(256)}, u32[]{:S(2)}) copy-start(s32[256]{0:T(256)} %param.8) | copy-start | bytes 3076
  24.6 15.7 %copy-start.3 = (bf16[256,256]{1,0:T(8,128)(2,1)S(1)}, bf16[256,256]{1,0:T(8,128)(2,1)}, u32[]{:S(2)}) copy-start(bf16[256,256]{1,0:T(8,128)(2,1)} %constant.6.clone.table_ref) | copy-start | bytes 393220
  40.8 3.4 %collective-permute-start.1 = (bf16[4,128,256]{2,1,0:T(8,128)(2,1)S(1)}, bf16[4,128,256]{2,1,0:T(8,128)(2,1)S(1)}, u32[]{:S(2)}, u32[]{:S(2)}) collective-permute-start(bf16[4,128,256]{2,1,0:T(8,128)(2,1)S(1)} %get-tuple-element.26), channel_id=1, source_target_pairs={{0,4},{8,12},{16,20},{24,28},{32,36},{40,44},{48,52},{56,60},{64,6... | collective-permute-start | bytes 786440 | tf_op jit(solution)/shard_map/ppermute | solution.py:227
  46.3 16.0 %copy-start = (bf16[768,256]{1,0:T(8,128)(2,1)S(1)}, bf16[768,256]{1,0:T(8,128)(2,1)}, u32[]{:S(2)}) copy-start(bf16[768,256]{1,0:T(8,128)(2,1)} %constant.8.clone.lags_ref) | copy-start | bytes 1179652
  46.4 16.0 %copy-start.2 = (f32[2,8,32,128]{3,2,1,0:T(8,128)S(1)}, f32[2,8,32,128]{3,2,1,0:T(8,128)}, u32[]{:S(2)}) copy-start(f32[2,8,32,128]{3,2,1,0:T(8,128)} %constant.7.clone.slant_ref) | copy-start | bytes 786436
  46.4 3.2 %collective-permute-start.2 = (f32[32,256]{1,0:T(8,128)S(1)}, f32[32,256]{1,0:T(8,128)S(1)}, u32[]{:S(2)}, u32[]{:S(2)}) collective-permute-start(f32[32,256]{1,0:T(8,128)S(1)} %get-tuple-element.27.gave_ref), channel_id=1, source_target_pairs={{0,4},{8,12},{16,20},{24,28},{32,36},{40,44},{48,52},{56,60},{64,6... | collective-permute-start | bytes 98312 | tf_op jit(solution)/shard_map/ppermute | solution.py:235

commit v7 on v2

--- a/solution.py
+++ b/solution.py
@@ -21,13 +21,8 @@
 HALF = BINS // 2
 VMEM_LIMIT = 48 * 1024 * 1024
 
-ROW_SAMPLE = (
-    16 * np.arange(16)[None, :, None] + 8 * np.arange(2)[:, None, None] + np.arange(8)[None, None, :]
-).reshape(-1)
-
-
 def dft_rows():
-    phase = 2.0 * math.pi / WIN * np.mod(ROW_SAMPLE[:, None] * np.arange(1, NF + 1)[None, :], WIN)
+    phase = 2.0 * math.pi / WIN * np.mod(np.arange(WIN)[:, None] * np.arange(1, NF + 1)[None, :], WIN)
     return np.concatenate([np.cos(phase), -np.sin(phase)], axis=1).astype(np.float32)
 
 
@@ -62,48 +57,48 @@
 
 
 def pack_kernel(raw_ref, out_ref):
-    low = lax.broadcasted_iota(jnp.int32, (8, 128), 1) < 64
-    for tile in range(raw_ref.shape[1] // 128):
-        both = raw_ref[:, 128 * tile : 128 * tile + 128].astype(jnp.float32)
-        first, second = both[:8], both[8:]
-        even = jnp.where(low, first, pltpu.roll(second, 64, 1))
-        odd = jnp.where(low, pltpu.roll(first, 64, 1), second)
-        out_ref[tile] = jnp.concatenate([even, odd], axis=0).astype(jnp.bfloat16)
-
-
-def mask_kernel(ids_ref, masks_ref):
-    ids = jnp.concatenate([ids_ref[0], ids_ref[1], ids_ref[2]], axis=1)
+    out_ref[0] = jnp.zeros((16, 128), jnp.bfloat16)
+    for chip in range(raw_ref.shape[1] // 128):
+        tile = raw_ref[:, 128 * chip : 128 * chip + 128]
+        out_ref[2 * chip + 1] = tile
+        if 2 * chip + 2 < out_ref.shape[0]:
+            out_ref[2 * chip + 2] = tile
+
+
+def mask_kernel(ids_ref, owner_ref, masks_ref, place_ref):
+    ids = jnp.concatenate([ids_ref[2], ids_ref[1], ids_ref[0]], axis=1)
     for bin_at in range(BINS):
         masks_ref[bin_at * CH_DEV : (bin_at + 1) * CH_DEV, :] = (
             (ids == bin_at).astype(jnp.float32).astype(jnp.bfloat16)
         )
-
-
-def place_kernel(owner_ref, place_ref):
     device = lax.axis_index("chan")
     owner = owner_ref[...]
     place_ref[0] = jnp.sum((owner < device).astype(jnp.int32)) - MB_DEV * (device - 1)
     place_ref[1] = jnp.sum((owner == device).astype(jnp.int32))
 
 
-def spectra_kernel(series_ref, table_ref, out_ref):
+def spectra_kernel(series_ref, table_ref, pair_ref, give_ref):
     table = table_ref[...]
+    odd = lax.rem(lax.axis_index("chan"), 2) == 1
     for window in range(NWIN):
-        turned = series_ref[window].astype(jnp.float32).T.astype(jnp.bfloat16)
-        series = jnp.concatenate([turned[:CH_DEV], turned[CH_DEV:]], axis=1)
-        spectra = jnp.dot(series, table, preferred_element_type=jnp.float32)
+        spectra = jnp.dot(series_ref[window].T, table, preferred_element_type=jnp.float32)
         power = jnp.mean(spectra * spectra, axis=-1, keepdims=True)
-        out_ref[window] = (spectra / jnp.sqrt(power + 1e-06)).astype(jnp.bfloat16)
-
-
-def bin_kernel(across, masks_ref, own_ref, near_ref, far_ref, out_ref):
+        whitened = (spectra / jnp.sqrt(power + 1e-06)).astype(jnp.bfloat16)
+        pair_ref[window] = whitened
+        give_ref[window] = jnp.where(odd, whitened[:CH_DEV], whitened[CH_DEV:])
+
+
+def bin_kernel(across, masks_ref, pair_ref, came_ref, out_ref):
     odd = lax.rem(lax.axis_index("chan"), 2)
     part = odd if across else 1 - odd
     rows = pl.ds(pl.multiple_of(part * HALF * CH_DEV, HALF * CH_DEV), HALF * CH_DEV)
     totals = None
     for window in range(NWIN):
-        own = own_ref[window]
-        partners = jnp.concatenate([own, near_ref[window], far_ref[window]], axis=0)
+        low, high, came = pair_ref[window, :CH_DEV], pair_ref[window, CH_DEV:], came_ref[window]
+        own = jnp.where(odd == 1, high, came)
+        partners = jnp.concatenate(
+            [jnp.where(odd == 1, came, low), jnp.where(odd == 1, low, high), own], axis=0
+        )
         own = own.astype(jnp.float32)
         own_real, own_imag = own[:, :NF], own[:, NF:]
         picked = jnp.dot(masks_ref[rows, :], partners, preferred_element_type=jnp.float32)
@@ -176,26 +171,31 @@
     periods = lax.axis_size("period")
     smem = pl.BlockSpec(memory_space=pltpu.SMEM)
     vmem = pl.BlockSpec(memory_space=pltpu.VMEM)
-    packed = call(pack_kernel, jax.ShapeDtypeStruct((count // 2, 16, 128), jnp.bfloat16))(raw_strain[0])
-    series = lax.all_to_all(packed.reshape(count, 8, 128), "chan", 0, 0, tiled=True)
-    masks = call(
+    packed = call(pack_kernel, jax.ShapeDtypeStruct((count, 16, 128), jnp.bfloat16))(raw_strain[0])
+    series = lax.all_to_all(packed, "chan", 0, 0, tiled=True)
+    masks, place = call(
         mask_kernel,
-        jax.ShapeDtypeStruct((BINS * CH_DEV, 3 * CH_DEV), jnp.bfloat16),
+        (
+            jax.ShapeDtypeStruct((BINS * CH_DEV, 3 * CH_DEV), jnp.bfloat16),
+            jax.ShapeDtypeStruct((2,), jnp.int32),
+        ),
         flops=2000000000,
-    )(bin_ids)
-    own = call(spectra_kernel, jax.ShapeDtypeStruct((NWIN, CH_DEV, 2 * NF), jnp.bfloat16))(
-        series.reshape(NWIN, 128, 128), jnp.asarray(dft_rows(), jnp.bfloat16)
-    )
-    near = lax.ppermute(own, "chan", [(i, i + 1) for i in range(count - 1)])
-    far = lax.ppermute(own, "chan", [(i, i + 2) for i in range(count - 2)])
-    place = call(place_kernel, jax.ShapeDtypeStruct((2,), jnp.int32), out_specs=smem)(
-        owner_map.reshape(2, 128)
-    )
+        out_specs=(vmem, smem),
+    )(bin_ids, owner_map.reshape(2, 128))
+    pair, gave = call(
+        spectra_kernel,
+        (
+            jax.ShapeDtypeStruct((NWIN, 2 * CH_DEV, 2 * NF), jnp.bfloat16),
+            jax.ShapeDtypeStruct((NWIN, CH_DEV, 2 * NF), jnp.bfloat16),
+        ),
+    )(series.reshape(NWIN, WIN, 128), jnp.asarray(dft_rows(), jnp.bfloat16))
+    cores = [(i, i + 1) for i in range(0, count, 2)]
+    came = lax.ppermute(gave, "chan", cores + [(j, i) for i, j in cores])
     part = jax.ShapeDtypeStruct((HALF, 2 * NF), jnp.float32)
-    across = call(functools.partial(bin_kernel, True), part)(masks, own, near, far)
+    across = call(functools.partial(bin_kernel, True), part)(masks, pair, came)
     pairs = [(2 * k + 1, 2 * k + 2) for k in range(count // 2 - 1)]
     arrived = lax.ppermute(across, "chan", pairs + [(j, i) for i, j in pairs])
-    inside = call(functools.partial(bin_kernel, False), part, flops=2000000000)(masks, own, near, far)
+    inside = call(functools.partial(bin_kernel, False), part, flops=2000000000)(masks, pair, came)
     merged = call(merge_kernel, jax.ShapeDtypeStruct((8, BINS, 2 * NF), jnp.bfloat16))(
         across, inside, arrived
     )

time: 69.1 us -> 63 us (0.912)
  blocking collectives: 32.1 us -> 47.3 us
  waiting for transfers between devices: 17.6 us -> 4.58 us
  starting transfers between devices: 10.6 us -> 3.84 us
  Pallas kernels: 6.44 us -> 5.74 us
    all_to_all x1 -> x2, blocking collectives: 32.1 us -> 47.3 us  [the longest x1 37.6 us: shards(): series = lax.all_to_all(packed, 'chan', 0, 0, tiled=True)]
    ppermute x2 -> x1, waiting for transfers between devices: 9.57 us -> 0.74 us  [shards(): came = lax.ppermute(gave, 'chan', cores + [(j, i) for i, j in cores])]
    all_to_all x1 -> x0, starting transfers between devices: 4.3 us -> none  [shards(): lax.all_to_all(merged, ('chan', 'period'), 0, 0, tiled=True, axis_index_g...]
    all_to_all x1 -> x0, waiting for transfers between devices: 4.15 us -> none  [shards(): lax.all_to_all(merged, ('chan', 'period'), 0, 0, tiled=True, axis_index_g...]
    ppermute x2 -> x1, starting transfers between devices: 4.41 us -> 1.92 us  [shards(): came = lax.ppermute(gave, 'chan', cores + [(j, i) for i, j in cores])]
    pallas_call x5 -> x4, Pallas kernels: 2.83 us -> 2.72 us  [the longest x1 1.37 us: shards(): across = call(functools.partial(bin_kernel, True), part)(masks, pair, came)]
  transfers between devices with their start and end apart: 4 -> 2, of which waited for: 4 -> 2; matrix products, arithmetic and copies ran while one was open for 0% -> 0% of each run, Pallas kernels for 3% -> 3%
where the time goes in v7:
time: 63 us; the launch traced here: 62.5 us
  blocking collectives  47.3 us (75%)
  Pallas kernels  5.74 us (9%)
  waiting for transfers between devices  4.58 us (7%)
  starting transfers between devices  3.84 us (6%)
  local copies, waits for them, and re-layouts  0.98 us (2%)
    all_to_all x1, blocking collectives, shards(): series = lax.all_to_all(packed, 'chan', 0, 0, tiled=True)  37.6 us
    all_to_all x1, blocking collectives, shards(): lax.all_to_all(merged, ('chan', 'period'), 0, 0, tiled=True, axis_index_g...  9.66 us
    ppermute x1, waiting for transfers between devices, shards(): arrived = lax.ppermute(across, 'chan', pairs + [(j, i) for i, j in pairs])  3.84 us
    ppermute x1, starting transfers between devices, shards(): came = lax.ppermute(gave, 'chan', cores + [(j, i) for i, j in cores])  1.92 us
    ppermute x1, starting transfers between devices, shards(): arrived = lax.ppermute(across, 'chan', pairs + [(j, i) for i, j in pairs])  1.92 us
    pallas_call x1, Pallas kernels, shards(): call(stack_kernel, jax.ShapeDtypeStruct((CAP * NP, WIN), jnp.float32), in...  1.63 us
    pallas_call x1, Pallas kernels, shards(): call(functools.partial(bin_kernel, False), part, flops=2000000000)  1.37 us
    pallas_call x1, Pallas kernels, shards(): across = call(functools.partial(bin_kernel, True), part)(masks, pair, came)  1.37 us
  transfers between devices with their start and end apart: 2, of which 2 were waited for; matrix products, arithmetic and copies ran while one was open for 0% of the time, Pallas kernels for 3%

profile of v7, /device:TPU:8, one launch (start us, length us, event | category | flops | bytes accessed | tf_op | source)
XLA Modules:
  0.0 62.5 jit_solution(1209654612144885654)
XLA Ops:
  0.0 0.0 copy-start.1
  0.0 0.9 %copy-done.1 = bf16[1,16,8192]{2,1,0:T(8,128)(2,1)S(1)} copy-done((bf16[1,16,8192]{2,1,0:T(8,128)(2,1)S(1)}, bf16[1,16,8192]{2,1,0:T(8,128)(2,1)}, u32[]{:S(2)}) %copy-start.1) | copy-done | bytes 262168
  1.0 0.1 shard_map.65
  1.0 0.0 copy-start.3
  1.0 37.6 %all_to_all.10 = bf16[128,16,128]{2,1,0:T(8,128)(2,1)S(1)} all-to-all(bf16[128,16,128]{2,1,0:T(8,128)(2,1)S(1)} %shard_map.65), channel_id=1, replica_groups=mesh['chan'=128,'period'=4] {'chan'}, dimensions={0} | all-to-all | bytes 1048576 | tf_op jit(solution)/shard_map/all_to_all | solution.py:175
  38.6 0.0 copy-done.3
  38.6 0.0 copy-start.4
  38.7 0.6 shard_map.66
  39.2 0.0 copy-start.5
  39.2 1.9 %collective-permute-start = (bf16[8,64,256]{2,1,0:T(8,128)(2,1)S(1)}, bf16[8,64,256]{2,1,0:T(8,128)(2,1)S(1)}, u32[]{:S(2)}, u32[]{:S(2)}) collective-permute-start(bf16[8,64,256]{2,1,0:T(8,128)(2,1)S(1)} %get-tuple-element.12), channel_id=1, source_target_pairs={{0,4},{8,12},{16,20},{24,28},{32,36},{40,44},{48,52},{56,60},{64,6... | collective-permute-start | bytes 786440 | tf_op jit(solution)/shard_map/ppermute | solution.py:193
  41.2 0.0 copy-done.4
  41.2 0.0 copy-done.5
  41.2 0.7 %shard_map.64 = (bf16[2048,192]{1,0:T(8,128)(2,1)S(1)}, s32[2]{0:T(128)S(1)}) custom-call(s32[3,64,64]{2,1,0:T(8,128)S(1)} %copy-done.4, s32[2,128]{1,0:T(2,128)S(1)} %bitcast.6), custom_call_target="tpu_custom_call" | custom-call | flops 2000000000 | bytes 7812500 | tf_op jit(solution)/shard_map/pallas_call | solution.py:176
  41.9 0.7 %collective-permute-done.came_ref = bf16[8,64,256]{2,1,0:T(8,128)(2,1)S(1)} collective-permute-done((bf16[8,64,256]{2,1,0:T(8,128)(2,1)S(1)}, bf16[8,64,256]{2,1,0:T(8,128)(2,1)S(1)}, u32[]{:S(2)}, u32[]{:S(2)}) %collective-permute-start) | collective-permute-done | bytes 262176 | tf_op jit(solution)/shard_map/ppermute | solution.py:193
  42.7 1.4 %shard_map.67.across_ref = f32[16,256]{1,0:T(8,128)S(1)} custom-call(bf16[2048,192]{1,0:T(8,128)(2,1)S(1)} %get-tuple-element.10.masks_ref, bf16[8,128,256]{2,1,0:T(8,128)(2,1)S(1)} %get-tuple-element.11.pair_ref, bf16[8,64,256]{2,1,0:T(8,128)(2,1)S(1)} %collective-permute-done.came_ref), custom_call_target="tpu_custom_call" | custom-call | tf_op jit(solution)/shard_map/pallas_call | solution.py:195
  44.0 1.9 %collective-permute-start.1 = (f32[16,256]{1,0:T(8,128)S(1)}, f32[16,256]{1,0:T(8,128)S(1)}, u32[]{:S(2)}, u32[]{:S(2)}) collective-permute-start(f32[16,256]{1,0:T(8,128)S(1)} %shard_map.67.across_ref), channel_id=1, source_target_pairs={{4,8},{12,16},{20,24},{28,32},{36,40},{44,48},{52,56},{60,64},{68,... | collective-permute-start | bytes 49160 | tf_op jit(solution)/shard_map/ppermute | solution.py:197
  46.0 0.0 copy-start.2
  46.0 1.4 %shard_map.68.inside_ref = f32[16,256]{1,0:T(8,128)S(1)} custom-call(bf16[2048,192]{1,0:T(8,128)(2,1)S(1)} %get-tuple-element.10.masks_ref, bf16[8,128,256]{2,1,0:T(8,128)(2,1)S(1)} %get-tuple-element.11.pair_ref, bf16[8,64,256]{2,1,0:T(8,128)(2,1)S(1)} %collective-permute-done.came_ref), custom_call_target="tpu_custom_call" | custom-call | flops 2000000000 | bytes 7812500 | tf_op jit(solution)/shard_map/pallas_call | solution.py:198
  47.3 0.0 copy-start
  47.4 3.8 %collective-permute-done.1.arrived_ref = f32[16,256]{1,0:T(8,128)S(1)} collective-permute-done((f32[16,256]{1,0:T(8,128)S(1)}, f32[16,256]{1,0:T(8,128)S(1)}, u32[]{:S(2)}, u32[]{:S(2)}) %collective-permute-start.1) | collective-permute-done | bytes 16416 | tf_op jit(solution)/shard_map/ppermute | solution.py:197
  51.2 9.7 %all_to_all.11.sums_ref = bf16[8,32,256]{2,1,0:T(8,128)(2,1)S(1)} all-to-all(bf16[8,32,256]{2,1,0:T(8,128)(2,1)S(1)} %shard_map.69), channel_id=1, replica_groups={{0,1,2,3,4,5,6,7},{8,9,10,11,12,13,14,15},{16,17,18,19,20,21,22,23},{24..., dimensions={0} | all-to-all | bytes 262144 | tf_op jit(solution)/shard_map/all_to_all | solution.py:206
  60.9 0.0 copy-done.2
  60.9 0.0 copy-done
  60.9 1.6 %shard_map.70 = f32[128,256]{1,0:T(8,128)} custom-call(s32[2]{0:T(128)S(1)} %get-tuple-element.9.place_ref, bf16[8,32,256]{2,1,0:T(8,128)(2,1)S(1)} %all_to_all.11.sums_ref, f32[2,8,32,128]{3,2,1,0:T(8,128)S(1)} %copy-done.2, bf16[768,256]{1,0:T(8,128)(2,1)S(1)} %copy-done), custom_call_target="tpu_custom_call" | custom-call | tf_op jit(solution)/shard_map/pallas_call | solution.py:209
  (1 shorter events, 0.0 us)
Async XLA Ops:
  0.0 0.9 %copy-start.1 = (bf16[1,16,8192]{2,1,0:T(8,128)(2,1)S(1)}, bf16[1,16,8192]{2,1,0:T(8,128)(2,1)}, u32[]{:S(2)}) copy-start(bf16[1,16,8192]{2,1,0:T(8,128)(2,1)} %param.6) | copy-start | bytes 786436
  1.0 37.6 %copy-start.3 = (bf16[256,256]{1,0:T(8,128)(2,1)S(1)}, bf16[256,256]{1,0:T(8,128)(2,1)}, u32[]{:S(2)}) copy-start(bf16[256,256]{1,0:T(8,128)(2,1)} %constant.6.clone.table_ref) | copy-start | bytes 393220
  38.6 2.5 %copy-start.4 = (s32[3,64,64]{2,1,0:T(8,128)S(1)}, s32[3,64,64]{2,1,0:T(8,128)}, u32[]{:S(2)}) copy-start(s32[3,64,64]{2,1,0:T(8,128)} %ids_ref.1) | copy-start | bytes 147460
  39.2 2.0 %copy-start.5 = (s32[256]{0:T(256)S(1)}, s32[256]{0:T(256)}, u32[]{:S(2)}) copy-start(s32[256]{0:T(256)} %param.8) | copy-start | bytes 3076
  39.2 3.4 %collective-permute-start = (bf16[8,64,256]{2,1,0:T(8,128)(2,1)S(1)}, bf16[8,64,256]{2,1,0:T(8,128)(2,1)S(1)}, u32[]{:S(2)}, u32[]{:S(2)}) collective-permute-start(bf16[8,64,256]{2,1,0:T(8,128)(2,1)S(1)} %get-tuple-element.12), channel_id=1, source_target_pairs={{0,4},{8,12},{16,20},{24,28},{32,36},{40,44},{48,52},{56,60},{64,6... | collective-permute-start | bytes 786440 | tf_op jit(solution)/shard_map/ppermute | solution.py:193
  44.0 7.2 %collective-permute-start.1 = (f32[16,256]{1,0:T(8,128)S(1)}, f32[16,256]{1,0:T(8,128)S(1)}, u32[]{:S(2)}, u32[]{:S(2)}) collective-permute-start(f32[16,256]{1,0:T(8,128)S(1)} %shard_map.67.across_ref), channel_id=1, source_target_pairs={{4,8},{12,16},{20,24},{28,32},{36,40},{44,48},{52,56},{60,64},{68,... | collective-permute-start | bytes 49160 | tf_op jit(solution)/shard_map/ppermute | solution.py:197
  46.0 14.9 %copy-start.2 = (f32[2,8,32,128]{3,2,1,0:T(8,128)S(1)}, f32[2,8,32,128]{3,2,1,0:T(8,128)}, u32[]{:S(2)}) copy-start(f32[2,8,32,128]{3,2,1,0:T(8,128)} %constant.7.clone.slant_ref) | copy-start | bytes 786436
  47.3 13.5 %copy-start = (bf16[768,256]{1,0:T(8,128)(2,1)S(1)}, bf16[768,256]{1,0:T(8,128)(2,1)}, u32[]{:S(2)}) copy-start(bf16[768,256]{1,0:T(8,128)(2,1)} %constant.8.clone.lags_ref) | copy-start | bytes 1179652

commit v8 on v7

--- a/solution.py
+++ b/solution.py
@@ -22,8 +22,11 @@
 VMEM_LIMIT = 48 * 1024 * 1024
 
 def dft_rows():
-    phase = 2.0 * math.pi / WIN * np.mod(np.arange(WIN)[:, None] * np.arange(1, NF + 1)[None, :], WIN)
-    return np.concatenate([np.cos(phase), -np.sin(phase)], axis=1).astype(np.float32)
+    sample = (
+        32 * np.arange(8)[None, :, None] + 16 * np.arange(2)[:, None, None] + np.arange(16)[None, None, :]
+    ).reshape(2, WIN // 2, 1)
+    phase = 2.0 * math.pi / WIN * np.mod(sample * np.arange(1, NF + 1)[None, None, :], WIN)
+    return np.concatenate([np.cos(phase), -np.sin(phase)], axis=2).astype(np.float32)
 
 
 def lag_table():
@@ -57,12 +60,12 @@
 
 
 def pack_kernel(raw_ref, out_ref):
-    out_ref[0] = jnp.zeros((16, 128), jnp.bfloat16)
-    for chip in range(raw_ref.shape[1] // 128):
+    out_ref[0, 0] = jnp.zeros((16, 128), jnp.bfloat16)
+    for chip in range(out_ref.shape[0]):
         tile = raw_ref[:, 128 * chip : 128 * chip + 128]
-        out_ref[2 * chip + 1] = tile
-        if 2 * chip + 2 < out_ref.shape[0]:
-            out_ref[2 * chip + 2] = tile
+        out_ref[chip, 1] = tile
+        if chip + 1 < out_ref.shape[0]:
+            out_ref[chip + 1, 0] = tile
 
 
 def mask_kernel(ids_ref, owner_ref, masks_ref, place_ref):
@@ -77,28 +80,38 @@
     place_ref[1] = jnp.sum((owner == device).astype(jnp.int32))
 
 
-def spectra_kernel(series_ref, table_ref, pair_ref, give_ref):
-    table = table_ref[...]
-    odd = lax.rem(lax.axis_index("chan"), 2) == 1
+def spectra_kernel(series_ref, came_ref, table_ref, out_ref):
+    core = lax.rem(lax.axis_index("chan"), 2)
+    odd = core == 1
+    table = jnp.concatenate([table_ref[core], table_ref[1 - core]], axis=0)
     for window in range(NWIN):
-        spectra = jnp.dot(series_ref[window].T, table, preferred_element_type=jnp.float32)
+        turned = []
+        for tile in range(2):
+            series = series_ref[window, :, tile].reshape(WIN // 2, 128)
+            came = came_ref[window, :, tile].reshape(WIN // 2, 128)
+            turned.append(jnp.concatenate([series.T, came.T], axis=1))
+        low, high = turned
+        blocks = jnp.concatenate(
+            [
+                jnp.where(odd, low[CH_DEV:], low[:CH_DEV]),
+                jnp.where(odd, high[:CH_DEV], low[CH_DEV:]),
+                jnp.where(odd, high[CH_DEV:], high[:CH_DEV]),
+            ],
+            axis=0,
+        )
+        spectra = jnp.dot(blocks, table, preferred_element_type=jnp.float32)
         power = jnp.mean(spectra * spectra, axis=-1, keepdims=True)
-        whitened = (spectra / jnp.sqrt(power + 1e-06)).astype(jnp.bfloat16)
-        pair_ref[window] = whitened
-        give_ref[window] = jnp.where(odd, whitened[:CH_DEV], whitened[CH_DEV:])
-
-
-def bin_kernel(across, masks_ref, pair_ref, came_ref, out_ref):
+        out_ref[window] = (spectra / jnp.sqrt(power + 1e-06)).astype(jnp.bfloat16)
+
+
+def bin_kernel(across, masks_ref, spectra_ref, out_ref):
     odd = lax.rem(lax.axis_index("chan"), 2)
     part = odd if across else 1 - odd
     rows = pl.ds(pl.multiple_of(part * HALF * CH_DEV, HALF * CH_DEV), HALF * CH_DEV)
     totals = None
     for window in range(NWIN):
-        low, high, came = pair_ref[window, :CH_DEV], pair_ref[window, CH_DEV:], came_ref[window]
-        own = jnp.where(odd == 1, high, came)
-        partners = jnp.concatenate(
-            [jnp.where(odd == 1, came, low), jnp.where(odd == 1, low, high), own], axis=0
-        )
+        partners = spectra_ref[window]
+        own = spectra_ref[window, 2 * CH_DEV :]
         own = own.astype(jnp.float32)
         own_real, own_imag = own[:, :NF], own[:, NF:]
         picked = jnp.dot(masks_ref[rows, :], partners, preferred_element_type=jnp.float32)
@@ -171,8 +184,11 @@
     periods = lax.axis_size("period")
     smem = pl.BlockSpec(memory_space=pltpu.SMEM)
     vmem = pl.BlockSpec(memory_space=pltpu.VMEM)
-    packed = call(pack_kernel, jax.ShapeDtypeStruct((count, 16, 128), jnp.bfloat16))(raw_strain[0])
-    series = lax.all_to_all(packed, "chan", 0, 0, tiled=True)
+    packed = call(pack_kernel, jax.ShapeDtypeStruct((count // 2, 2, 16, 128), jnp.bfloat16))(raw_strain[0])
+    groups = [list(range(core, count, 2)) for core in range(2)]
+    series = lax.all_to_all(packed, "chan", 0, 0, tiled=True, axis_index_groups=groups)
+    cores = [(i, i + 1) for i in range(0, count, 2)]
+    came = lax.ppermute(series, "chan", cores + [(j, i) for i, j in cores])
     masks, place = call(
         mask_kernel,
         (
@@ -182,20 +198,15 @@
         flops=2000000000,
         out_specs=(vmem, smem),
     )(bin_ids, owner_map.reshape(2, 128))
-    pair, gave = call(
-        spectra_kernel,
-        (
-            jax.ShapeDtypeStruct((NWIN, 2 * CH_DEV, 2 * NF), jnp.bfloat16),
-            jax.ShapeDtypeStruct((NWIN, CH_DEV, 2 * NF), jnp.bfloat16),
-        ),
-    )(series.reshape(NWIN, WIN, 128), jnp.asarray(dft_rows(), jnp.bfloat16))
-    cores = [(i, i + 1) for i in range(0, count, 2)]
-    came = lax.ppermute(gave, "chan", cores + [(j, i) for i, j in cores])
+    samples = (NWIN, 8, 2, 16, 128)
+    spectra = call(spectra_kernel, jax.ShapeDtypeStruct((NWIN, 3 * CH_DEV, 2 * NF), jnp.bfloat16))(
+        series.reshape(samples), came.reshape(samples), jnp.asarray(dft_rows(), jnp.bfloat16)
+    )
     part = jax.ShapeDtypeStruct((HALF, 2 * NF), jnp.float32)
-    across = call(functools.partial(bin_kernel, True), part)(masks, pair, came)
+    across = call(functools.partial(bin_kernel, True), part)(masks, spectra)
     pairs = [(2 * k + 1, 2 * k + 2) for k in range(count // 2 - 1)]
     arrived = lax.ppermute(across, "chan", pairs + [(j, i) for i, j in pairs])
-    inside = call(functools.partial(bin_kernel, False), part, flops=2000000000)(masks, pair, came)
+    inside = call(functools.partial(bin_kernel, False), part, flops=2000000000)(masks, spectra)
     merged = call(merge_kernel, jax.ShapeDtypeStruct((8, BINS, 2 * NF), jnp.bfloat16))(
         across, inside, arrived
     )

time: 63 us -> 61.9 us (0.983)
  the two profiles are of different devices: /device:TPU:8 before, /device:TPU:17 now
where the time goes in v8:
time: 61.9 us; the launch traced here: 61.6 us
  blocking collectives  45.5 us (74%)
  starting transfers between devices  7.2 us (12%)
  Pallas kernels  5.83 us (9%)
  waiting for transfers between devices  1.99 us (3%)
  local copies, waits for them, and re-layouts  0.98 us (2%)
    all_to_all x1, blocking collectives, shards(): lax.all_to_all(packed, 'chan', 0, 0, tiled=True, axis_index_groups=groups)  33.8 us
    all_to_all x1, blocking collectives, shards(): lax.all_to_all(merged, ('chan', 'period'), 0, 0, tiled=True, axis_index_g...  11.7 us
    ppermute x1, starting transfers between devices, shards(): came = lax.ppermute(series, 'chan', cores + [(j, i) for i, j in cores])  4.73 us
    ppermute x1, starting transfers between devices, shards(): arrived = lax.ppermute(across, 'chan', pairs + [(j, i) for i, j in pairs])  2.46 us
    pallas_call x1, Pallas kernels, shards(): call(stack_kernel, jax.ShapeDtypeStruct((CAP * NP, WIN), jnp.float32), in...  1.63 us
    pallas_call x1, Pallas kernels, shards(): across = call(functools.partial(bin_kernel, True), part)(masks, spectra)  1.31 us
    pallas_call x1, Pallas kernels, shards(): call(functools.partial(bin_kernel, False), part, flops=2000000000)  1.31 us
    ppermute x1, waiting for transfers between devices, shards(): arrived = lax.ppermute(across, 'chan', pairs + [(j, i) for i, j in pairs])  1.25 us
  transfers between devices with their start and end apart: 2, of which 2 were waited for; matrix products, arithmetic and copies ran while one was open for 0% of the time, Pallas kernels for 3%

profile of v8, /device:TPU:17, one launch (start us, length us, event | category | flops | bytes accessed | tf_op | source)
XLA Modules:
  0.0 61.6 jit_solution(5886051815274959631)
XLA Ops:
  0.0 0.0 copy-start.1
  0.0 0.9 %copy-done.1 = bf16[1,16,8192]{2,1,0:T(8,128)(2,1)S(1)} copy-done((bf16[1,16,8192]{2,1,0:T(8,128)(2,1)S(1)}, bf16[1,16,8192]{2,1,0:T(8,128)(2,1)}, u32[]{:S(2)}) %copy-start.1) | copy-done | bytes 262168
  1.0 0.1 shard_map.65
  1.0 0.0 copy-start.4
  1.0 33.8 %all_to_all.10 = bf16[64,2,16,128]{3,2,1,0:T(8,128)(2,1)S(1)} all-to-all(bf16[64,2,16,128]{3,2,1,0:T(8,128)(2,1)S(1)} %shard_map.65), channel_id=1, replica_groups={{0,8,16,24,32,40,48,56,64,72,80,88,96,104,112,120,128,136,144,152,160,1..., dimensions={0} | all-to-all | bytes 1048576 | tf_op jit(solution)/shard_map/all_to_all | solution.py:189
  34.8 0.0 copy-start.5
  34.8 4.7 %collective-permute-start = (bf16[64,2,16,128]{3,2,1,0:T(8,128)(2,1)S(1)}, bf16[64,2,16,128]{3,2,1,0:T(8,128)(2,1)S(1)}, u32[]{:S(2)}, u32[]{:S(2)}) collective-permute-start(bf16[64,2,16,128]{3,2,1,0:T(8,128)(2,1)S(1)} %all_to_all.10), channel_id=1, source_target_pairs={{0,4},{8,12},{16,20},{24,28},{32,36},{40,44},{48,52},{56,60},{64,6... | collective-permute-start | bytes 1572872 | tf_op jit(solution)/shard_map/ppermute | solution.py:191
  39.6 0.0 copy-done.4
  39.6 0.0 copy-done.5
  39.6 0.0 copy-start.3
  39.6 0.7 %shard_map.64 = (bf16[2048,192]{1,0:T(8,128)(2,1)S(1)}, s32[2]{0:T(128)S(1)}) custom-call(s32[3,64,64]{2,1,0:T(8,128)S(1)} %copy-done.4, s32[2,128]{1,0:T(2,128)S(1)} %bitcast.8), custom_call_target="tpu_custom_call" | custom-call | flops 2000000000 | bytes 7812500 | tf_op jit(solution)/shard_map/pallas_call | solution.py:192
  40.3 0.7 %collective-permute-done = bf16[64,2,16,128]{3,2,1,0:T(8,128)(2,1)S(1)} collective-permute-done((bf16[64,2,16,128]{3,2,1,0:T(8,128)(2,1)S(1)}, bf16[64,2,16,128]{3,2,1,0:T(8,128)(2,1)S(1)}, u32[]{:S(2)}, u32[]{:S(2)}) %collective-permute-start) | collective-permute-done | bytes 524320 | tf_op jit(solution)/shard_map/ppermute | solution.py:191
  41.1 0.0 copy-done.3
  41.1 0.8 %shard_map.66.spectra_ref = bf16[8,192,256]{2,1,0:T(8,128)(2,1)S(1)} custom-call(bf16[8,8,2,16,128]{4,3,2,1,0:T(8,128)(2,1)S(1)} %bitcast.5, bf16[8,8,2,16,128]{4,3,2,1,0:T(8,128)(2,1)S(1)} %bitcast.6, bf16[2,128,256]{2,1,0:T(8,128)(2,1)S(1)} %copy-done.3), custom_call_target="tpu_custom_call" | custom-call | tf_op jit(solution)/shard_map/pallas_call | solution.py:202
  41.8 1.3 %shard_map.67.across_ref = f32[16,256]{1,0:T(8,128)S(1)} custom-call(bf16[2048,192]{1,0:T(8,128)(2,1)S(1)} %get-tuple-element.8.masks_ref, bf16[8,192,256]{2,1,0:T(8,128)(2,1)S(1)} %shard_map.66.spectra_ref), custom_call_target="tpu_custom_call" | custom-call | tf_op jit(solution)/shard_map/pallas_call | solution.py:206
  43.2 2.5 %collective-permute-start.1 = (f32[16,256]{1,0:T(8,128)S(1)}, f32[16,256]{1,0:T(8,128)S(1)}, u32[]{:S(2)}, u32[]{:S(2)}) collective-permute-start(f32[16,256]{1,0:T(8,128)S(1)} %shard_map.67.across_ref), channel_id=1, source_target_pairs={{4,8},{12,16},{20,24},{28,32},{36,40},{44,48},{52,56},{60,64},{68,... | collective-permute-start | bytes 49160 | tf_op jit(solution)/shard_map/ppermute | solution.py:208
  45.6 0.0 copy-start.2
  45.6 1.3 %shard_map.68.inside_ref = f32[16,256]{1,0:T(8,128)S(1)} custom-call(bf16[2048,192]{1,0:T(8,128)(2,1)S(1)} %get-tuple-element.8.masks_ref, bf16[8,192,256]{2,1,0:T(8,128)(2,1)S(1)} %shard_map.66.spectra_ref), custom_call_target="tpu_custom_call" | custom-call | flops 2000000000 | bytes 7812500 | tf_op jit(solution)/shard_map/pallas_call | solution.py:209
  47.0 0.0 copy-start
  47.0 1.2 %collective-permute-done.1.arrived_ref = f32[16,256]{1,0:T(8,128)S(1)} collective-permute-done((f32[16,256]{1,0:T(8,128)S(1)}, f32[16,256]{1,0:T(8,128)S(1)}, u32[]{:S(2)}, u32[]{:S(2)}) %collective-permute-start.1) | collective-permute-done | bytes 16416 | tf_op jit(solution)/shard_map/ppermute | solution.py:208
  48.2 11.7 %all_to_all.11.sums_ref = bf16[8,32,256]{2,1,0:T(8,128)(2,1)S(1)} all-to-all(bf16[8,32,256]{2,1,0:T(8,128)(2,1)S(1)} %shard_map.69), channel_id=1, replica_groups={{0,1,2,3,4,5,6,7},{8,9,10,11,12,13,14,15},{16,17,18,19,20,21,22,23},{24..., dimensions={0} | all-to-all | bytes 262144 | tf_op jit(solution)/shard_map/all_to_all | solution.py:217
  60.0 0.0 copy-done.2
  60.0 0.0 copy-done
  60.0 1.6 %shard_map.70 = f32[128,256]{1,0:T(8,128)} custom-call(s32[2]{0:T(128)S(1)} %get-tuple-element.7.place_ref, bf16[8,32,256]{2,1,0:T(8,128)(2,1)S(1)} %all_to_all.11.sums_ref, f32[2,8,32,128]{3,2,1,0:T(8,128)S(1)} %copy-done.2, bf16[768,256]{1,0:T(8,128)(2,1)S(1)} %copy-done), custom_call_target="tpu_custom_call" | custom-call | tf_op jit(solution)/shard_map/pallas_call | solution.py:220
  (1 shorter events, 0.0 us)
Async XLA Ops:
  0.0 0.9 %copy-start.1 = (bf16[1,16,8192]{2,1,0:T(8,128)(2,1)S(1)}, bf16[1,16,8192]{2,1,0:T(8,128)(2,1)}, u32[]{:S(2)}) copy-start(bf16[1,16,8192]{2,1,0:T(8,128)(2,1)} %param.6) | copy-start | bytes 786436
  1.0 38.5 %copy-start.4 = (s32[3,64,64]{2,1,0:T(8,128)S(1)}, s32[3,64,64]{2,1,0:T(8,128)}, u32[]{:S(2)}) copy-start(s32[3,64,64]{2,1,0:T(8,128)} %ids_ref.1) | copy-start | bytes 147460
  34.8 4.8 %copy-start.5 = (s32[256]{0:T(256)S(1)}, s32[256]{0:T(256)}, u32[]{:S(2)}) copy-start(s32[256]{0:T(256)} %param.8) | copy-start | bytes 3076
  34.8 6.3 %collective-permute-start = (bf16[64,2,16,128]{3,2,1,0:T(8,128)(2,1)S(1)}, bf16[64,2,16,128]{3,2,1,0:T(8,128)(2,1)S(1)}, u32[]{:S(2)}, u32[]{:S(2)}) collective-permute-start(bf16[64,2,16,128]{3,2,1,0:T(8,128)(2,1)S(1)} %all_to_all.10), channel_id=1, source_target_pairs={{0,4},{8,12},{16,20},{24,28},{32,36},{40,44},{48,52},{56,60},{64,6... | collective-permute-start | bytes 1572872 | tf_op jit(solution)/shard_map/ppermute | solution.py:191
  39.6 1.5 %copy-start.3 = (bf16[2,128,256]{2,1,0:T(8,128)(2,1)S(1)}, bf16[2,128,256]{2,1,0:T(8,128)(2,1)}, u32[]{:S(2)}) copy-start(bf16[2,128,256]{2,1,0:T(8,128)(2,1)} %constant.6.clone.table_ref) | copy-start | bytes 393220
  43.2 5.1 %collective-permute-start.1 = (f32[16,256]{1,0:T(8,128)S(1)}, f32[16,256]{1,0:T(8,128)S(1)}, u32[]{:S(2)}, u32[]{:S(2)}) collective-permute-start(f32[16,256]{1,0:T(8,128)S(1)} %shard_map.67.across_ref), channel_id=1, source_target_pairs={{4,8},{12,16},{20,24},{28,32},{36,40},{44,48},{52,56},{60,64},{68,... | collective-permute-start | bytes 49160 | tf_op jit(solution)/shard_map/ppermute | solution.py:208
  45.6 14.3 %copy-start.2 = (f32[2,8,32,128]{3,2,1,0:T(8,128)S(1)}, f32[2,8,32,128]{3,2,1,0:T(8,128)}, u32[]{:S(2)}) copy-start(f32[2,8,32,128]{3,2,1,0:T(8,128)} %constant.7.clone.slant_ref) | copy-start | bytes 786436
  47.0 13.0 %copy-start = (bf16[768,256]{1,0:T(8,128)(2,1)S(1)}, bf16[768,256]{1,0:T(8,128)(2,1)}, u32[]{:S(2)}) copy-start(bf16[768,256]{1,0:T(8,128)(2,1)} %constant.8.clone.lags_ref) | copy-start | bytes 1179652

commit v9 on v8

--- a/solution.py
+++ b/solution.py
@@ -59,13 +59,17 @@
     )
 
 
+CHIP_ORDER = [8 * (at % 8) + (at // 8 + at % 8) % 8 for at in range(64)]
+
+
 def pack_kernel(raw_ref, out_ref):
-    out_ref[0, 0] = jnp.zeros((16, 128), jnp.bfloat16)
-    for chip in range(out_ref.shape[0]):
-        tile = raw_ref[:, 128 * chip : 128 * chip + 128]
-        out_ref[chip, 1] = tile
-        if chip + 1 < out_ref.shape[0]:
-            out_ref[chip + 1, 0] = tile
+    for place, chip in enumerate(CHIP_ORDER):
+        at = 128 * chip
+        out_ref[place, 1] = raw_ref[:, at : at + 128]
+        if chip:
+            out_ref[place, 0] = raw_ref[:, at - 128 : at]
+        else:
+            out_ref[place, 0] = jnp.zeros((16, 128), jnp.bfloat16)
 
 
 def mask_kernel(ids_ref, owner_ref, masks_ref, place_ref):
@@ -80,28 +84,36 @@
     place_ref[1] = jnp.sum((owner == device).astype(jnp.int32))
 
 
-def spectra_kernel(series_ref, came_ref, table_ref, out_ref):
-    core = lax.rem(lax.axis_index("chan"), 2)
-    odd = core == 1
-    table = jnp.concatenate([table_ref[core], table_ref[1 - core]], axis=0)
+def turned_blocks(series_ref, window):
+    odd = lax.rem(lax.axis_index("chan"), 2) == 1
+    places = [CHIP_ORDER.index(8 * window + z) for z in range(8)]
+    low, high = [
+        jnp.concatenate([series_ref[place, tile] for place in places], axis=0).T for tile in range(2)
+    ]
+    return jnp.concatenate(
+        [
+            jnp.where(odd, low[CH_DEV:], low[:CH_DEV]),
+            jnp.where(odd, high[:CH_DEV], low[CH_DEV:]),
+            jnp.where(odd, high[CH_DEV:], high[:CH_DEV]),
+        ],
+        axis=0,
+    )
+
+
+def own_kernel(series_ref, table_ref, out_ref):
+    table = table_ref[lax.rem(lax.axis_index("chan"), 2)]
     for window in range(NWIN):
-        turned = []
-        for tile in range(2):
-            series = series_ref[window, :, tile].reshape(WIN // 2, 128)
-            came = came_ref[window, :, tile].reshape(WIN // 2, 128)
-            turned.append(jnp.concatenate([series.T, came.T], axis=1))
-        low, high = turned
-        blocks = jnp.concatenate(
-            [
-                jnp.where(odd, low[CH_DEV:], low[:CH_DEV]),
-                jnp.where(odd, high[:CH_DEV], low[CH_DEV:]),
-                jnp.where(odd, high[CH_DEV:], high[:CH_DEV]),
-            ],
-            axis=0,
-        )
-        spectra = jnp.dot(blocks, table, preferred_element_type=jnp.float32)
+        blocks = turned_blocks(series_ref, window)
+        out_ref[window] = jnp.dot(blocks, table, preferred_element_type=jnp.float32)
+
+
+def spectra_kernel(own_ref, came_ref, table_ref, out_ref):
+    table = table_ref[1 - lax.rem(lax.axis_index("chan"), 2)]
+    for window in range(NWIN):
+        blocks = turned_blocks(came_ref, window)
+        spectra = own_ref[window] + jnp.dot(blocks, table, preferred_element_type=jnp.float32)
         power = jnp.mean(spectra * spectra, axis=-1, keepdims=True)
-        out_ref[window] = (spectra / jnp.sqrt(power + 1e-06)).astype(jnp.bfloat16)
+        out_ref[window] = (spectra * (1.0 / jnp.sqrt(power + 1e-06))).astype(jnp.bfloat16)
 
 
 def bin_kernel(across, masks_ref, spectra_ref, out_ref):
@@ -176,7 +188,7 @@
         jnp.concatenate([high, low, high], axis=1), lags_ref[...], preferred_element_type=jnp.float32
     )
     power = jnp.mean(traces * traces, axis=-1, keepdims=True)
-    out_ref[...] = traces / jnp.sqrt(power + 1e-06)
+    out_ref[...] = traces * (1.0 / jnp.sqrt(power + 1e-06))
 
 
 def shards(raw_strain, bin_ids, owner_map):
@@ -185,7 +197,7 @@
     smem = pl.BlockSpec(memory_space=pltpu.SMEM)
     vmem = pl.BlockSpec(memory_space=pltpu.VMEM)
     packed = call(pack_kernel, jax.ShapeDtypeStruct((count // 2, 2, 16, 128), jnp.bfloat16))(raw_strain[0])
-    groups = [list(range(core, count, 2)) for core in range(2)]
+    groups = [[2 * chip + core for chip in CHIP_ORDER] for core in range(2)]
     series = lax.all_to_all(packed, "chan", 0, 0, tiled=True, axis_index_groups=groups)
     cores = [(i, i + 1) for i in range(0, count, 2)]
     came = lax.ppermute(series, "chan", cores + [(j, i) for i, j in cores])
@@ -198,9 +210,12 @@
         flops=2000000000,
         out_specs=(vmem, smem),
     )(bin_ids, owner_map.reshape(2, 128))
-    samples = (NWIN, 8, 2, 16, 128)
+    table = jnp.asarray(dft_rows(), jnp.bfloat16)
+    own = call(
+        own_kernel, jax.ShapeDtypeStruct((NWIN, 3 * CH_DEV, 2 * NF), jnp.float32), flops=2000000000
+    )(series, table)
     spectra = call(spectra_kernel, jax.ShapeDtypeStruct((NWIN, 3 * CH_DEV, 2 * NF), jnp.bfloat16))(
-        series.reshape(samples), came.reshape(samples), jnp.asarray(dft_rows(), jnp.bfloat16)
+        own, came, table
     )
     part = jax.ShapeDtypeStruct((HALF, 2 * NF), jnp.float32)
     across = call(functools.partial(bin_kernel, True), part)(masks, spectra)

time: 61.9 us -> 61 us (0.985)
  the two profiles are of different devices: /device:TPU:17 before, /device:TPU:8 now
where the time goes in v9:
time: 61 us; the launch traced here: 60.5 us
  blocking collectives  44.7 us (73%)
  Pallas kernels  6.18 us (10%)
  starting transfers between devices  5.62 us (9%)
  waiting for transfers between devices  2.81 us (5%)
  local copies, waits for them, and re-layouts  1.14 us (2%)
    all_to_all x1, blocking collectives, shards(): lax.all_to_all(packed, 'chan', 0, 0, tiled=True, axis_index_groups=groups)  35 us
    all_to_all x1, blocking collectives, shards(): lax.all_to_all(merged, ('chan', 'period'), 0, 0, tiled=True, axis_index_g...  9.65 us
    ppermute x1, starting transfers between devices, shards(): arrived = lax.ppermute(across, 'chan', pairs + [(j, i) for i, j in pairs])  3.71 us
    ppermute x1, waiting for transfers between devices, shards(): arrived = lax.ppermute(across, 'chan', pairs + [(j, i) for i, j in pairs])  2.27 us
    ppermute x1, starting transfers between devices, shards(): came = lax.ppermute(series, 'chan', cores + [(j, i) for i, j in cores])  1.91 us
    pallas_call x1, Pallas kernels, shards(): call(stack_kernel, jax.ShapeDtypeStruct((CAP * NP, WIN), jnp.float32), in...  1.63 us
    pallas_call x1, Pallas kernels, shards(): across = call(functools.partial(bin_kernel, True), part)(masks, spectra)  1.31 us
    pallas_call x1, Pallas kernels, shards(): call(functools.partial(bin_kernel, False), part, flops=2000000000)  1.31 us
  transfers between devices with their start and end apart: 2, of which 2 were waited for; matrix products, arithmetic and copies ran while one was open for 0% of the time, Pallas kernels for 4%

profile of v9, /device:TPU:8, one launch (start us, length us, event | category | flops | bytes accessed | tf_op | source)
XLA Modules:
  0.0 60.5 jit_solution(11832092792072049135)
XLA Ops:
  0.0 0.0 copy-start.5
  0.0 0.0 copy-start.1
  0.0 1.0 %copy-done.1 = bf16[1,16,8192]{2,1,0:T(8,128)(2,1)S(1)} copy-done((bf16[1,16,8192]{2,1,0:T(8,128)(2,1)S(1)}, bf16[1,16,8192]{2,1,0:T(8,128)(2,1)}, u32[]{:S(2)}) %copy-start.1) | copy-done | bytes 262168
  1.0 0.1 shard_map.65
  1.0 35.0 %all_to_all.10.series_ref = bf16[64,2,16,128]{3,2,1,0:T(8,128)(2,1)S(1)} all-to-all(bf16[64,2,16,128]{3,2,1,0:T(8,128)(2,1)S(1)} %shard_map.65), channel_id=1, replica_groups={{0,72,144,216,288,360,432,504,8,80,152,224,296,368,440,448,16,88,160,23..., dimensions={0} | all-to-all | bytes 1048576 | tf_op jit(solution)/shard_map/all_to_all | solution.py:201
  36.1 1.9 %collective-permute-start = (bf16[64,2,16,128]{3,2,1,0:T(8,128)(2,1)S(1)}, bf16[64,2,16,128]{3,2,1,0:T(8,128)(2,1)S(1)}, u32[]{:S(2)}, u32[]{:S(2)}) collective-permute-start(bf16[64,2,16,128]{3,2,1,0:T(8,128)(2,1)S(1)} %all_to_all.10.series_ref), channel_id=1, source_target_pairs={{0,4},{8,12},{16,20},{24,28},{32,36},{40,44},{48,52},{56,60},{64,6... | collective-permute-start | bytes 1572872 | tf_op jit(solution)/shard_map/ppermute | solution.py:203
  38.0 0.0 copy-done.5
  38.0 0.0 copy-done.4
  38.0 0.0 copy-start.3
  38.0 0.7 %shard_map.64 = (bf16[2048,192]{1,0:T(8,128)(2,1)S(1)}, s32[2]{0:T(128)S(1)}) custom-call(s32[3,64,64]{2,1,0:T(8,128)S(1)} %copy-done.4, s32[2,128]{1,0:T(2,128)S(1)} %bitcast.4), custom_call_target="tpu_custom_call" | custom-call | flops 2000000000 | bytes 7812500 | tf_op jit(solution)/shard_map/pallas_call | solution.py:204
  38.8 0.2 copy-done.3
  38.9 0.4 shard_map.66.own_ref
  39.3 0.5 collective-permute-done.came_ref
  39.9 0.7 %shard_map.67.spectra_ref = bf16[8,192,256]{2,1,0:T(8,128)(2,1)S(1)} custom-call(f32[8,192,256]{2,1,0:T(8,128)S(1)} %shard_map.66.own_ref, bf16[64,2,16,128]{3,2,1,0:T(8,128)(2,1)S(1)} %collective-permute-done.came_ref, bf16[2,128,256]{2,1,0:T(8,128)(2,1)S(1)} %copy-done.3), custom_call_target="tpu_custom_call" | custom-call | tf_op jit(solution)/shard_map/pallas_call | solution.py:217
  40.6 1.3 %shard_map.68.across_ref = f32[16,256]{1,0:T(8,128)S(1)} custom-call(bf16[2048,192]{1,0:T(8,128)(2,1)S(1)} %get-tuple-element.8.masks_ref, bf16[8,192,256]{2,1,0:T(8,128)(2,1)S(1)} %shard_map.67.spectra_ref), custom_call_target="tpu_custom_call" | custom-call | tf_op jit(solution)/shard_map/pallas_call | solution.py:221
  41.9 0.0 copy-start
  41.9 0.0 copy-start.2
  41.9 3.7 %collective-permute-start.1 = (f32[16,256]{1,0:T(8,128)S(1)}, f32[16,256]{1,0:T(8,128)S(1)}, u32[]{:S(2)}, u32[]{:S(2)}) collective-permute-start(f32[16,256]{1,0:T(8,128)S(1)} %shard_map.68.across_ref), channel_id=1, source_target_pairs={{4,8},{12,16},{20,24},{28,32},{36,40},{44,48},{52,56},{60,64},{68,... | collective-permute-start | bytes 49160 | tf_op jit(solution)/shard_map/ppermute | solution.py:223
  45.6 1.3 %shard_map.69.inside_ref = f32[16,256]{1,0:T(8,128)S(1)} custom-call(bf16[2048,192]{1,0:T(8,128)(2,1)S(1)} %get-tuple-element.8.masks_ref, bf16[8,192,256]{2,1,0:T(8,128)(2,1)S(1)} %shard_map.67.spectra_ref), custom_call_target="tpu_custom_call" | custom-call | flops 2000000000 | bytes 7812500 | tf_op jit(solution)/shard_map/pallas_call | solution.py:224
  46.9 2.3 %collective-permute-done.1.arrived_ref = f32[16,256]{1,0:T(8,128)S(1)} collective-permute-done((f32[16,256]{1,0:T(8,128)S(1)}, f32[16,256]{1,0:T(8,128)S(1)}, u32[]{:S(2)}, u32[]{:S(2)}) %collective-permute-start.1) | collective-permute-done | bytes 16416 | tf_op jit(solution)/shard_map/ppermute | solution.py:223
  49.2 9.7 %all_to_all.11.sums_ref = bf16[8,32,256]{2,1,0:T(8,128)(2,1)S(1)} all-to-all(bf16[8,32,256]{2,1,0:T(8,128)(2,1)S(1)} %shard_map.70), channel_id=1, replica_groups={{0,1,2,3,4,5,6,7},{8,9,10,11,12,13,14,15},{16,17,18,19,20,21,22,23},{24..., dimensions={0} | all-to-all | bytes 262144 | tf_op jit(solution)/shard_map/all_to_all | solution.py:232
  58.9 0.0 copy-done
  58.9 0.0 copy-done.2
  58.9 1.6 %shard_map.71 = f32[128,256]{1,0:T(8,128)} custom-call(s32[2]{0:T(128)S(1)} %get-tuple-element.7.place_ref, bf16[8,32,256]{2,1,0:T(8,128)(2,1)S(1)} %all_to_all.11.sums_ref, f32[2,8,32,128]{3,2,1,0:T(8,128)S(1)} %copy-done.2, bf16[768,256]{1,0:T(8,128)(2,1)S(1)} %copy-done), custom_call_target="tpu_custom_call" | custom-call | tf_op jit(solution)/shard_map/pallas_call | solution.py:235
  (2 shorter events, 0.0 us)
Async XLA Ops:
  0.0 38.0 %copy-start.5 = (s32[256]{0:T(256)S(1)}, s32[256]{0:T(256)}, u32[]{:S(2)}) copy-start(s32[256]{0:T(256)} %param.8) | copy-start | bytes 3076
  0.0 1.0 %copy-start.1 = (bf16[1,16,8192]{2,1,0:T(8,128)(2,1)S(1)}, bf16[1,16,8192]{2,1,0:T(8,128)(2,1)}, u32[]{:S(2)}) copy-start(bf16[1,16,8192]{2,1,0:T(8,128)(2,1)} %param.6) | copy-start | bytes 786436
  1.0 37.0 %copy-start.4 = (s32[3,64,64]{2,1,0:T(8,128)S(1)}, s32[3,64,64]{2,1,0:T(8,128)}, u32[]{:S(2)}) copy-start(s32[3,64,64]{2,1,0:T(8,128)} %ids_ref.1) | copy-start | bytes 147460
  36.1 3.8 %collective-permute-start = (bf16[64,2,16,128]{3,2,1,0:T(8,128)(2,1)S(1)}, bf16[64,2,16,128]{3,2,1,0:T(8,128)(2,1)S(1)}, u32[]{:S(2)}, u32[]{:S(2)}) collective-permute-start(bf16[64,2,16,128]{3,2,1,0:T(8,128)(2,1)S(1)} %all_to_all.10.series_ref), channel_id=1, source_target_pairs={{0,4},{8,12},{16,20},{24,28},{32,36},{40,44},{48,52},{56,60},{64,6... | collective-permute-start | bytes 1572872 | tf_op jit(solution)/shard_map/ppermute | solution.py:203
  38.0 0.9 %copy-start.3 = (bf16[2,128,256]{2,1,0:T(8,128)(2,1)S(1)}, bf16[2,128,256]{2,1,0:T(8,128)(2,1)}, u32[]{:S(2)}) copy-start(bf16[2,128,256]{2,1,0:T(8,128)(2,1)} %constant.6.clone.table_ref) | copy-start | bytes 393220
  41.9 17.0 %copy-start = (bf16[768,256]{1,0:T(8,128)(2,1)S(1)}, bf16[768,256]{1,0:T(8,128)(2,1)}, u32[]{:S(2)}) copy-start(bf16[768,256]{1,0:T(8,128)(2,1)} %constant.8.clone.lags_ref) | copy-start | bytes 1179652
  41.9 17.0 %copy-start.2 = (f32[2,8,32,128]{3,2,1,0:T(8,128)S(1)}, f32[2,8,32,128]{3,2,1,0:T(8,128)}, u32[]{:S(2)}) copy-start(f32[2,8,32,128]{3,2,1,0:T(8,128)} %constant.7.clone.slant_ref) | copy-start | bytes 786436
  41.9 7.3 %collective-permute-start.1 = (f32[16,256]{1,0:T(8,128)S(1)}, f32[16,256]{1,0:T(8,128)S(1)}, u32[]{:S(2)}, u32[]{:S(2)}) collective-permute-start(f32[16,256]{1,0:T(8,128)S(1)} %shard_map.68.across_ref), channel_id=1, source_target_pairs={{4,8},{12,16},{20,24},{28,32},{36,40},{44,48},{52,56},{60,64},{68,... | collective-permute-start | bytes 49160 | tf_op jit(solution)/shard_map/ppermute | solution.py:223

commit v10 on v9

--- a/solution.py
+++ b/solution.py
@@ -59,12 +59,21 @@
     )
 
 
-CHIP_ORDER = [8 * (at % 8) + (at // 8 + at % 8) % 8 for at in range(64)]
+CHIP_ORDERS = (
+    [8 * (at % 8) + (at // 8 + at % 8) % 8 for at in range(64)],
+    [8 * (at % 8) + (7 - at // 8 + at % 8) % 8 for at in range(64)],
+)
+
+
+def place_of(chip, odd):
+    even_place, odd_place = CHIP_ORDERS[0].index(chip), CHIP_ORDERS[1].index(chip)
+    return jnp.where(odd, odd_place, even_place)
 
 
 def pack_kernel(raw_ref, out_ref):
-    for place, chip in enumerate(CHIP_ORDER):
-        at = 128 * chip
+    odd = lax.rem(lax.axis_index("chan"), 2) == 1
+    for chip in range(out_ref.shape[0]):
+        place, at = place_of(chip, odd), 128 * chip
         out_ref[place, 1] = raw_ref[:, at : at + 128]
         if chip:
             out_ref[place, 0] = raw_ref[:, at - 128 : at]
@@ -84,9 +93,10 @@
     place_ref[1] = jnp.sum((owner == device).astype(jnp.int32))
 
 
-def turned_blocks(series_ref, window):
+def turned_blocks(series_ref, window, came):
     odd = lax.rem(lax.axis_index("chan"), 2) == 1
-    places = [CHIP_ORDER.index(8 * window + z) for z in range(8)]
+    listed = jnp.logical_xor(odd, came)
+    places = [place_of(8 * window + z, listed) for z in range(8)]
     low, high = [
         jnp.concatenate([series_ref[place, tile] for place in places], axis=0).T for tile in range(2)
     ]
@@ -103,14 +113,14 @@
 def own_kernel(series_ref, table_ref, out_ref):
     table = table_ref[lax.rem(lax.axis_index("chan"), 2)]
     for window in range(NWIN):
-        blocks = turned_blocks(series_ref, window)
+        blocks = turned_blocks(series_ref, window, False)
         out_ref[window] = jnp.dot(blocks, table, preferred_element_type=jnp.float32)
 
 
 def spectra_kernel(own_ref, came_ref, table_ref, out_ref):
     table = table_ref[1 - lax.rem(lax.axis_index("chan"), 2)]
     for window in range(NWIN):
-        blocks = turned_blocks(came_ref, window)
+        blocks = turned_blocks(came_ref, window, True)
         spectra = own_ref[window] + jnp.dot(blocks, table, preferred_element_type=jnp.float32)
         power = jnp.mean(spectra * spectra, axis=-1, keepdims=True)
         out_ref[window] = (spectra * (1.0 / jnp.sqrt(power + 1e-06))).astype(jnp.bfloat16)
@@ -197,7 +207,7 @@
     smem = pl.BlockSpec(memory_space=pltpu.SMEM)
     vmem = pl.BlockSpec(memory_space=pltpu.VMEM)
     packed = call(pack_kernel, jax.ShapeDtypeStruct((count // 2, 2, 16, 128), jnp.bfloat16))(raw_strain[0])
-    groups = [[2 * chip + core for chip in CHIP_ORDER] for core in range(2)]
+    groups = [[2 * chip + core for chip in CHIP_ORDERS[core]] for core in range(2)]
     series = lax.all_to_all(packed, "chan", 0, 0, tiled=True, axis_index_groups=groups)
     cores = [(i, i + 1) for i in range(0, count, 2)]
     came = lax.ppermute(series, "chan", cores + [(j, i) for i, j in cores])

time: 61 us -> 59.7 us (0.979)
  blocking collectives: 44.7 us -> 43.3 us
    all_to_all x1, blocking collectives: 35 us -> 33.7 us  [shards(): lax.all_to_all(packed, 'chan', 0, 0, tiled=True, axis_index_groups=groups)]
where the time goes in v10:
time: 59.7 us; the launch traced here: 59.2 us
  blocking collectives  43.3 us (73%)
  Pallas kernels  6.2 us (10%)
  starting transfers between devices  6.05 us (10%)
  waiting for transfers between devices  2.37 us (4%)
  local copies, waits for them, and re-layouts  1.14 us (2%)
    all_to_all x1, blocking collectives, shards(): lax.all_to_all(packed, 'chan', 0, 0, tiled=True, axis_index_groups=groups)  33.7 us
    all_to_all x1, blocking collectives, shards(): lax.all_to_all(merged, ('chan', 'period'), 0, 0, tiled=True, axis_index_g...  9.66 us
    ppermute x1, starting transfers between devices, shards(): arrived = lax.ppermute(across, 'chan', pairs + [(j, i) for i, j in pairs])  4.14 us
    ppermute x1, starting transfers between devices, shards(): came = lax.ppermute(series, 'chan', cores + [(j, i) for i, j in cores])  1.91 us
    ppermute x1, waiting for transfers between devices, shards(): arrived = lax.ppermute(across, 'chan', pairs + [(j, i) for i, j in pairs])  1.83 us
    pallas_call x1, Pallas kernels, shards(): call(stack_kernel, jax.ShapeDtypeStruct((CAP * NP, WIN), jnp.float32), in...  1.63 us
    pallas_call x1, Pallas kernels, shards(): across = call(functools.partial(bin_kernel, True), part)(masks, spectra)  1.31 us
    pallas_call x1, Pallas kernels, shards(): call(functools.partial(bin_kernel, False), part, flops=2000000000)  1.31 us
  transfers between devices with their start and end apart: 2, of which 2 were waited for; matrix products, arithmetic and copies ran while one was open for 0% of the time, Pallas kernels for 4%

profile of v10, /device:TPU:8, one launch (start us, length us, event | category | flops | bytes accessed | tf_op | source)
XLA Modules:
  0.0 59.2 jit_solution(16743376841441669317)
XLA Ops:
  0.0 0.0 copy-start.5
  0.0 0.0 copy-start.1
  0.0 1.0 %copy-done.1 = bf16[1,16,8192]{2,1,0:T(8,128)(2,1)S(1)} copy-done((bf16[1,16,8192]{2,1,0:T(8,128)(2,1)S(1)}, bf16[1,16,8192]{2,1,0:T(8,128)(2,1)}, u32[]{:S(2)}) %copy-start.1) | copy-done | bytes 262168
  1.0 0.1 shard_map.65
  1.1 33.7 %all_to_all.10.series_ref = bf16[64,2,16,128]{3,2,1,0:T(8,128)(2,1)S(1)} all-to-all(bf16[64,2,16,128]{3,2,1,0:T(8,128)(2,1)S(1)} %shard_map.65), channel_id=1, replica_groups={{0,72,144,216,288,360,432,504,8,80,152,224,296,368,440,448,16,88,160,23..., dimensions={0} | all-to-all | bytes 1048576 | tf_op jit(solution)/shard_map/all_to_all | solution.py:211
  34.7 1.9 %collective-permute-start = (bf16[64,2,16,128]{3,2,1,0:T(8,128)(2,1)S(1)}, bf16[64,2,16,128]{3,2,1,0:T(8,128)(2,1)S(1)}, u32[]{:S(2)}, u32[]{:S(2)}) collective-permute-start(bf16[64,2,16,128]{3,2,1,0:T(8,128)(2,1)S(1)} %all_to_all.10.series_ref), channel_id=1, source_target_pairs={{0,4},{8,12},{16,20},{24,28},{32,36},{40,44},{48,52},{56,60},{64,6... | collective-permute-start | bytes 1572872 | tf_op jit(solution)/shard_map/ppermute | solution.py:213
  36.6 0.0 copy-done.5
  36.7 0.0 copy-done.4
  36.7 0.0 copy-start.3
  36.7 0.7 %shard_map.64 = (bf16[2048,192]{1,0:T(8,128)(2,1)S(1)}, s32[2]{0:T(128)S(1)}) custom-call(s32[3,64,64]{2,1,0:T(8,128)S(1)} %copy-done.4, s32[2,128]{1,0:T(2,128)S(1)} %bitcast.4), custom_call_target="tpu_custom_call" | custom-call | flops 2000000000 | bytes 7812500 | tf_op jit(solution)/shard_map/pallas_call | solution.py:214
  37.4 0.2 copy-done.3
  37.6 0.4 shard_map.66.own_ref
  38.0 0.5 collective-permute-done.came_ref
  38.5 0.7 %shard_map.67.spectra_ref = bf16[8,192,256]{2,1,0:T(8,128)(2,1)S(1)} custom-call(f32[8,192,256]{2,1,0:T(8,128)S(1)} %shard_map.66.own_ref, bf16[64,2,16,128]{3,2,1,0:T(8,128)(2,1)S(1)} %collective-permute-done.came_ref, bf16[2,128,256]{2,1,0:T(8,128)(2,1)S(1)} %copy-done.3), custom_call_target="tpu_custom_call" | custom-call | tf_op jit(solution)/shard_map/pallas_call | solution.py:227
  39.2 1.3 %shard_map.68.across_ref = f32[16,256]{1,0:T(8,128)S(1)} custom-call(bf16[2048,192]{1,0:T(8,128)(2,1)S(1)} %get-tuple-element.8.masks_ref, bf16[8,192,256]{2,1,0:T(8,128)(2,1)S(1)} %shard_map.67.spectra_ref), custom_call_target="tpu_custom_call" | custom-call | tf_op jit(solution)/shard_map/pallas_call | solution.py:231
  40.5 0.0 copy-start
  40.6 0.0 copy-start.2
  40.6 4.1 %collective-permute-start.1 = (f32[16,256]{1,0:T(8,128)S(1)}, f32[16,256]{1,0:T(8,128)S(1)}, u32[]{:S(2)}, u32[]{:S(2)}) collective-permute-start(f32[16,256]{1,0:T(8,128)S(1)} %shard_map.68.across_ref), channel_id=1, source_target_pairs={{4,8},{12,16},{20,24},{28,32},{36,40},{44,48},{52,56},{60,64},{68,... | collective-permute-start | bytes 49160 | tf_op jit(solution)/shard_map/ppermute | solution.py:233
  44.7 1.3 %shard_map.69.inside_ref = f32[16,256]{1,0:T(8,128)S(1)} custom-call(bf16[2048,192]{1,0:T(8,128)(2,1)S(1)} %get-tuple-element.8.masks_ref, bf16[8,192,256]{2,1,0:T(8,128)(2,1)S(1)} %shard_map.67.spectra_ref), custom_call_target="tpu_custom_call" | custom-call | flops 2000000000 | bytes 7812500 | tf_op jit(solution)/shard_map/pallas_call | solution.py:234
  46.0 1.8 %collective-permute-done.1.arrived_ref = f32[16,256]{1,0:T(8,128)S(1)} collective-permute-done((f32[16,256]{1,0:T(8,128)S(1)}, f32[16,256]{1,0:T(8,128)S(1)}, u32[]{:S(2)}, u32[]{:S(2)}) %collective-permute-start.1) | collective-permute-done | bytes 16416 | tf_op jit(solution)/shard_map/ppermute | solution.py:233
  47.9 9.7 %all_to_all.11.sums_ref = bf16[8,32,256]{2,1,0:T(8,128)(2,1)S(1)} all-to-all(bf16[8,32,256]{2,1,0:T(8,128)(2,1)S(1)} %shard_map.70), channel_id=1, replica_groups={{0,1,2,3,4,5,6,7},{8,9,10,11,12,13,14,15},{16,17,18,19,20,21,22,23},{24..., dimensions={0} | all-to-all | bytes 262144 | tf_op jit(solution)/shard_map/all_to_all | solution.py:242
  57.5 0.0 copy-done
  57.6 0.0 copy-done.2
  57.6 1.6 %shard_map.71 = f32[128,256]{1,0:T(8,128)} custom-call(s32[2]{0:T(128)S(1)} %get-tuple-element.7.place_ref, bf16[8,32,256]{2,1,0:T(8,128)(2,1)S(1)} %all_to_all.11.sums_ref, f32[2,8,32,128]{3,2,1,0:T(8,128)S(1)} %copy-done.2, bf16[768,256]{1,0:T(8,128)(2,1)S(1)} %copy-done), custom_call_target="tpu_custom_call" | custom-call | tf_op jit(solution)/shard_map/pallas_call | solution.py:245
  (2 shorter events, 0.0 us)
Async XLA Ops:
  0.0 36.7 %copy-start.5 = (s32[256]{0:T(256)S(1)}, s32[256]{0:T(256)}, u32[]{:S(2)}) copy-start(s32[256]{0:T(256)} %param.8) | copy-start | bytes 3076
  0.0 1.0 %copy-start.1 = (bf16[1,16,8192]{2,1,0:T(8,128)(2,1)S(1)}, bf16[1,16,8192]{2,1,0:T(8,128)(2,1)}, u32[]{:S(2)}) copy-start(bf16[1,16,8192]{2,1,0:T(8,128)(2,1)} %param.6) | copy-start | bytes 786436
  1.0 35.7 %copy-start.4 = (s32[3,64,64]{2,1,0:T(8,128)S(1)}, s32[3,64,64]{2,1,0:T(8,128)}, u32[]{:S(2)}) copy-start(s32[3,64,64]{2,1,0:T(8,128)} %ids_ref.1) | copy-start | bytes 147460
  34.7 3.8 %collective-permute-start = (bf16[64,2,16,128]{3,2,1,0:T(8,128)(2,1)S(1)}, bf16[64,2,16,128]{3,2,1,0:T(8,128)(2,1)S(1)}, u32[]{:S(2)}, u32[]{:S(2)}) collective-permute-start(bf16[64,2,16,128]{3,2,1,0:T(8,128)(2,1)S(1)} %all_to_all.10.series_ref), channel_id=1, source_target_pairs={{0,4},{8,12},{16,20},{24,28},{32,36},{40,44},{48,52},{56,60},{64,6... | collective-permute-start | bytes 1572872 | tf_op jit(solution)/shard_map/ppermute | solution.py:213
  36.7 0.9 %copy-start.3 = (bf16[2,128,256]{2,1,0:T(8,128)(2,1)S(1)}, bf16[2,128,256]{2,1,0:T(8,128)(2,1)}, u32[]{:S(2)}) copy-start(bf16[2,128,256]{2,1,0:T(8,128)(2,1)} %constant.6.clone.table_ref) | copy-start | bytes 393220
  40.5 17.0 %copy-start = (bf16[768,256]{1,0:T(8,128)(2,1)S(1)}, bf16[768,256]{1,0:T(8,128)(2,1)}, u32[]{:S(2)}) copy-start(bf16[768,256]{1,0:T(8,128)(2,1)} %constant.8.clone.lags_ref) | copy-start | bytes 1179652
  40.6 17.0 %copy-start.2 = (f32[2,8,32,128]{3,2,1,0:T(8,128)S(1)}, f32[2,8,32,128]{3,2,1,0:T(8,128)}, u32[]{:S(2)}) copy-start(f32[2,8,32,128]{3,2,1,0:T(8,128)} %constant.7.clone.slant_ref) | copy-start | bytes 786436
  40.6 7.3 %collective-permute-start.1 = (f32[16,256]{1,0:T(8,128)S(1)}, f32[16,256]{1,0:T(8,128)S(1)}, u32[]{:S(2)}, u32[]{:S(2)}) collective-permute-start(f32[16,256]{1,0:T(8,128)S(1)} %shard_map.68.across_ref), channel_id=1, source_target_pairs={{4,8},{12,16},{20,24},{28,32},{36,40},{44,48},{52,56},{60,64},{68,... | collective-permute-start | bytes 49160 | tf_op jit(solution)/shard_map/ppermute | solution.py:233

commit v11 on v10

--- a/solution.py
+++ b/solution.py
@@ -61,7 +61,7 @@
 
 CHIP_ORDERS = (
     [8 * (at % 8) + (at // 8 + at % 8) % 8 for at in range(64)],
-    [8 * (at % 8) + (7 - at // 8 + at % 8) % 8 for at in range(64)],
+    [8 * (7 - at % 8) + (at // 8 + 7 - at % 8) % 8 for at in range(64)],
 )
 
 

time: 59.7 us -> 58.3 us (0.977)
  blocking collectives: 43.3 us -> 41.9 us
    all_to_all x1, blocking collectives: 33.7 us -> 32.3 us  [shards(): lax.all_to_all(packed, 'chan', 0, 0, tiled=True, axis_index_groups=groups)]
where the time goes in v11:
time: 58.3 us; the launch traced here: 57.8 us
  blocking collectives  41.9 us (72%)
  Pallas kernels  6.2 us (11%)
  starting transfers between devices  5.63 us (10%)
  waiting for transfers between devices  2.79 us (5%)
  local copies, waits for them, and re-layouts  1.14 us (2%)
    all_to_all x1, blocking collectives, shards(): lax.all_to_all(packed, 'chan', 0, 0, tiled=True, axis_index_groups=groups)  32.3 us
    all_to_all x1, blocking collectives, shards(): lax.all_to_all(merged, ('chan', 'period'), 0, 0, tiled=True, axis_index_g...  9.65 us
    ppermute x1, starting transfers between devices, shards(): arrived = lax.ppermute(across, 'chan', pairs + [(j, i) for i, j in pairs])  3.73 us
    ppermute x1, waiting for transfers between devices, shards(): arrived = lax.ppermute(across, 'chan', pairs + [(j, i) for i, j in pairs])  2.25 us
    ppermute x1, starting transfers between devices, shards(): came = lax.ppermute(series, 'chan', cores + [(j, i) for i, j in cores])  1.91 us
    pallas_call x1, Pallas kernels, shards(): call(stack_kernel, jax.ShapeDtypeStruct((CAP * NP, WIN), jnp.float32), in...  1.63 us
    pallas_call x1, Pallas kernels, shards(): across = call(functools.partial(bin_kernel, True), part)(masks, spectra)  1.31 us
    pallas_call x1, Pallas kernels, shards(): call(functools.partial(bin_kernel, False), part, flops=2000000000)  1.31 us
  transfers between devices with their start and end apart: 2, of which 2 were waited for; matrix products, arithmetic and copies ran while one was open for 0% of the time, Pallas kernels for 4%

profile of v11, /device:TPU:8, one launch (start us, length us, event | category | flops | bytes accessed | tf_op | source)
XLA Modules:
  0.0 57.8 jit_solution(9182780766761593587)
XLA Ops:
  0.0 0.0 copy-start.5
  0.0 0.0 copy-start.1
  0.0 1.0 %copy-done.1 = bf16[1,16,8192]{2,1,0:T(8,128)(2,1)S(1)} copy-done((bf16[1,16,8192]{2,1,0:T(8,128)(2,1)S(1)}, bf16[1,16,8192]{2,1,0:T(8,128)(2,1)}, u32[]{:S(2)}) %copy-start.1) | copy-done | bytes 262168
  1.0 0.1 shard_map.65
  1.1 32.3 %all_to_all.10.series_ref = bf16[64,2,16,128]{3,2,1,0:T(8,128)(2,1)S(1)} all-to-all(bf16[64,2,16,128]{3,2,1,0:T(8,128)(2,1)S(1)} %shard_map.65), channel_id=1, replica_groups={{0,72,144,216,288,360,432,504,8,80,152,224,296,368,440,448,16,88,160,23..., dimensions={0} | all-to-all | bytes 1048576 | tf_op jit(solution)/shard_map/all_to_all | solution.py:211
  33.3 1.9 %collective-permute-start = (bf16[64,2,16,128]{3,2,1,0:T(8,128)(2,1)S(1)}, bf16[64,2,16,128]{3,2,1,0:T(8,128)(2,1)S(1)}, u32[]{:S(2)}, u32[]{:S(2)}) collective-permute-start(bf16[64,2,16,128]{3,2,1,0:T(8,128)(2,1)S(1)} %all_to_all.10.series_ref), channel_id=1, source_target_pairs={{0,4},{8,12},{16,20},{24,28},{32,36},{40,44},{48,52},{56,60},{64,6... | collective-permute-start | bytes 1572872 | tf_op jit(solution)/shard_map/ppermute | solution.py:213
  35.2 0.0 copy-done.5
  35.3 0.0 copy-done.4
  35.3 0.0 copy-start.3
  35.3 0.7 %shard_map.64 = (bf16[2048,192]{1,0:T(8,128)(2,1)S(1)}, s32[2]{0:T(128)S(1)}) custom-call(s32[3,64,64]{2,1,0:T(8,128)S(1)} %copy-done.4, s32[2,128]{1,0:T(2,128)S(1)} %bitcast.4), custom_call_target="tpu_custom_call" | custom-call | flops 2000000000 | bytes 7812500 | tf_op jit(solution)/shard_map/pallas_call | solution.py:214
  36.0 0.2 copy-done.3
  36.2 0.4 shard_map.66.own_ref
  36.6 0.5 collective-permute-done.came_ref
  37.1 0.7 %shard_map.67.spectra_ref = bf16[8,192,256]{2,1,0:T(8,128)(2,1)S(1)} custom-call(f32[8,192,256]{2,1,0:T(8,128)S(1)} %shard_map.66.own_ref, bf16[64,2,16,128]{3,2,1,0:T(8,128)(2,1)S(1)} %collective-permute-done.came_ref, bf16[2,128,256]{2,1,0:T(8,128)(2,1)S(1)} %copy-done.3), custom_call_target="tpu_custom_call" | custom-call | tf_op jit(solution)/shard_map/pallas_call | solution.py:227
  37.8 1.3 %shard_map.68.across_ref = f32[16,256]{1,0:T(8,128)S(1)} custom-call(bf16[2048,192]{1,0:T(8,128)(2,1)S(1)} %get-tuple-element.8.masks_ref, bf16[8,192,256]{2,1,0:T(8,128)(2,1)S(1)} %shard_map.67.spectra_ref), custom_call_target="tpu_custom_call" | custom-call | tf_op jit(solution)/shard_map/pallas_call | solution.py:231
  39.1 0.0 copy-start
  39.2 0.0 copy-start.2
  39.2 3.7 %collective-permute-start.1 = (f32[16,256]{1,0:T(8,128)S(1)}, f32[16,256]{1,0:T(8,128)S(1)}, u32[]{:S(2)}, u32[]{:S(2)}) collective-permute-start(f32[16,256]{1,0:T(8,128)S(1)} %shard_map.68.across_ref), channel_id=1, source_target_pairs={{4,8},{12,16},{20,24},{28,32},{36,40},{44,48},{52,56},{60,64},{68,... | collective-permute-start | bytes 49160 | tf_op jit(solution)/shard_map/ppermute | solution.py:233
  42.9 1.3 %shard_map.69.inside_ref = f32[16,256]{1,0:T(8,128)S(1)} custom-call(bf16[2048,192]{1,0:T(8,128)(2,1)S(1)} %get-tuple-element.8.masks_ref, bf16[8,192,256]{2,1,0:T(8,128)(2,1)S(1)} %shard_map.67.spectra_ref), custom_call_target="tpu_custom_call" | custom-call | flops 2000000000 | bytes 7812500 | tf_op jit(solution)/shard_map/pallas_call | solution.py:234
  44.2 2.3 %collective-permute-done.1.arrived_ref = f32[16,256]{1,0:T(8,128)S(1)} collective-permute-done((f32[16,256]{1,0:T(8,128)S(1)}, f32[16,256]{1,0:T(8,128)S(1)}, u32[]{:S(2)}, u32[]{:S(2)}) %collective-permute-start.1) | collective-permute-done | bytes 16416 | tf_op jit(solution)/shard_map/ppermute | solution.py:233
  46.5 9.7 %all_to_all.11.sums_ref = bf16[8,32,256]{2,1,0:T(8,128)(2,1)S(1)} all-to-all(bf16[8,32,256]{2,1,0:T(8,128)(2,1)S(1)} %shard_map.70), channel_id=1, replica_groups={{0,1,2,3,4,5,6,7},{8,9,10,11,12,13,14,15},{16,17,18,19,20,21,22,23},{24..., dimensions={0} | all-to-all | bytes 262144 | tf_op jit(solution)/shard_map/all_to_all | solution.py:242
  56.1 0.0 copy-done
  56.1 0.0 copy-done.2
  56.2 1.6 %shard_map.71 = f32[128,256]{1,0:T(8,128)} custom-call(s32[2]{0:T(128)S(1)} %get-tuple-element.7.place_ref, bf16[8,32,256]{2,1,0:T(8,128)(2,1)S(1)} %all_to_all.11.sums_ref, f32[2,8,32,128]{3,2,1,0:T(8,128)S(1)} %copy-done.2, bf16[768,256]{1,0:T(8,128)(2,1)S(1)} %copy-done), custom_call_target="tpu_custom_call" | custom-call | tf_op jit(solution)/shard_map/pallas_call | solution.py:245
  (2 shorter events, 0.0 us)
Async XLA Ops:
  0.0 35.2 %copy-start.5 = (s32[256]{0:T(256)S(1)}, s32[256]{0:T(256)}, u32[]{:S(2)}) copy-start(s32[256]{0:T(256)} %param.8) | copy-start | bytes 3076
  0.0 1.0 %copy-start.1 = (bf16[1,16,8192]{2,1,0:T(8,128)(2,1)S(1)}, bf16[1,16,8192]{2,1,0:T(8,128)(2,1)}, u32[]{:S(2)}) copy-start(bf16[1,16,8192]{2,1,0:T(8,128)(2,1)} %param.6) | copy-start | bytes 786436
  1.0 34.3 %copy-start.4 = (s32[3,64,64]{2,1,0:T(8,128)S(1)}, s32[3,64,64]{2,1,0:T(8,128)}, u32[]{:S(2)}) copy-start(s32[3,64,64]{2,1,0:T(8,128)} %ids_ref.1) | copy-start | bytes 147460
  33.3 3.8 %collective-permute-start = (bf16[64,2,16,128]{3,2,1,0:T(8,128)(2,1)S(1)}, bf16[64,2,16,128]{3,2,1,0:T(8,128)(2,1)S(1)}, u32[]{:S(2)}, u32[]{:S(2)}) collective-permute-start(bf16[64,2,16,128]{3,2,1,0:T(8,128)(2,1)S(1)} %all_to_all.10.series_ref), channel_id=1, source_target_pairs={{0,4},{8,12},{16,20},{24,28},{32,36},{40,44},{48,52},{56,60},{64,6... | collective-permute-start | bytes 1572872 | tf_op jit(solution)/shard_map/ppermute | solution.py:213
  35.3 0.9 %copy-start.3 = (bf16[2,128,256]{2,1,0:T(8,128)(2,1)S(1)}, bf16[2,128,256]{2,1,0:T(8,128)(2,1)}, u32[]{:S(2)}) copy-start(bf16[2,128,256]{2,1,0:T(8,128)(2,1)} %constant.6.clone.table_ref) | copy-start | bytes 393220
  39.1 17.0 %copy-start = (bf16[768,256]{1,0:T(8,128)(2,1)S(1)}, bf16[768,256]{1,0:T(8,128)(2,1)}, u32[]{:S(2)}) copy-start(bf16[768,256]{1,0:T(8,128)(2,1)} %constant.8.clone.lags_ref) | copy-start | bytes 1179652
  39.2 17.0 %copy-start.2 = (f32[2,8,32,128]{3,2,1,0:T(8,128)S(1)}, f32[2,8,32,128]{3,2,1,0:T(8,128)}, u32[]{:S(2)}) copy-start(f32[2,8,32,128]{3,2,1,0:T(8,128)} %constant.7.clone.slant_ref) | copy-start | bytes 786436
  39.2 7.3 %collective-permute-start.1 = (f32[16,256]{1,0:T(8,128)S(1)}, f32[16,256]{1,0:T(8,128)S(1)}, u32[]{:S(2)}, u32[]{:S(2)}) collective-permute-start(f32[16,256]{1,0:T(8,128)S(1)} %shard_map.68.across_ref), channel_id=1, source_target_pairs={{4,8},{12,16},{20,24},{28,32},{36,40},{44,48},{52,56},{60,64},{68,... | collective-permute-start | bytes 49160 | tf_op jit(solution)/shard_map/ppermute | solution.py:233

commit v12 on v11

--- a/solution.py
+++ b/solution.py
@@ -61,7 +61,7 @@
 
 CHIP_ORDERS = (
     [8 * (at % 8) + (at // 8 + at % 8) % 8 for at in range(64)],
-    [8 * (7 - at % 8) + (at // 8 + 7 - at % 8) % 8 for at in range(64)],
+    [8 * (7 - at % 8) + (at // 8 + at % 8) % 8 for at in range(64)],
 )
 
 

time: 58.3 us -> 59.9 us (1.027)
  the two profiles are of different devices: /device:TPU:8 before, /device:TPU:33 now
where the time goes in v12:
time: 59.9 us; the launch traced here: 59.7 us
  blocking collectives  43.4 us (72%)
  starting transfers between devices  7.37 us (12%)
  Pallas kernels  6.21 us (10%)
  waiting for transfers between devices  1.45 us (2%)
  local copies, waits for them, and re-layouts  1.14 us (2%)
    all_to_all x1, blocking collectives, shards(): lax.all_to_all(packed, 'chan', 0, 0, tiled=True, axis_index_groups=groups)  30.4 us
    all_to_all x1, blocking collectives, shards(): lax.all_to_all(merged, ('chan', 'period'), 0, 0, tiled=True, axis_index_g...  13 us
    ppermute x1, starting transfers between devices, shards(): came = lax.ppermute(series, 'chan', cores + [(j, i) for i, j in cores])  4.78 us
    ppermute x1, starting transfers between devices, shards(): arrived = lax.ppermute(across, 'chan', pairs + [(j, i) for i, j in pairs])  2.59 us
    pallas_call x1, Pallas kernels, shards(): call(stack_kernel, jax.ShapeDtypeStruct((CAP * NP, WIN), jnp.float32), in...  1.63 us
    pallas_call x1, Pallas kernels, shards(): call(functools.partial(bin_kernel, False), part, flops=2000000000)  1.31 us
    pallas_call x1, Pallas kernels, shards(): across = call(functools.partial(bin_kernel, True), part)(masks, spectra)  1.31 us
    ppermute x1, waiting for transfers between devices, shards(): arrived = lax.ppermute(across, 'chan', pairs + [(j, i) for i, j in pairs])  1.27 us
  transfers between devices with their start and end apart: 2, of which 2 were waited for; matrix products, arithmetic and copies ran while one was open for 0% of the time, Pallas kernels for 4%

profile of v12, /device:TPU:33, one launch (start us, length us, event | category | flops | bytes accessed | tf_op | source)
XLA Modules:
  0.0 59.7 jit_solution(615243730127536981)
XLA Ops:
  0.0 0.0 copy-start.5
  0.0 0.0 copy-start.1
  0.0 1.0 %copy-done.1 = bf16[1,16,8192]{2,1,0:T(8,128)(2,1)S(1)} copy-done((bf16[1,16,8192]{2,1,0:T(8,128)(2,1)S(1)}, bf16[1,16,8192]{2,1,0:T(8,128)(2,1)}, u32[]{:S(2)}) %copy-start.1) | copy-done | bytes 262168
  1.0 0.1 shard_map.65
  1.1 30.4 %all_to_all.10.series_ref = bf16[64,2,16,128]{3,2,1,0:T(8,128)(2,1)S(1)} all-to-all(bf16[64,2,16,128]{3,2,1,0:T(8,128)(2,1)S(1)} %shard_map.65), channel_id=1, replica_groups={{0,72,144,216,288,360,432,504,8,80,152,224,296,368,440,448,16,88,160,23..., dimensions={0} | all-to-all | bytes 1048576 | tf_op jit(solution)/shard_map/all_to_all | solution.py:211
  31.5 4.8 %collective-permute-start = (bf16[64,2,16,128]{3,2,1,0:T(8,128)(2,1)S(1)}, bf16[64,2,16,128]{3,2,1,0:T(8,128)(2,1)S(1)}, u32[]{:S(2)}, u32[]{:S(2)}) collective-permute-start(bf16[64,2,16,128]{3,2,1,0:T(8,128)(2,1)S(1)} %all_to_all.10.series_ref), channel_id=1, source_target_pairs={{0,4},{8,12},{16,20},{24,28},{32,36},{40,44},{48,52},{56,60},{64,6... | collective-permute-start | bytes 1572872 | tf_op jit(solution)/shard_map/ppermute | solution.py:213
  36.3 0.0 copy-done.5
  36.3 0.0 copy-done.4
  36.3 0.0 copy-start.3
  36.3 0.7 %shard_map.64 = (bf16[2048,192]{1,0:T(8,128)(2,1)S(1)}, s32[2]{0:T(128)S(1)}) custom-call(s32[3,64,64]{2,1,0:T(8,128)S(1)} %copy-done.4, s32[2,128]{1,0:T(2,128)S(1)} %bitcast.4), custom_call_target="tpu_custom_call" | custom-call | flops 2000000000 | bytes 7812500 | tf_op jit(solution)/shard_map/pallas_call | solution.py:214
  37.1 0.2 copy-done.3
  37.2 0.4 shard_map.66.own_ref
  37.6 0.2 collective-permute-done.came_ref
  37.8 0.7 %shard_map.67.spectra_ref = bf16[8,192,256]{2,1,0:T(8,128)(2,1)S(1)} custom-call(f32[8,192,256]{2,1,0:T(8,128)S(1)} %shard_map.66.own_ref, bf16[64,2,16,128]{3,2,1,0:T(8,128)(2,1)S(1)} %collective-permute-done.came_ref, bf16[2,128,256]{2,1,0:T(8,128)(2,1)S(1)} %copy-done.3), custom_call_target="tpu_custom_call" | custom-call | tf_op jit(solution)/shard_map/pallas_call | solution.py:227
  38.5 1.3 %shard_map.68.across_ref = f32[16,256]{1,0:T(8,128)S(1)} custom-call(bf16[2048,192]{1,0:T(8,128)(2,1)S(1)} %get-tuple-element.8.masks_ref, bf16[8,192,256]{2,1,0:T(8,128)(2,1)S(1)} %shard_map.67.spectra_ref), custom_call_target="tpu_custom_call" | custom-call | tf_op jit(solution)/shard_map/pallas_call | solution.py:231
  39.8 0.0 copy-start
  39.8 0.0 copy-start.2
  39.9 2.6 %collective-permute-start.1 = (f32[16,256]{1,0:T(8,128)S(1)}, f32[16,256]{1,0:T(8,128)S(1)}, u32[]{:S(2)}, u32[]{:S(2)}) collective-permute-start(f32[16,256]{1,0:T(8,128)S(1)} %shard_map.68.across_ref), channel_id=1, source_target_pairs={{4,8},{12,16},{20,24},{28,32},{36,40},{44,48},{52,56},{60,64},{68,... | collective-permute-start | bytes 49160 | tf_op jit(solution)/shard_map/ppermute | solution.py:233
  42.5 1.3 %shard_map.69.inside_ref = f32[16,256]{1,0:T(8,128)S(1)} custom-call(bf16[2048,192]{1,0:T(8,128)(2,1)S(1)} %get-tuple-element.8.masks_ref, bf16[8,192,256]{2,1,0:T(8,128)(2,1)S(1)} %shard_map.67.spectra_ref), custom_call_target="tpu_custom_call" | custom-call | flops 2000000000 | bytes 7812500 | tf_op jit(solution)/shard_map/pallas_call | solution.py:234
  43.8 1.3 %collective-permute-done.1.arrived_ref = f32[16,256]{1,0:T(8,128)S(1)} collective-permute-done((f32[16,256]{1,0:T(8,128)S(1)}, f32[16,256]{1,0:T(8,128)S(1)}, u32[]{:S(2)}, u32[]{:S(2)}) %collective-permute-start.1) | collective-permute-done | bytes 16416 | tf_op jit(solution)/shard_map/ppermute | solution.py:233
  45.1 13.0 %all_to_all.11.sums_ref = bf16[8,32,256]{2,1,0:T(8,128)(2,1)S(1)} all-to-all(bf16[8,32,256]{2,1,0:T(8,128)(2,1)S(1)} %shard_map.70), channel_id=1, replica_groups={{0,1,2,3,4,5,6,7},{8,9,10,11,12,13,14,15},{16,17,18,19,20,21,22,23},{24..., dimensions={0} | all-to-all | bytes 262144 | tf_op jit(solution)/shard_map/all_to_all | solution.py:242
  58.0 0.0 copy-done
  58.0 0.0 copy-done.2
  58.0 1.6 %shard_map.71 = f32[128,256]{1,0:T(8,128)} custom-call(s32[2]{0:T(128)S(1)} %get-tuple-element.7.place_ref, bf16[8,32,256]{2,1,0:T(8,128)(2,1)S(1)} %all_to_all.11.sums_ref, f32[2,8,32,128]{3,2,1,0:T(8,128)S(1)} %copy-done.2, bf16[768,256]{1,0:T(8,128)(2,1)S(1)} %copy-done), custom_call_target="tpu_custom_call" | custom-call | tf_op jit(solution)/shard_map/pallas_call | solution.py:245
  (2 shorter events, 0.0 us)
Async XLA Ops:
  0.0 36.3 %copy-start.5 = (s32[256]{0:T(256)S(1)}, s32[256]{0:T(256)}, u32[]{:S(2)}) copy-start(s32[256]{0:T(256)} %param.8) | copy-start | bytes 3076
  0.0 1.0 %copy-start.1 = (bf16[1,16,8192]{2,1,0:T(8,128)(2,1)S(1)}, bf16[1,16,8192]{2,1,0:T(8,128)(2,1)}, u32[]{:S(2)}) copy-start(bf16[1,16,8192]{2,1,0:T(8,128)(2,1)} %param.6) | copy-start | bytes 786436
  1.0 35.3 %copy-start.4 = (s32[3,64,64]{2,1,0:T(8,128)S(1)}, s32[3,64,64]{2,1,0:T(8,128)}, u32[]{:S(2)}) copy-start(s32[3,64,64]{2,1,0:T(8,128)} %ids_ref.1) | copy-start | bytes 147460
  31.5 6.3 %collective-permute-start = (bf16[64,2,16,128]{3,2,1,0:T(8,128)(2,1)S(1)}, bf16[64,2,16,128]{3,2,1,0:T(8,128)(2,1)S(1)}, u32[]{:S(2)}, u32[]{:S(2)}) collective-permute-start(bf16[64,2,16,128]{3,2,1,0:T(8,128)(2,1)S(1)} %all_to_all.10.series_ref), channel_id=1, source_target_pairs={{0,4},{8,12},{16,20},{24,28},{32,36},{40,44},{48,52},{56,60},{64,6... | collective-permute-start | bytes 1572872 | tf_op jit(solution)/shard_map/ppermute | solution.py:213
  36.3 0.9 %copy-start.3 = (bf16[2,128,256]{2,1,0:T(8,128)(2,1)S(1)}, bf16[2,128,256]{2,1,0:T(8,128)(2,1)}, u32[]{:S(2)}) copy-start(bf16[2,128,256]{2,1,0:T(8,128)(2,1)} %constant.6.clone.table_ref) | copy-start | bytes 393220
  39.8 18.2 %copy-start = (bf16[768,256]{1,0:T(8,128)(2,1)S(1)}, bf16[768,256]{1,0:T(8,128)(2,1)}, u32[]{:S(2)}) copy-start(bf16[768,256]{1,0:T(8,128)(2,1)} %constant.8.clone.lags_ref) | copy-start | bytes 1179652
  39.8 18.2 %copy-start.2 = (f32[2,8,32,128]{3,2,1,0:T(8,128)S(1)}, f32[2,8,32,128]{3,2,1,0:T(8,128)}, u32[]{:S(2)}) copy-start(f32[2,8,32,128]{3,2,1,0:T(8,128)} %constant.7.clone.slant_ref) | copy-start | bytes 786436
  39.9 5.2 %collective-permute-start.1 = (f32[16,256]{1,0:T(8,128)S(1)}, f32[16,256]{1,0:T(8,128)S(1)}, u32[]{:S(2)}, u32[]{:S(2)}) collective-permute-start(f32[16,256]{1,0:T(8,128)S(1)} %shard_map.68.across_ref), channel_id=1, source_target_pairs={{4,8},{12,16},{20,24},{28,32},{36,40},{44,48},{52,56},{60,64},{68,... | collective-permute-start | bytes 49160 | tf_op jit(solution)/shard_map/ppermute | solution.py:233
